TPU v7x, 512 devices: a whole 4x4x16 slice. The times are simulated.
512 devices in a mesh: ctx: 16 (over z_lo, core), head: 32 (over z_hi, y, x).
Axes of the slice: x: 4, y: 4, z: 16 (z_hi: 2, z_lo: 8; z = z_hi * 8 + z_lo), core: 2. Of those that a mesh axis runs over, the one named last changes fastest.
Arguments:
- queries: bfloat16 [4096, 8192], P('ctx', 'head'), may hold values from -5 to 5
- key_rows: bfloat16 [4096, 1024], P('ctx'), may hold values from -5 to 5
- value_rows: bfloat16 [4096, 1024], P('ctx'), may hold values from -6 to 6
- state_input: bfloat16 [4096, 8192], P('ctx', 'head'), may hold values from -6 to 6
- state_write: bfloat16 [4096, 8192], P('ctx', 'head'), may hold values from -0.119628906 to 0.119628906
- state_read: bfloat16 [4096, 8192], P('ctx', 'head'), may hold values from -6 to 6
- gate_input: bfloat16 [4096, 8192], P('ctx', 'head'), may hold values from -6 to 6
- decay_codes: int32 [4096, 64], P('ctx', 'head'), may hold values from 1 to 8192
- decay_rates: float32 [64], P('head'), may hold values from 2.9296875e-05 to 0.03
- skip_gain: float32 [64], P('head'), may hold values from 0.5 to 2
- norm_gain: float32 [8192], P('head'), may hold values from 0.5 to 1.5
- attend_readout: float32 [8192], P('head'), may hold values from -1.5 to 1.5
- state_readout: float32 [8192], P('head'), may hold values from -0.12 to 0.12
- segment_index: int32 [4096], P('ctx'), may hold values from 0 to 31, never falling along the last dimension, each value on 1 to 256 neighbouring positions
Outputs:
- attended: bfloat16 [4096, 8192], P('ctx', 'head')
- state_mixed: bfloat16 [4096, 8192], P('ctx', 'head')
- segment_values: float32 [32], replicated
All inputs are finite; a program needn't handle non-finite values.
Results may differ from a plain program's by a relative error of at most 0.018.
Values may be sent and summed in bfloat16 or wider, within the bound.
No kernel may reach another device: no remote copies, remote signals or barrier semaphores. Data moves between devices by JAX's collectives and lax.ppermute only.
A program may use at most 64 MiB of HBM per device.

v0:
```python
import math

import jax
import jax.numpy as jnp
from jax import lax
from jax.sharding import PartitionSpec as P

HEADS = 64
KV_HEADS = 8
HEAD_DIM = 128
SCAN_HEADS = 64
SCAN_DIM = 128
STATE = 128
BLOCK = 128
SEG_MEAN = 128


floor_score = -1e30


def prefix(array, axis, combine, identity):
    count, index = (lax.axis_size(axis), lax.axis_index(axis))
    everything = jax.tree.map(
        lambda part, kind: lax.all_gather(part.astype(kind), axis),
        array,
        (jnp.bfloat16, jnp.bfloat16),
    )
    start = jax.tree.map(
        lambda part, zero: jnp.broadcast_to(jnp.asarray(zero, part.dtype), part.shape),
        array,
        identity,
    )

    def turn(k, before):
        reached = k < index
        new = combine(
            before, jax.tree.map(lambda part, own: part[k].astype(own.dtype), everything, array)
        )
        return jax.tree.map(lambda a, b: jnp.where(reached, a, b), new, before)

    return lax.fori_loop(0, count, turn, start)


def absorb_group(inner, keys_piece, values_piece, start, third_request_vector, query_pos):
    rows = keys_piece.shape[0]
    per_head_dimension = third_request_vector.shape[2]
    width = math.gcd(rows, 512)
    scale = per_head_dimension ** (-0.5)

    def one_block(index, state):
        top, total, summed = state
        begin = index * width
        key_block = lax.dynamic_slice_in_dim(keys_piece, begin, width, 0)
        value_block = lax.dynamic_slice_in_dim(values_piece, begin, width, 0)
        scores = (
            jnp.einsum(
                "qhd,kd->qhk", third_request_vector, key_block, preferred_element_type=jnp.float32
            )
            * scale
        )
        key_pos = begin + jnp.arange(width, dtype=jnp.int32)
        allowed = (key_pos[None, :] <= query_pos[:, None])[:, None, :]
        masked = jnp.where(allowed, scores, floor_score)
        new_top = jnp.maximum(top, jnp.max(masked, axis=2))
        weights = jnp.where(allowed, jnp.exp(masked - new_top[:, :, None]), 0.0)
        fade = jnp.exp(top - new_top)
        total = total * fade + jnp.sum(weights, axis=2)
        summed = summed * fade[:, :, None] + jnp.einsum(
            "qhk,kd->qhd",
            weights.astype(jnp.bfloat16),
            value_block,
            preferred_element_type=jnp.float32,
        )
        return (new_top, total, summed)

    def compute(state):
        return lax.fori_loop(0, rows // width, one_block, state)

    def keep(state):
        return state

    needed = jnp.logical_and(start >= 0, start <= jnp.max(query_pos))
    return lax.cond(needed, compute, keep, inner)


def merge_state_pairs(earlier, later):
    return (earlier[0] * later[0], later[0][:, None, None] * earlier[1] + later[1])


def per_device(
    queries,
    key_rows,
    value_rows,
    state_input,
    state_write,
    state_read,
    gate_input,
    decay_codes,
    decay_rates,
    skip_gain,
    norm_gain,
    attend_readout,
    state_readout,
    segment_index,
):
    tokens_here = queries.shape[0]
    heads_here = queries.shape[1] // HEAD_DIM
    n_ctx = lax.axis_size("ctx")
    position = lax.axis_index("ctx")
    first = position * tokens_here
    shared_head = lax.axis_index("head") * heads_here // (HEADS // KV_HEADS)
    key_mine = lax.dynamic_slice_in_dim(key_rows, shared_head * HEAD_DIM, HEAD_DIM, 1)
    value_mine = lax.dynamic_slice_in_dim(value_rows, shared_head * HEAD_DIM, HEAD_DIM, 1)
    scan_here = decay_rates.shape[0]
    blocks = tokens_here // BLOCK
    inputs_four = state_input.reshape(blocks, BLOCK, scan_here, SCAN_DIM)
    write_four = state_write.reshape(blocks, BLOCK, scan_here, STATE)
    read_four = state_read.reshape(blocks, BLOCK, scan_here, STATE)
    log_decay = -decay_rates[None, :] * decay_codes.astype(jnp.float32)
    run = jnp.cumsum(log_decay.reshape(blocks, BLOCK, scan_here), axis=1)
    run_heads = jnp.transpose(run, (0, 2, 1))
    gap = run_heads[:, :, :, None] - run_heads[:, :, None, :]
    places = jnp.arange(BLOCK, dtype=jnp.int32)
    lower = places[:, None] >= places[None, :]
    decay = jnp.where(lower[None, None], jnp.exp(jnp.minimum(gap, 0.0)), 0.0)
    scan_scores = jnp.einsum(
        "bthn,bshn->bhts", read_four, write_four, preferred_element_type=jnp.float32
    )
    mix = (scan_scores * decay).astype(jnp.bfloat16)
    local = jnp.einsum("bhts,bshp->bthp", mix, inputs_four, preferred_element_type=jnp.float32)
    tail = jnp.exp(run[:, -1:, :] - run)
    written = (write_four.astype(jnp.float32) * tail[:, :, :, None]).astype(jnp.bfloat16)
    block_state = jnp.einsum(
        "bshn,bshp->bhnp", written, inputs_four, preferred_element_type=jnp.float32
    )
    block_fade = jnp.exp(run[:, -1, :])

    def carry_step(state, item):
        current, product = state
        fade_now, new_state = item
        return (
            (fade_now[:, None, None] * current + new_state, product * fade_now),
            (current, product),
        )

    start_state = (
        jnp.zeros((scan_here, STATE, SCAN_DIM), jnp.float32),
        jnp.ones((scan_here,), jnp.float32),
    )
    (end_state, total_fade), (entering_local, fade_before) = lax.scan(
        carry_step, start_state, (block_fade, block_state)
    )
    prefix_pair = prefix(
        (total_fade, end_state),
        "ctx",
        merge_state_pairs,
        (jnp.ones_like(total_fade), jnp.zeros_like(end_state)),
    )
    incoming = prefix_pair[1]
    entering = entering_local + fade_before[:, :, None, None] * incoming[None]
    carried = jnp.exp(run)[:, :, :, None] * jnp.einsum(
        "bthn,bhnp->bthp", read_four.astype(jnp.float32), entering, precision=lax.Precision.HIGHEST
    )
    mixed_y = local + carried + skip_gain[None, None, :, None] * inputs_four.astype(jnp.float32)
    gated = mixed_y.reshape(tokens_here, scan_here * SCAN_DIM) * jax.nn.silu(
        gate_input.astype(jnp.float32)
    )
    squares = lax.psum(jnp.sum(gated * gated, axis=1), "head")
    state_mixed = (
        gated * lax.rsqrt(squares / (SCAN_HEADS * SCAN_DIM) + 1e-05)[:, None] * norm_gain[None, :]
    ).astype(jnp.bfloat16)
    groups = (
        (
            queries.reshape(tokens_here, heads_here, HEAD_DIM),
            first + jnp.arange(tokens_here, dtype=jnp.int32),
        ),
    )
    initial = tuple(
        (
            (
                jnp.full((item[0].shape[0], heads_here), floor_score, jnp.float32),
                jnp.zeros((item[0].shape[0], heads_here), jnp.float32),
                jnp.zeros((item[0].shape[0], heads_here, HEAD_DIM), jnp.float32),
            )
            for item in groups
        )
    )
    pieces = (
        lax.all_gather(key_mine, "ctx", axis=0, tiled=True),
        lax.all_gather(value_mine, "ctx", axis=0, tiled=True),
    )
    start = jnp.int32(0)
    inner = tuple(
        (
            absorb_group(
                initial[number], pieces[0], pieces[1], start, groups[number][0], groups[number][1]
            )
            for number in range(len(groups))
        )
    )
    outputs = []
    for state in inner:
        top, total, summed = state
        outputs.append(
            (summed / total[:, :, None])
            .reshape(summed.shape[0], heads_here * HEAD_DIM)
            .astype(jnp.bfloat16)
        )
    attended = outputs[0]
    score = jnp.sum(attended.astype(jnp.float32) * attend_readout[None, :], axis=1)
    score = score + jnp.sum(state_mixed.astype(jnp.float32) * state_readout[None, :], axis=1)
    segment_count = tokens_here * n_ctx // SEG_MEAN
    member = (segment_index[:, None] == jnp.arange(segment_count, dtype=jnp.int32)[None, :]).astype(
        jnp.float32
    )
    partial_sums = jnp.dot(score, member, precision=lax.Precision.HIGHEST)
    counted = jnp.sum(member, axis=0) * (lax.axis_index("head") == 0).astype(jnp.float32)
    sums, counts = lax.psum((partial_sums, counted), ("ctx", "head"))
    return (attended, state_mixed, sums / counts)


def solution(mesh):
    in_specs = (
        P("ctx", "head"),
        P("ctx", None),
        P("ctx", None),
        P("ctx", "head"),
        P("ctx", "head"),
        P("ctx", "head"),
        P("ctx", "head"),
        P("ctx", "head"),
        P("head"),
        P("head"),
        P("head"),
        P("head"),
        P("head"),
        P("ctx"),
    )
    out_specs = (P("ctx", "head"), P("ctx", "head"), P())
    return jax.shard_map(
        per_device, mesh=mesh, in_specs=in_specs, out_specs=out_specs, check_vma=False
    )
```

profile of v0, /device:TPU:1, one launch (start us, length us, event | category | flops | bytes accessed | tf_op | source)
XLA Modules:
  0.0 475.2 jit_solution(627773776391355571)
XLA Ops:
  12.4 1.5 constant_dynamic-slice_fusion.1
  15.5 1.3 dynamic-slice
  17.6 51.5 %all-reduce = bf16[32]{0:T(256)(128)(2,1)S(1)} all-reduce(bf16[32]{0:T(256)(128)(2,1)S(1)} %dynamic-update-slice), channel_id=2, replica_groups=mesh['ctx'=16,'head'=32] {'ctx'}, use_global_device_ids=true, to_apply=%add | all-reduce | flops 32 | bytes 128
  70.3 45.0 %all-gather.10.cloned.1.call-done = bf16[32,128,128]{2,1,0:T(8,128)(2,1)} async-done(((bf16[2,128,128]{2,1,0:T(8,128)(2,1)}), bf16[32,128,128]{2,1,0:T(8,128)(2,1)}) %all-gather.10.cloned.1.call-update) | async-done | bytes 1048592 | tf_op jit(solution)/shard_map/all_gather | solution.py:24
  115.3 15.6 %while.53 = (s32[]{:T(128)}, f32[2,128,128]{2,1,0:T(8,128)S(1)}, s32[]{:T(128)}, bf16[16,2]{1,0:T(8,128)(2,1)S(1)}, bf16[16,2,128,128]{3,2,1,0:T(8,128)(2,1)}) while((s32[]{:T(128)}, f32[2,128,128]{2,1,0:T(8,128)S(1)}, s32[]{:T(128)}, bf16[16,2]{1,0:T(8,128)(2,1)S(1)}, bf16[16,2,128,128]{3,2,1,0:T(8,128)(2,1)}) %tuple.138), condition=%wide.region_11.12_spmd.clone.clone, body=%wide.region_10.11_spmd.clone.sunk.clone | while | flops 163846 | bytes 327797 | solution.py:41
  133.1 141.2 %psum.21 = f32[256]{0:T(256)S(1)} all-reduce(f32[256]{0:T(256)S(1)} %multiply_reduce_fusion.2), channel_id=1, replica_groups=mesh['ctx'=16,'head'=32] {'head'}, use_global_device_ids=true, to_apply=%region_13.14 | all-reduce | flops 256 | bytes 2048 | tf_op jit(solution)/shard_map/psum | solution.py:168
  274.2 45.6 %all-gather.8.cloned.1.call-done = bf16[4096,128]{1,0:T(8,128)(2,1)} async-done(((bf16[256,128]{1,0:T(8,128)(2,1)}), bf16[4096,128]{1,0:T(8,128)(2,1)}) %all-gather.8.cloned.1.call-update) | async-done | bytes 1048592 | tf_op jit(solution)/shard_map/all_gather | solution.py:190
  319.9 40.2 %conditional.1 = (f32[256,2]{0,1:T(2,128)}, f32[256,2,128]{2,0,1:T(8,128)}) conditional(s32[]{:T(128)} %convert_element_type.82, () %tuple.48, (bf16[256,256]{1,0:T(8,128)(2,1)S(1)}, s32[256]{0:T(256)S(1)}, bf16[4096,128]{1,0:T(8,128)(2,1)}, bf16[4096,128]{1,0:T(8,128)(2,1)}) %tuple.137), branch_computations={%region_1.2_spmd, %region_2.7_spmd} | conditional | flops 136907776 | bytes 5149947 | solution.py:83
  320.1 40.0 %while.51 = (s32[]{:T(128)}, f32[256,2]{0,1:T(2,128)S(1)}, f32[256,2]{0,1:T(2,128)}, f32[256,2,128]{2,0,1:T(8,128)}, s32[256]{0:T(256)S(1)}, /*index=5*/bf16[409...) while((s32[]{:T(128)}, f32[256,2]{0,1:T(2,128)S(1)}, ...), condition=%wide.region_6.6_spmd.clone.clone, body=%wide.region_3.5_spmd.clone.sunk.clone | while | flops 136907776 | bytes 4625571 | solution.py:77
  320.3 1.2 fusion.79
  322.4 2.1 convolution_add_fusion.3
  324.6 1.2 fusion.79
  326.1 1.3 fusion.82
  327.3 2.2 convolution_add_fusion.3
  329.7 1.2 fusion.79
  331.1 1.3 fusion.82
  332.4 2.2 convolution_add_fusion.3
  334.8 1.2 fusion.79
  336.2 1.3 fusion.82
  337.5 2.2 convolution_add_fusion.3
  339.9 1.2 fusion.79
  341.3 1.3 fusion.82
  342.6 2.2 convolution_add_fusion.3
  345.0 1.2 fusion.79
  346.4 1.3 fusion.82
  347.7 2.2 convolution_add_fusion.3
  350.1 1.2 fusion.79
  351.5 1.3 fusion.82
  352.8 2.2 convolution_add_fusion.3
  356.6 1.3 fusion.82
  357.9 2.2 convolution_add_fusion.3
  363.6 104.5 %all-reduce.1 = (f32[32]{0:T(128)S(1)}, f32[32]{0:T(128)S(1)}) all-reduce(f32[32]{0:T(128)S(1)} %convolution_bitcast_fusion.2, f32[32]{0:T(128)S(1)} %broadcast_multiply_fusion), channel_id=1, replica_groups=mesh['ctx'=16,'head'=32] {'ctx','head'}, use_global_device_ids=true, to_apply=%region_16.17 | all-reduce | flops 64 | bytes 512 | tf_op jit(solution)/shard_map/psum | solution.py:218
  (163 shorter events, 34.0 us)
Async XLA Ops:
  7.2 4.5 copy-start
  7.2 108.1 %all-gather.10.cloned.1.call-start = ((), (), s32[]{:S(2)}) async-start(), calls=%async_computation.2 | async-start | bytes 1114112 | tf_op jit(solution)/shard_map/all_gather | solution.py:24
  7.2 0.7 copy-start.12
  7.3 0.7 copy-start.6
  8.4 0.9 copy-start.2
  9.4 0.9 copy-start.3
  11.6 262.6 %all-gather.6.cloned.1.call-start = ((), (), s32[]{:S(2)}) async-start(), calls=%async_computation | async-start | bytes 1114112 | tf_op jit(solution)/shard_map/all_gather | solution.py:189
  12.3 307.5 %all-gather.8.cloned.1.call-start = ((), (), s32[]{:S(2)}) async-start(), calls=%async_computation.1 | async-start | bytes 1114112 | tf_op jit(solution)/shard_map/all_gather | solution.py:190
  13.9 1.5 copy-start.4
  69.2 0.7 copy-start.11
  130.9 0.7 copy-start.10
  132.0 0.9 copy-start.1
  132.9 187.0 %copy-start.5 = (bf16[256,256]{1,0:T(8,128)(2,1)S(1)}, bf16[256,256]{1,0:T(8,128)(2,1)}, u32[]{:S(2)}) copy-start(bf16[256,256]{1,0:T(8,128)(2,1)} %param.22) | copy-start | bytes 393220
  360.1 0.7 copy-start.7
  360.8 1.2 copy-start.8
  360.8 1.2 copy-start.9
Sparse Core Ops, SparseCore 0:
  11.7 103.5 all-gather.9
  118.0 99.8 all-gather.5
  220.6 99.2 all-gather.7
where the time goes:
time: 477 us; the launch traced here: 475 us
  blocking collectives  297 us (62%)
  waiting for transfers between devices  90.7 us (19%)
  other arithmetic  32.4 us (7%)
  matrix products  28.1 us (6%)
  between operations  15.3 us (3%)
  local copies, waits for them, and re-layouts  10.5 us (2%)
    psum x1, blocking collectives, per_device(): squares = lax.psum(jnp.sum(gated * gated, axis=1), 'head')  141 us
    psum x1, blocking collectives, per_device(): sums, counts = lax.psum((partial_sums, counted), ('ctx', 'head'))  105 us
    unnamed x1, blocking collectives  51.5 us
    all_gather x1, waiting for transfers between devices, per_device(): lax.all_gather(value_mine, 'ctx', axis=0, tiled=True)  45.6 us
    all_gather x1, waiting for transfers between devices, prefix(): lax.all_gather(part.astype(kind), axis)  45 us
    dot_general x8, matrix products, one_block(): jnp.einsum('qhk,kd->qhd', weights.astype(jnp.bfloat16), value_block, pref...  17.4 us
    select_n x16, other arithmetic, turn(): return jax.tree.map(lambda a, b: jnp.where(reached, a, b), new, before)  14.9 us
    dot_general x8, matrix products, one_block(): jnp.einsum('qhd,kd->qhk', third_request_vector, key_block, preferred_elem...  9.77 us
  transfers between devices with their start and end apart: 3, of which 2 were waited for; matrix products, arithmetic and copies ran while one was open for 4% of the time, Pallas kernels for 0%

commit v1 on v0

v1 whole, which is shorter than its diff:
```python
import functools
import math

import jax
import jax.numpy as jnp
from jax import lax
from jax.experimental import pallas as pl
from jax.experimental.pallas import tpu as pltpu
from jax.sharding import Mesh
from jax.sharding import PartitionSpec as P

HEADS = 64
KV_HEADS = 8
DIM = 128
BLOCK = 128
SEGMENTS = 32
COLUMNS = 8192
EPS = 1e-5

F32 = jnp.float32
BF16 = jnp.bfloat16
CTX = ("zl", "core")
HEAD = ("zh", "y", "x")
VMEM = pl.BlockSpec(memory_space=pltpu.VMEM)
SMEM = pl.BlockSpec(memory_space=pltpu.SMEM)
ANY = pl.BlockSpec(memory_space=pl.ANY)
NEG = -1e30
FADE = 2 * DIM
STATE_ROWS = FADE + 16


def call(kernel, outs, ins, scratch=(), flops=10**6, moved=10**6, mib=24):
    many = isinstance(outs, (tuple, list))
    return pl.pallas_call(
        kernel,
        out_shape=outs,
        in_specs=ins,
        out_specs=[VMEM] * len(outs) if many else VMEM,
        scratch_shapes=scratch,
        cost_estimate=pl.CostEstimate(flops=flops, bytes_accessed=moved, transcendentals=0),
        compiler_params=pltpu.CompilerParams(vmem_limit_bytes=mib * 2**20),
    )


def shape(dims, kind=F32):
    return jax.ShapeDtypeStruct(dims, kind)


def dot(a, b, ca=1, cb=0):
    return lax.dot_general(a, b, (((ca,), (cb,)), ((), ())), preferred_element_type=F32)


def split(v):
    high = v.astype(BF16)
    return high, (v - high.astype(F32)).astype(BF16)


def pack_kernel(k_ref, v_ref, o_ref, piece, sems):
    group = lax.axis_index("zh") * 4 + lax.axis_index("y")
    rows = pl.ds(pl.multiple_of(lax.axis_index("x") * 64, 64), 64)
    cols = pl.ds(pl.multiple_of(group * DIM, DIM), DIM)
    copies = [
        pltpu.make_async_copy(ref.at[rows, cols], piece.at[pl.ds(64 * n, 64)], sems.at[n])
        for n, ref in enumerate((k_ref, v_ref))
    ]
    for c in copies:
        c.start()
    for c in copies:
        c.wait()
    both = piece[...]
    for n in range(o_ref.shape[0]):
        o_ref[n] = both


def code_sums(codes_ref):
    rows = []
    for b in range(2):
        part = codes_ref[:, b * BLOCK : (b + 1) * BLOCK]
        rows += [part >> 6, part & 63]
    stacked = jnp.concatenate(rows, axis=0).astype(F32).astype(BF16)
    upto = lax.broadcasted_iota(jnp.int32, (BLOCK, BLOCK), 0) <= lax.broadcasted_iota(
        jnp.int32, (BLOCK, BLOCK), 1
    )
    total = dot(stacked, jnp.where(upto, 1.0, 0.0).astype(BF16))
    sums = {}
    for b in range(2):
        for h in range(2):
            sums[b, h] = 64.0 * total[4 * b + h : 4 * b + h + 1] + total[4 * b + 2 + h : 4 * b + 3 + h]
    return sums


def square(row):
    lanes = jnp.broadcast_to(row, (DIM, DIM))
    return lanes, jnp.transpose(lanes)


def states_kernel(x_ref, w_ref, codes_ref, rates_ref, own_ref, send_ref):
    sums = code_sums(codes_ref)
    row = lax.broadcasted_iota(jnp.int32, (8, DIM), 0)
    fades, marks = jnp.zeros((8, DIM), F32), jnp.zeros((8, DIM), F32)
    for h in range(2):
        cols = pl.ds(h * DIM, DIM)
        rate = rates_ref[h]
        state = None
        whole = None
        for b in range(2):
            rows = pl.ds(b * BLOCK, BLOCK)
            _, down = square(sums[b, h])
            last = down[BLOCK - 1 : BLOCK]
            tail = jnp.exp(rate * (down - last))
            written = (w_ref[rows, cols].astype(F32) * tail).astype(BF16)
            added = dot(written, x_ref[rows, cols], 0, 0)
            fade = jnp.exp(-rate * last)
            state = added if b == 0 else fade * state + added
            whole = last if b == 0 else whole + last
        own_ref[pl.ds(h * DIM, DIM)] = state
        send_ref[pl.ds(h * DIM, DIM)] = state.astype(BF16)
        fade = jnp.exp(-rate * whole)
        high = fade.astype(BF16).astype(F32)
        marks = jnp.where(row == h, fade, marks)
        fades = jnp.where(row == 2 * h, high, jnp.where(row == 2 * h + 1, fade - high, fades))
    own_ref[pl.ds(FADE, 8)] = marks
    send_ref[pl.ds(FADE, 16)] = jnp.concatenate([fades, jnp.zeros((8, DIM), F32)], axis=0).astype(BF16)


def first_kernel(got_ref, t_ref, t_out, x_out, send_ref):
    merge(got_ref, t_ref, None, t_out, x_out, send_ref)


def middle_kernel(got_ref, t_ref, x_ref, t_out, x_out, send_ref):
    merge(got_ref, t_ref, x_ref, t_out, x_out, send_ref)


def merge(got_ref, t_ref, x_ref, t_out, x_out, send_ref):
    got_fades = got_ref[pl.ds(FADE, 16)].astype(F32)
    row = lax.broadcasted_iota(jnp.int32, (8, DIM), 0)
    fades, marks_t, marks_x = (jnp.zeros((8, DIM), F32) for _ in range(3))
    for h in range(2):
        rows = pl.ds(h * DIM, DIM)
        got = got_ref[rows].astype(F32)
        got_fade = got_fades[2 * h : 2 * h + 1] + got_fades[2 * h + 1 : 2 * h + 2]
        mine = t_ref[pl.ds(FADE, 8)][h : h + 1]
        state = mine * got + t_ref[rows]
        t_out[rows] = state
        send_ref[rows] = state.astype(BF16)
        fade = mine * got_fade
        if x_ref is None:
            x_out[rows] = got
            x_fade = got_fade
        else:
            before = x_ref[pl.ds(FADE, 8)][h : h + 1]
            x_out[rows] = before * got + x_ref[rows]
            x_fade = before * got_fade
        high = fade.astype(BF16).astype(F32)
        marks_t = jnp.where(row == h, fade, marks_t)
        marks_x = jnp.where(row == h, x_fade, marks_x)
        fades = jnp.where(row == 2 * h, high, jnp.where(row == 2 * h + 1, fade - high, fades))
    t_out[pl.ds(FADE, 8)] = marks_t
    x_out[pl.ds(FADE, 8)] = marks_x
    send_ref[pl.ds(FADE, 16)] = jnp.concatenate([fades, jnp.zeros((8, DIM), F32)], axis=0).astype(BF16)


def local_kernel(x_ref, w_ref, r_ref, g_ref, codes_ref, rates_ref, skip_ref, base_ref, carry_ref):
    sums = code_sums(codes_ref)
    lower = lax.broadcasted_iota(jnp.int32, (BLOCK, BLOCK), 0) >= lax.broadcasted_iota(
        jnp.int32, (BLOCK, BLOCK), 1
    )
    for h in range(2):
        cols = pl.ds(h * DIM, DIM)
        rate, skip = rates_ref[h], skip_ref[h]
        state, before = None, None
        for b in range(2):
            rows = pl.ds(b * BLOCK, BLOCK)
            across, down = square(sums[b, h])
            x, w, r = x_ref[rows, cols], w_ref[rows, cols], r_ref[rows, cols]
            decay = jnp.exp(jnp.minimum(rate * (across - down), 0.0))
            scores = dot(r, w, 1, 1)
            mix = jnp.where(lower, scores * decay, 0.0).astype(BF16)
            y = dot(mix, x) + skip * x.astype(F32)
            if b == 0:
                last = down[BLOCK - 1 : BLOCK]
                tail = jnp.exp(rate * (down - last))
                state = dot((w.astype(F32) * tail).astype(BF16), x, 0, 0)
                before = last
                carry = jnp.exp(-rate * down)
            else:
                high, low = split(state)
                y = y + jnp.exp(-rate * down) * (dot(r, high) + dot(r, low))
                carry = jnp.exp(-rate * (down + before))
            gate = g_ref[rows, cols].astype(F32)
            silu = gate / (1.0 + jnp.exp(-gate))
            base_ref[rows, cols] = y * silu
            carry_ref[rows, cols] = carry * silu


def to_lanes(v):
    halves = v[:, :DIM] + v[:, DIM:]
    return [
        jnp.sum(jnp.transpose(halves[b * DIM : (b + 1) * DIM]), axis=0, keepdims=True)
        for b in range(2)
    ]


def carried_kernel(got_ref, x_ref, r_ref, base_ref, carry_ref, gain_ref, readout_ref, gated_ref, stat_ref):
    parts = []
    for h in range(2):
        rows, cols = pl.ds(h * DIM, DIM), pl.ds(h * DIM, DIM)
        before = x_ref[pl.ds(FADE, 8)][h : h + 1]
        entering = before * got_ref[rows].astype(F32) + x_ref[rows]
        high, low = split(entering)
        r = r_ref[:, cols]
        parts.append(base_ref[:, cols] + carry_ref[:, cols] * (dot(r, high) + dot(r, low)))
    gated = jnp.concatenate(parts, axis=1)
    gated_ref[...] = gated
    weight = gain_ref[...] * readout_ref[...]
    stat_ref[...] = jnp.concatenate(to_lanes(gated * gated) + to_lanes(gated * weight), axis=0)


def attend_kernel(q_ref, *refs):
    own, other = refs[0:4], refs[4:8]
    readout_ref, stat_ref, o_ref, send_ref, m_ref, l_ref, acc_ref = refs[8:]
    zl, core, x = (lax.axis_index(a) for a in ("zl", "core", "x"))
    m_ref[...] = jnp.full(m_ref.shape, NEG, F32)
    l_ref[...] = jnp.zeros(l_ref.shape, F32)
    acc_ref[...] = jnp.zeros(acc_ref.shape, F32)
    c = math.log2(math.e) / math.sqrt(DIM)

    def tile(k, masked):
        keys = jnp.concatenate([ref[k, 0:64] for ref in own + other], axis=0)
        values = jnp.concatenate([ref[k, 64:128] for ref in own + other], axis=0)
        width = keys.shape[0]
        if masked:
            lane = lax.broadcasted_iota(jnp.int32, (128, 128), 1)
            place = []
            for n in range(2):
                first = jnp.bitwise_xor(x, 2 * n) * 64
                second = jnp.bitwise_xor(x, 2 * n + 1) * 64 - 64
                place.append(lane + jnp.where(lane < 64, first, second))
            far = jnp.full((128, 128), jnp.where(core == 1, 0, 1 << 20), jnp.int32)
            place = jnp.concatenate(place + [far, far], axis=1)
        for h in range(2):
            for n in range(2):
                rows = pl.ds(n * 128, 128)
                at = pl.ds(h * 256 + n * 128, 128)
                s = dot(q_ref[rows, pl.ds(h * DIM, DIM)], keys, 1, 1)
                if masked:
                    spot = lax.broadcasted_iota(jnp.int32, (128, width), 0) + n * 128
                    s = jnp.where(place <= spot, s, NEG)
                old = m_ref[at]
                peak = jnp.max(s, axis=1, keepdims=True)
                new = jnp.maximum(old, peak)
                fade = jnp.exp2((old - new) * c)
                m_ref[at] = new
                p = jnp.concatenate(
                    [jnp.exp2((s[:, i : i + 128] - new) * c) for i in range(0, width, 128)], axis=1
                )
                part = p[:, 0:128]
                for i in range(128, width, 128):
                    part = part + p[:, i : i + 128]
                l_ref[at] = l_ref[at] * fade + part
                acc_ref[at] = acc_ref[at] * fade + dot(p.astype(BF16), values)

    def full(k, _):
        tile(k, False)
        return 0

    lax.fori_loop(0, zl, full, 0)
    tile(zl, True)
    parts = []
    for h in range(2):
        at = pl.ds(h * 256, 256)
        parts.append(acc_ref[at] / jnp.sum(l_ref[at], axis=1, keepdims=True))
    attended = jnp.concatenate(parts, axis=1).astype(BF16)
    o_ref[...] = attended
    a = to_lanes(attended.astype(F32) * readout_ref[...])
    stats = jnp.concatenate([stat_ref[...]] + a + [jnp.zeros((2, DIM), F32)], axis=0)
    for n in range(send_ref.shape[0]):
        send_ref[n] = stats


def segment_row(values):
    full = jnp.concatenate([values, jnp.zeros((DIM - SEGMENTS, DIM), F32)], axis=0)
    return jnp.sum(jnp.transpose(full), axis=0, keepdims=True)


def middle_sums_kernel(got_ref, seg_ref, send_ref):
    total = got_ref[0]
    for n in range(1, got_ref.shape[0]):
        total = total + got_ref[n]
    segment = lax.broadcasted_iota(jnp.int32, (SEGMENTS, DIM), 0)
    seg = seg_ref[...]
    part = jnp.zeros((SEGMENTS, DIM), F32)
    for j in range(2):
        part = part + jnp.where(seg[j : j + 1] == segment, total[4 + j : 5 + j], 0.0)
    part = segment_row(part)
    high = part.astype(BF16).astype(F32)
    out = jnp.concatenate([total[0:4], high, part - high, seg.astype(F32)], axis=0).astype(BF16)
    for n in range(send_ref.shape[0]):
        send_ref[n] = out


def final_kernel(got_ref, gated_ref, gain_ref, o_ref, values_ref):
    index = lax.axis_index("zl") * 2 + lax.axis_index("core")
    mine = got_ref[2 * index].astype(F32) + got_ref[2 * index + 1].astype(F32)
    gain = gain_ref[...]
    for b in range(2):
        rows = pl.ds(b * DIM, DIM)
        scale = lax.rsqrt(mine[b : b + 1] * (1.0 / COLUMNS) + EPS)
        _, down = square(scale)
        for h in range(2):
            cols = slice(h * DIM, (h + 1) * DIM)
            o_ref[rows, cols] = (gated_ref[rows, cols] * down * gain[:, cols]).astype(BF16)
    segment = lax.broadcasted_iota(jnp.int32, (SEGMENTS, DIM), 0)
    part = jnp.zeros((SEGMENTS, DIM), F32)
    count = jnp.zeros((SEGMENTS, DIM), F32)
    extra = jnp.zeros((8, DIM), F32)
    for s in range(got_ref.shape[0] // 2):
        low = got_ref[2 * s].astype(F32)
        both = low + got_ref[2 * s + 1].astype(F32)
        extra = extra + both
        scale = lax.rsqrt(both[0:2] * (1.0 / COLUMNS) + EPS)
        score = scale * both[2:4]
        seg = low[6:8].astype(jnp.int32)
        for j in range(2):
            member = seg[j : j + 1] == segment
            part = part + jnp.where(member, score[j : j + 1], 0.0)
            count = count + jnp.where(member, 1.0, 0.0)
    total = segment_row(part) + extra[4:5] + extra[5:6]
    held = segment_row(count)
    values_ref[...] = (total / jnp.maximum(held, 1.0))[:, :SEGMENTS]


def per_device(
    queries,
    key_rows,
    value_rows,
    state_input,
    state_write,
    state_read,
    gate_input,
    decay_codes,
    decay_rates,
    skip_gain,
    norm_gain,
    attend_readout,
    state_readout,
    segment_index,
):
    tokens = queries.shape[0]
    codes = decay_codes.T
    seg = segment_index.reshape(2, DIM)
    gain = norm_gain.reshape(1, 256)
    state_out = state_readout.reshape(1, 256)
    attend_out = attend_readout.reshape(1, 256)
    chips, wide = lax.axis_size("zl"), lax.axis_size("x")
    ctx = chips * lax.axis_size("core")

    packed = call(
        pack_kernel,
        shape((chips, DIM, DIM), BF16),
        [ANY, ANY],
        [pltpu.VMEM((DIM, DIM), BF16), pltpu.SemaphoreType.DMA((2,))],
    )(key_rows, value_rows)
    quarter = lax.all_to_all(packed, "zl", 0, 0)

    state_shapes = (shape((FADE + 8, DIM)), shape((STATE_ROWS, DIM), BF16))
    own, send = call(states_kernel, state_shapes, [VMEM, VMEM, VMEM, SMEM])(
        state_input, state_write, codes, decay_rates
    )

    def shifted(v, by):
        return lax.ppermute(v, CTX, [(i, i + by) for i in range(ctx - by)])

    merged = (shape((FADE + 8, DIM)), shape((FADE + 8, DIM)), shape((STATE_ROWS, DIM), BF16))
    got = shifted(send, 1)
    t, before, send = call(first_kernel, merged, [VMEM] * 2)(got, own)
    got = shifted(send, 2)
    base, carry = call(
        local_kernel, (shape((tokens, 256)), shape((tokens, 256))), [VMEM] * 5 + [SMEM] * 2
    )(state_input, state_write, state_read, gate_input, codes, decay_rates, skip_gain)
    t, before, send = call(middle_kernel, merged, [VMEM] * 3)(got, t, before)
    got = shifted(send, 4)
    t, before, send = call(middle_kernel, merged, [VMEM] * 3)(got, t, before)
    got = shifted(send, 8)

    pieces = [quarter] + [
        lax.ppermute(quarter, "x", [(i, i ^ k) for i in range(wide)]) for k in range(1, wide)
    ]
    others = [lax.ppermute(p, "core", [(0, 1), (1, 0)]) for p in pieces]

    gated, stats = call(
        carried_kernel, (shape((tokens, 256)), shape((4, DIM))), [VMEM] * 7
    )(got, before, state_read, base, carry, gain, state_out)

    head_plane = lax.axis_size("y") * wide
    attended, send = call(
        attend_kernel,
        (shape((tokens, 256), BF16), shape((head_plane, 8, DIM))),
        [VMEM] * 11,
        [pltpu.VMEM((512, DIM), F32) for _ in range(3)],
    )(queries, *pieces, *others, attend_out, stats)
    summed = lax.all_to_all(send, ("y", "x"), 0, 0)
    line = ctx * lax.axis_size("zh")
    send = call(middle_sums_kernel, shape((line, 8, DIM), BF16), [VMEM] * 2)(summed, seg)
    summed = lax.all_to_all(send, ("zl", "core", "zh"), 0, 0)
    state_mixed, values = call(
        final_kernel, (shape((tokens, 256), BF16), shape((1, SEGMENTS))), [VMEM] * 3
    )(summed, gated, gain)
    return attended, state_mixed, values.reshape(SEGMENTS)


def solution(mesh):
    grid = mesh.devices.shape
    inner = Mesh(mesh.devices.reshape(grid[0] // 2, 2, 2, 4, grid[1] // 8), CTX + HEAD)
    both = P(CTX, HEAD)
    rows, heads = P(CTX), P(HEAD)
    in_specs = (both, P(CTX, None), P(CTX, None)) + (both,) * 5 + (heads,) * 5 + (rows,)
    return jax.shard_map(
        per_device, mesh=inner, in_specs=in_specs, out_specs=(both, both, P()), check_vma=False
    )
```

time: 477 us -> 131 us (0.27)
  blocking collectives: 297 us -> 74.3 us
  waiting for transfers between devices: 90.7 us -> 2.72 us
  starting transfers between devices: 0.12 us -> 41.4 us
  other arithmetic: 32.4 us -> 0 us
  matrix products: 28.1 us -> 0 us
  between operations: 15.3 us -> 0.95 us
  Pallas kernels: 0 us -> 6.58 us
  local copies, waits for them, and re-layouts: 10.5 us -> 4.15 us
    psum x2 -> x0, blocking collectives: 246 us -> none  [the longest x1 141 us: per_device(): squares = lax.psum(jnp.sum(gated * gated, axis=1), 'head')]
    all_gather x3 -> x0, waiting for transfers between devices: 90.7 us -> none  [the longest x1 45.6 us: per_device(): lax.all_gather(value_mine, 'ctx', axis=0, tiled=True)]
    all_to_all x0 -> x3, blocking collectives: none -> 74.3 us  [the longest x1 36.4 us: per_device(): summed = lax.all_to_all(send, ('zl', 'core', 'zh'), 0, 0)]
    unnamed x1 -> x0, blocking collectives: 51.5 us -> none
    ppermute x0 -> x11, starting transfers between devices: none -> 41.4 us  [the longest x4 23.1 us: shifted(): return lax.ppermute(v, CTX, [(i, i + by) for i in range(ctx - by)])]
    dot_general x20 -> x0, matrix products: 28.1 us -> none  [the longest x8 17.4 us: one_block(): jnp.einsum('qhk,kd->qhd', weights.astype(jnp.bfloat16), value_block, pref...]
    select_n x16 -> x0, other arithmetic: 14.9 us -> none  [turn(): return jax.tree.map(lambda a, b: jnp.where(reached, a, b), new, before)]
    add x20 -> x0, other arithmetic: 9.75 us -> none  [the longest x8 9.55 us: one_block(): total = total * fade + jnp.sum(weights, axis=2)]
  transfers between devices with their start and end apart: 3 -> 11, of which waited for: 2 -> 2; matrix products, arithmetic and copies ran while one was open for 4% -> 0% of each run, Pallas kernels for 0% -> 3%
where the time goes in v1:
time: 131 us; the launch traced here: 130 us
  blocking collectives  74.3 us (57%)
  starting transfers between devices  41.4 us (32%)
  Pallas kernels  6.58 us (5%)
  local copies, waits for them, and re-layouts  4.15 us (3%)
  waiting for transfers between devices  2.72 us (2%)
    all_to_all x1, blocking collectives, per_device(): summed = lax.all_to_all(send, ('zl', 'core', 'zh'), 0, 0)  36.4 us
    all_to_all x1, blocking collectives, per_device(): quarter = lax.all_to_all(packed, 'zl', 0, 0)  25.2 us
    ppermute x4, starting transfers between devices, shifted(): return lax.ppermute(v, CTX, [(i, i + by) for i in range(ctx - by)])  23.1 us
    all_to_all x1, blocking collectives, per_device(): summed = lax.all_to_all(send, ('y', 'x'), 0, 0)  12.7 us
    ppermute x3, starting transfers between devices, per_device(): lax.ppermute(quarter, 'x', [(i, i ^ k) for i in range(wide)])  9.7 us
    ppermute x4, starting transfers between devices, per_device(): others = [lax.ppermute(p, 'core', [(0, 1), (1, 0)]) for p in pieces]  8.65 us
    unnamed x28, local copies, waits for them, and re-layouts  4.15 us
    ppermute x4, waiting for transfers between devices, shifted(): return lax.ppermute(v, CTX, [(i, i + by) for i in range(ctx - by)])  2.7 us
  transfers between devices with their start and end apart: 11, of which 2 were waited for; matrix products, arithmetic and copies ran while one was open for 0% of the time, Pallas kernels for 3%

profile of v1, /device:TPU:1, one launch (start us, length us, event | category | flops | bytes accessed | tf_op | source)
XLA Modules:
  0.0 130.1 jit_solution(16273839608600136501)
XLA Ops:
  0.6 1.0 copy-done
  1.7 1.0 copy-done.1
  2.7 0.1 shard_map.157
  2.8 0.0 copy-start.3
  2.8 0.0 copy-start.7
  2.8 25.2 %all_to_all.15.refs_0_ = bf16[8,128,128]{2,1,0:T(8,128)(2,1)S(1)} all-to-all(bf16[8,128,128]{2,1,0:T(8,128)(2,1)S(1)} %shard_map.157), channel_id=1, replica_groups=mesh['zl'=8,'core'=2,'zh'=2,'y'=4,'x'=4] {'zl'}, dimensions={0} | all-to-all | bytes 524288 | tf_op jit(solution)/shard_map/all_to_all | solution.py:364
  28.0 3.2 %collective-permute-start = (bf16[8,128,128]{2,1,0:T(8,128)(2,1)S(1)}, bf16[8,128,128]{2,1,0:T(8,128)(2,1)S(1)}, u32[]{:S(2)}, u32[]{:S(2)}) collective-permute-start(bf16[8,128,128]{2,1,0:T(8,128)(2,1)S(1)} %all_to_all.15.refs_0_), channel_id=1, source_target_pairs={{0,1},{1,0},{2,3},{3,2},{4,5},{5,4},{6,7},{7,6},{8,9},{9,8},{10,11... | collective-permute-start | bytes 786440 | tf_op jit(solution)/shard_map/ppermute | solution.py:387
  31.3 4.4 %collective-permute-start.1 = (bf16[8,128,128]{2,1,0:T(8,128)(2,1)S(1)}, bf16[8,128,128]{2,1,0:T(8,128)(2,1)S(1)}, u32[]{:S(2)}, u32[]{:S(2)}) collective-permute-start(bf16[8,128,128]{2,1,0:T(8,128)(2,1)S(1)} %all_to_all.15.refs_0_), channel_id=1, source_target_pairs={{0,2},{1,3},{2,0},{3,1},{4,6},{5,7},{6,4},{7,5},{8,10},{9,11},{10,... | collective-permute-start | bytes 786440 | tf_op jit(solution)/shard_map/ppermute | solution.py:387
  35.6 2.1 %collective-permute-start.2 = (bf16[8,128,128]{2,1,0:T(8,128)(2,1)S(1)}, bf16[8,128,128]{2,1,0:T(8,128)(2,1)S(1)}, u32[]{:S(2)}, u32[]{:S(2)}) collective-permute-start(bf16[8,128,128]{2,1,0:T(8,128)(2,1)S(1)} %all_to_all.15.refs_0_), channel_id=1, source_target_pairs={{0,3},{1,2},{2,1},{3,0},{4,7},{5,6},{6,5},{7,4},{8,11},{9,10},{10,... | collective-permute-start | bytes 786440 | tf_op jit(solution)/shard_map/ppermute | solution.py:387
  37.8 1.0 shard_map.158
  38.8 9.4 %collective-permute-start.7 = (bf16[272,128]{1,0:T(8,128)(2,1)S(1)}, bf16[272,128]{1,0:T(8,128)(2,1)S(1)}, u32[]{:S(2)}, u32[]{:S(2)}) collective-permute-start(bf16[272,128]{1,0:T(8,128)(2,1)S(1)} %get-tuple-element.21), channel_id=1, source_target_pairs={{0,32},{32,64},{64,96},{96,128},{128,160},{160,192},{192,224},{224... | collective-permute-start | bytes 208904 | tf_op jit(solution)/shard_map/ppermute | solution.py:372
  48.2 1.9 %collective-permute-start.3 = (bf16[8,128,128]{2,1,0:T(8,128)(2,1)S(1)}, bf16[8,128,128]{2,1,0:T(8,128)(2,1)S(1)}, u32[]{:S(2)}, u32[]{:S(2)}) collective-permute-start(bf16[8,128,128]{2,1,0:T(8,128)(2,1)S(1)} %all_to_all.15.refs_0_), channel_id=1, source_target_pairs={{0,32},{32,0},{1,33},{33,1},{2,34},{34,2},{3,35},{35,3},{4,36},{36... | collective-permute-start | bytes 786440 | tf_op jit(solution)/shard_map/ppermute | solution.py:389
  50.2 2.4 %collective-permute-start.4 = (bf16[8,128,128]{2,1,0:T(8,128)(2,1)S(1)}, bf16[8,128,128]{2,1,0:T(8,128)(2,1)S(1)}, u32[]{:S(2)}, u32[]{:S(2)}) collective-permute-start(bf16[8,128,128]{2,1,0:T(8,128)(2,1)S(1)} %collective-permute-done.refs_1_), channel_id=1, source_target_pairs={{0,32},{32,0},{1,33},{33,1},{2,34},{34,2},{3,35},{35,3},{4,36},{36... | collective-permute-start | bytes 786440 | tf_op jit(solution)/shard_map/ppermute | solution.py:389
  52.6 1.9 %collective-permute-start.5 = (bf16[8,128,128]{2,1,0:T(8,128)(2,1)S(1)}, bf16[8,128,128]{2,1,0:T(8,128)(2,1)S(1)}, u32[]{:S(2)}, u32[]{:S(2)}) collective-permute-start(bf16[8,128,128]{2,1,0:T(8,128)(2,1)S(1)} %collective-permute-done.1.refs_2_), channel_id=1, source_target_pairs={{0,32},{32,0},{1,33},{33,1},{2,34},{34,2},{3,35},{35,3},{4,36},{36... | collective-permute-start | bytes 786440 | tf_op jit(solution)/shard_map/ppermute | solution.py:389
  54.5 2.4 %collective-permute-start.6 = (bf16[8,128,128]{2,1,0:T(8,128)(2,1)S(1)}, bf16[8,128,128]{2,1,0:T(8,128)(2,1)S(1)}, u32[]{:S(2)}, u32[]{:S(2)}) collective-permute-start(bf16[8,128,128]{2,1,0:T(8,128)(2,1)S(1)} %collective-permute-done.2.refs_3_), channel_id=1, source_target_pairs={{0,32},{32,0},{1,33},{33,1},{2,34},{34,2},{3,35},{35,3},{4,36},{36... | collective-permute-start | bytes 786440 | tf_op jit(solution)/shard_map/ppermute | solution.py:389
  57.0 1.8 %collective-permute-start.8 = (bf16[272,128]{1,0:T(8,128)(2,1)S(1)}, bf16[272,128]{1,0:T(8,128)(2,1)S(1)}, u32[]{:S(2)}, u32[]{:S(2)}) collective-permute-start(bf16[272,128]{1,0:T(8,128)(2,1)S(1)} %get-tuple-element.23), channel_id=1, source_target_pairs={{0,64},{32,96},{64,128},{96,160},{128,192},{160,224},{192,256},{22... | collective-permute-start | bytes 208904 | tf_op jit(solution)/shard_map/ppermute | solution.py:372
  58.9 1.3 %collective-permute-done.8.got_ref = bf16[272,128]{1,0:T(8,128)(2,1)S(1)} collective-permute-done((bf16[272,128]{1,0:T(8,128)(2,1)S(1)}, bf16[272,128]{1,0:T(8,128)(2,1)S(1)}, u32[]{:S(2)}, u32[]{:S(2)}) %collective-permute-start.8) | collective-permute-done | bytes 69664 | tf_op jit(solution)/shard_map/ppermute | solution.py:372
  60.2 4.0 %collective-permute-start.9 = (bf16[272,128]{1,0:T(8,128)(2,1)S(1)}, bf16[272,128]{1,0:T(8,128)(2,1)S(1)}, u32[]{:S(2)}, u32[]{:S(2)}) collective-permute-start(bf16[272,128]{1,0:T(8,128)(2,1)S(1)} %get-tuple-element.26), channel_id=1, source_target_pairs={{0,128},{32,160},{64,192},{96,224},{128,256},{160,288},{192,320},{... | collective-permute-start | bytes 208904 | tf_op jit(solution)/shard_map/ppermute | solution.py:372
  64.2 1.3 %collective-permute-done.9.got_ref = bf16[272,128]{1,0:T(8,128)(2,1)S(1)} collective-permute-done((bf16[272,128]{1,0:T(8,128)(2,1)S(1)}, bf16[272,128]{1,0:T(8,128)(2,1)S(1)}, u32[]{:S(2)}, u32[]{:S(2)}) %collective-permute-start.9) | collective-permute-done | bytes 69664 | tf_op jit(solution)/shard_map/ppermute | solution.py:372
  65.6 0.7 shard_map.161
  66.2 7.9 %collective-permute-start.10 = (bf16[272,128]{1,0:T(8,128)(2,1)S(1)}, bf16[272,128]{1,0:T(8,128)(2,1)S(1)}, u32[]{:S(2)}, u32[]{:S(2)}) collective-permute-start(bf16[272,128]{1,0:T(8,128)(2,1)S(1)} %get-tuple-element.29), channel_id=1, source_target_pairs={{0,256},{32,288},{64,320},{96,352},{128,384},{160,416},{192,448},{... | collective-permute-start | bytes 208904 | tf_op jit(solution)/shard_map/ppermute | solution.py:372
  74.2 1.4 %shard_map.162 = (f32[256,256]{1,0:T(8,128)S(1)}, f32[256,256]{1,0:T(8,128)S(1)}) custom-call(bf16[256,256]{1,0:T(8,128)(2,1)S(1)} %copy-done.2, bf16[256,256]{1,0:T(8,128)(2,1)S(1)} %copy-done.3, bf16[256,256]{1,0:T(8,128)(2,1)S(1)} %copy-done.4, bf16[256,256]{1,0:T(8,128)(2,1)S(1)} %copy-done.6, s32[2,256]{1,0:T(2,128)S(1)} %bitcast.7, f32[2]{0:T(128)S(1)} %copy-done.9, ...), custom_call_target="tpu_custom_call" | custom-call | flops 1000000 | bytes 1000000 | tf_op jit(solution)/shard_map/pallas_call | solution.py:378
  75.6 0.7 copy-done.8
  76.2 0.4 shard_map.163
  76.6 0.5 copy-done.5
  77.1 0.2 copy-done.11
  77.3 2.0 %shard_map.164 = (bf16[256,256]{1,0:T(8,128)(2,1)}, f32[16,8,128]{2,1,0:T(8,128)S(1)}) custom-call(bf16[256,256]{1,0:T(8,128)(2,1)S(1)} %copy-done.5, bf16[8,128,128]{2,1,0:T(8,128)(2,1)S(1)} %all_to_all.15.refs_0_, bf16[8,128,128]{2,1,0:T(8,128)(2,1)S(1)} %collective-permute-done.refs_1_, bf16[8,128,128]{2,1,0:T(8,128)(2,1)S(1)} %collective-permute-done.1.refs_2_, ...), custom_call_target="tpu_custom_call" | custom-call | flops 1000000 | bytes 1000000 | tf_op jit(solution)/shard_map/pallas_call | solution.py:396
  79.3 12.7 %all_to_all.16.got_ref = f32[16,8,128]{2,1,0:T(8,128)S(1)} all-to-all(f32[16,8,128]{2,1,0:T(8,128)S(1)} %get-tuple-element.35), channel_id=1, replica_groups=mesh['zl'=8,'core'=2,'zh'=2,'y'=4,'x'=4] {'y','x'}, dimensions={0} | all-to-all | bytes 131072 | tf_op jit(solution)/shard_map/all_to_all | solution.py:402
  92.0 0.7 copy-done.12
  92.7 0.1 shard_map.165
  92.8 36.4 %all_to_all.17.got_ref = bf16[32,8,128]{2,1,0:T(8,128)(2,1)S(1)} all-to-all(bf16[32,8,128]{2,1,0:T(8,128)(2,1)S(1)} %shard_map.165), channel_id=1, replica_groups=mesh['zl'=8,'core'=2,'zh'=2,'y'=4,'x'=4] {'zl','core','zh'}, dimensions={0} | all-to-all | bytes 131072 | tf_op jit(solution)/shard_map/all_to_all | solution.py:405
  129.2 0.9 shard_map.166
  (31 shorter events, 0.1 us)
Async XLA Ops:
  0.6 1.0 copy-start
  1.7 1.0 copy-start.1
  2.8 35.0 %copy-start.2 = (bf16[256,256]{1,0:T(8,128)(2,1)S(1)}, bf16[256,256]{1,0:T(8,128)(2,1)}, u32[]{:S(2)}) copy-start(bf16[256,256]{1,0:T(8,128)(2,1)} %x_ref.3) | copy-start | bytes 393220
  2.8 35.0 %copy-start.3 = (bf16[256,256]{1,0:T(8,128)(2,1)S(1)}, bf16[256,256]{1,0:T(8,128)(2,1)}, u32[]{:S(2)}) copy-start(bf16[256,256]{1,0:T(8,128)(2,1)} %w_ref.3) | copy-start | bytes 393220
  2.8 35.0 %copy-start.7 = (s32[256,2]{0,1:T(2,128)S(1)}, s32[256,2]{0,1:T(2,128)}, u32[]{:S(2)}) copy-start(s32[256,2]{0,1:T(2,128)} %param.21) | copy-start | bytes 6148
  28.0 9.8 %copy-start.9 = (f32[2]{0:T(128)S(1)}, f32[2]{0:T(128)}, u32[]{:S(2)}) copy-start(f32[2]{0:T(128)} %rates_ref.3) | copy-start | bytes 28
  28.0 22.1 %collective-permute-start = (bf16[8,128,128]{2,1,0:T(8,128)(2,1)S(1)}, bf16[8,128,128]{2,1,0:T(8,128)(2,1)S(1)}, u32[]{:S(2)}, u32[]{:S(2)}) collective-permute-start(bf16[8,128,128]{2,1,0:T(8,128)(2,1)S(1)} %all_to_all.15.refs_0_), channel_id=1, source_target_pairs={{0,1},{1,0},{2,3},{3,2},{4,5},{5,4},{6,7},{7,6},{8,9},{9,8},{10,11... | collective-permute-start | bytes 786440 | tf_op jit(solution)/shard_map/ppermute | solution.py:387
  31.3 21.3 %collective-permute-start.1 = (bf16[8,128,128]{2,1,0:T(8,128)(2,1)S(1)}, bf16[8,128,128]{2,1,0:T(8,128)(2,1)S(1)}, u32[]{:S(2)}, u32[]{:S(2)}) collective-permute-start(bf16[8,128,128]{2,1,0:T(8,128)(2,1)S(1)} %all_to_all.15.refs_0_), channel_id=1, source_target_pairs={{0,2},{1,3},{2,0},{3,1},{4,6},{5,7},{6,4},{7,5},{8,10},{9,11},{10,... | collective-permute-start | bytes 786440 | tf_op jit(solution)/shard_map/ppermute | solution.py:387
  35.6 18.9 %collective-permute-start.2 = (bf16[8,128,128]{2,1,0:T(8,128)(2,1)S(1)}, bf16[8,128,128]{2,1,0:T(8,128)(2,1)S(1)}, u32[]{:S(2)}, u32[]{:S(2)}) collective-permute-start(bf16[8,128,128]{2,1,0:T(8,128)(2,1)S(1)} %all_to_all.15.refs_0_), channel_id=1, source_target_pairs={{0,3},{1,2},{2,1},{3,0},{4,7},{5,6},{6,5},{7,4},{8,11},{9,10},{10,... | collective-permute-start | bytes 786440 | tf_op jit(solution)/shard_map/ppermute | solution.py:387
  38.8 18.1 %collective-permute-start.7 = (bf16[272,128]{1,0:T(8,128)(2,1)S(1)}, bf16[272,128]{1,0:T(8,128)(2,1)S(1)}, u32[]{:S(2)}, u32[]{:S(2)}) collective-permute-start(bf16[272,128]{1,0:T(8,128)(2,1)S(1)} %get-tuple-element.21), channel_id=1, source_target_pairs={{0,32},{32,64},{64,96},{96,128},{128,160},{160,192},{192,224},{224... | collective-permute-start | bytes 208904 | tf_op jit(solution)/shard_map/ppermute | solution.py:372
  48.2 28.4 %collective-permute-start.3 = (bf16[8,128,128]{2,1,0:T(8,128)(2,1)S(1)}, bf16[8,128,128]{2,1,0:T(8,128)(2,1)S(1)}, u32[]{:S(2)}, u32[]{:S(2)}) collective-permute-start(bf16[8,128,128]{2,1,0:T(8,128)(2,1)S(1)} %all_to_all.15.refs_0_), channel_id=1, source_target_pairs={{0,32},{32,0},{1,33},{33,1},{2,34},{34,2},{3,35},{35,3},{4,36},{36... | collective-permute-start | bytes 786440 | tf_op jit(solution)/shard_map/ppermute | solution.py:389
  50.2 26.4 %collective-permute-start.4 = (bf16[8,128,128]{2,1,0:T(8,128)(2,1)S(1)}, bf16[8,128,128]{2,1,0:T(8,128)(2,1)S(1)}, u32[]{:S(2)}, u32[]{:S(2)}) collective-permute-start(bf16[8,128,128]{2,1,0:T(8,128)(2,1)S(1)} %collective-permute-done.refs_1_), channel_id=1, source_target_pairs={{0,32},{32,0},{1,33},{33,1},{2,34},{34,2},{3,35},{35,3},{4,36},{36... | collective-permute-start | bytes 786440 | tf_op jit(solution)/shard_map/ppermute | solution.py:389
  52.6 24.0 %collective-permute-start.5 = (bf16[8,128,128]{2,1,0:T(8,128)(2,1)S(1)}, bf16[8,128,128]{2,1,0:T(8,128)(2,1)S(1)}, u32[]{:S(2)}, u32[]{:S(2)}) collective-permute-start(bf16[8,128,128]{2,1,0:T(8,128)(2,1)S(1)} %collective-permute-done.1.refs_2_), channel_id=1, source_target_pairs={{0,32},{32,0},{1,33},{33,1},{2,34},{34,2},{3,35},{35,3},{4,36},{36... | collective-permute-start | bytes 786440 | tf_op jit(solution)/shard_map/ppermute | solution.py:389
  54.5 22.1 %collective-permute-start.6 = (bf16[8,128,128]{2,1,0:T(8,128)(2,1)S(1)}, bf16[8,128,128]{2,1,0:T(8,128)(2,1)S(1)}, u32[]{:S(2)}, u32[]{:S(2)}) collective-permute-start(bf16[8,128,128]{2,1,0:T(8,128)(2,1)S(1)} %collective-permute-done.2.refs_3_), channel_id=1, source_target_pairs={{0,32},{32,0},{1,33},{33,1},{2,34},{34,2},{3,35},{35,3},{4,36},{36... | collective-permute-start | bytes 786440 | tf_op jit(solution)/shard_map/ppermute | solution.py:389
  57.0 3.2 %collective-permute-start.8 = (bf16[272,128]{1,0:T(8,128)(2,1)S(1)}, bf16[272,128]{1,0:T(8,128)(2,1)S(1)}, u32[]{:S(2)}, u32[]{:S(2)}) collective-permute-start(bf16[272,128]{1,0:T(8,128)(2,1)S(1)} %get-tuple-element.23), channel_id=1, source_target_pairs={{0,64},{32,96},{64,128},{96,160},{128,192},{160,224},{192,256},{22... | collective-permute-start | bytes 208904 | tf_op jit(solution)/shard_map/ppermute | solution.py:372
  60.2 5.3 %collective-permute-start.9 = (bf16[272,128]{1,0:T(8,128)(2,1)S(1)}, bf16[272,128]{1,0:T(8,128)(2,1)S(1)}, u32[]{:S(2)}, u32[]{:S(2)}) collective-permute-start(bf16[272,128]{1,0:T(8,128)(2,1)S(1)} %get-tuple-element.26), channel_id=1, source_target_pairs={{0,128},{32,160},{64,192},{96,224},{128,256},{160,288},{192,320},{... | collective-permute-start | bytes 208904 | tf_op jit(solution)/shard_map/ppermute | solution.py:372
  65.6 8.6 %copy-start.4 = (bf16[256,256]{1,0:T(8,128)(2,1)S(1)}, bf16[256,256]{1,0:T(8,128)(2,1)}, u32[]{:S(2)}) copy-start(bf16[256,256]{1,0:T(8,128)(2,1)} %r_ref.3) | copy-start | bytes 393220
  65.6 8.6 %copy-start.6 = (bf16[256,256]{1,0:T(8,128)(2,1)S(1)}, bf16[256,256]{1,0:T(8,128)(2,1)}, u32[]{:S(2)}) copy-start(bf16[256,256]{1,0:T(8,128)(2,1)} %g_ref.1) | copy-start | bytes 393220
  66.2 7.9 %copy-start.13 = (f32[2]{0:T(128)S(1)}, f32[2]{0:T(128)}, u32[]{:S(2)}) copy-start(f32[2]{0:T(128)} %skip_ref.1) | copy-start | bytes 28
  66.2 9.3 %collective-permute-start.10 = (bf16[272,128]{1,0:T(8,128)(2,1)S(1)}, bf16[272,128]{1,0:T(8,128)(2,1)S(1)}, u32[]{:S(2)}, u32[]{:S(2)}) collective-permute-start(bf16[272,128]{1,0:T(8,128)(2,1)S(1)} %get-tuple-element.29), channel_id=1, source_target_pairs={{0,256},{32,288},{64,320},{96,352},{128,384},{160,416},{192,448},{... | collective-permute-start | bytes 208904 | tf_op jit(solution)/shard_map/ppermute | solution.py:372
  74.1 1.4 %copy-start.10 = (f32[256]{0:T(256)S(1)}, f32[256]{0:T(256)}, u32[]{:S(2)}) copy-start(f32[256]{0:T(256)} %param.26) | copy-start | bytes 3076
  75.5 0.7 copy-start.8
  76.2 0.9 copy-start.5
  76.6 0.7 copy-start.11
  92.0 0.7 copy-start.12

commit v2 on v1

--- a/solution.py
+++ b/solution.py
@@ -23,7 +23,7 @@
 HEAD = ("zh", "y", "x")
 VMEM = pl.BlockSpec(memory_space=pltpu.VMEM)
 SMEM = pl.BlockSpec(memory_space=pltpu.SMEM)
-ANY = pl.BlockSpec(memory_space=pl.ANY)
+HBM = pl.BlockSpec(memory_space=pltpu.HBM)
 NEG = -1e30
 FADE = 2 * DIM
 STATE_ROWS = FADE + 16
@@ -123,7 +123,9 @@
     send_ref[pl.ds(FADE, 16)] = jnp.concatenate([fades, jnp.zeros((8, DIM), F32)], axis=0).astype(BF16)
 
 
-def first_kernel(got_ref, t_ref, t_out, x_out, send_ref):
+def first_kernel(got_ref, t_ref, quarter_ref, t_out, x_out, send_ref, fan_ref):
+    for n in range(fan_ref.shape[0]):
+        fan_ref[n] = quarter_ref[...]
     merge(got_ref, t_ref, None, t_out, x_out, send_ref)
 
 
@@ -201,7 +203,9 @@
     ]
 
 
-def carried_kernel(got_ref, x_ref, r_ref, base_ref, carry_ref, gain_ref, readout_ref, gated_ref, stat_ref):
+def carried_kernel(
+    got_ref, x_ref, r_ref, base_ref, carry_ref, gain_ref, readout_ref, a_ref, gated_ref, send_ref
+):
     parts = []
     for h in range(2):
         rows, cols = pl.ds(h * DIM, DIM), pl.ds(h * DIM, DIM)
@@ -213,69 +217,107 @@
     gated = jnp.concatenate(parts, axis=1)
     gated_ref[...] = gated
     weight = gain_ref[...] * readout_ref[...]
-    stat_ref[...] = jnp.concatenate(to_lanes(gated * gated) + to_lanes(gated * weight), axis=0)
-
-
-def attend_kernel(q_ref, *refs):
-    own, other = refs[0:4], refs[4:8]
-    readout_ref, stat_ref, o_ref, send_ref, m_ref, l_ref, acc_ref = refs[8:]
-    zl, core, x = (lax.axis_index(a) for a in ("zl", "core", "x"))
+    stats = to_lanes(gated * gated) + to_lanes(gated * weight)
+    stats = jnp.concatenate(stats + [a_ref[...], jnp.zeros((2, DIM), F32)], axis=0)
+    for n in range(send_ref.shape[0]):
+        send_ref[n] = stats
+
+
+def keys_of(ref, k):
+    return jnp.concatenate([ref[n, k + i, 0:64] for i in range(2) for n in range(4)], axis=0)
+
+
+def values_of(ref, k):
+    return jnp.concatenate([ref[n, k + i, 64:128] for i in range(2) for n in range(4)], axis=0)
+
+
+def spread(q_ref, scaled_ref):
+    c = math.log2(math.e) / math.sqrt(DIM)
+    for h in range(2):
+        high, low = split(q_ref[:, h * DIM : (h + 1) * DIM].astype(F32) * c)
+        scaled_ref[pl.ds(h * 256, 256)] = jnp.concatenate([high, low], axis=1)
+
+
+def scan_keys(kv_ref, core, scaled_ref, scores_ref, m_ref, l_ref, acc_ref, fresh):
+    zl, here = lax.axis_index("zl"), lax.axis_index("core")
+    tiles = zl + 1 if fresh else zl + here
+    pairs = zl // 2 if fresh else tiles // 2
+    rows = scaled_ref.shape[0]
+
+    def lanes_max(s):
+        return jnp.maximum(
+            jnp.maximum(s[:, 0:128], s[:, 128:256]), jnp.maximum(s[:, 256:384], s[:, 384:512])
+        )
+
+    def scores(i):
+        keys = keys_of(kv_ref, 2 * i)
+        return dot(scaled_ref[...], jnp.concatenate([keys, keys], axis=1), 1, 1)
+
+    def first(i, _):
+        s = scores(i)
+        scores_ref[i] = s
+        m_ref[...] = jnp.maximum(m_ref[...], lanes_max(s))
+        return 0
+
+    def tail(i):
+        key = lax.broadcasted_iota(jnp.int32, (rows, 512), 1)
+        key = (i * 2) * 512 + core * 256 + jnp.where(key < 256, key, key + 256)
+        spot = lax.broadcasted_iota(jnp.int32, (rows, 512), 0)
+        spot = zl * 512 + here * 256 + jnp.where(spot < 256, spot, spot - 256)
+        s = jnp.where(key <= spot, scores(i), NEG)
+        scores_ref[i] = s
+        m_ref[...] = jnp.maximum(m_ref[...], lanes_max(s))
+
+    old = m_ref[...]
+    lax.fori_loop(0, pairs, first, 0)
+    ragged = 2 * pairs < tiles
+
+    @pl.when(ragged)
+    def _():
+        tail(pairs)
+
+    top = jnp.broadcast_to(jnp.max(m_ref[...], axis=1, keepdims=True), m_ref.shape)
+    if fresh:
+        l_ref[...] = jnp.zeros(l_ref.shape, F32)
+        acc_ref[...] = jnp.zeros(acc_ref.shape, F32)
+    else:
+        fade = jnp.exp2(old - top)
+        l_ref[...] = l_ref[...] * fade
+        acc_ref[...] = acc_ref[...] * fade
+    m_ref[...] = top
+
+    def second(i, _):
+        top = m_ref[...]
+        p = [jnp.exp2(scores_ref[i, :, n : n + 128] - top) for n in range(0, 512, 128)]
+        l_ref[...] += (p[0] + p[1]) + (p[2] + p[3])
+        weights = jnp.concatenate([v.astype(BF16) for v in p], axis=1)
+        acc_ref[...] += dot(weights, values_of(kv_ref, 2 * i))
+        return 0
+
+    lax.fori_loop(0, pairs + ragged.astype(jnp.int32), second, 0)
+
+
+def attend_own_kernel(q_ref, kv_ref, scaled_ref, m_ref, l_ref, acc_ref, scores_ref):
+    spread(q_ref, scaled_ref)
     m_ref[...] = jnp.full(m_ref.shape, NEG, F32)
-    l_ref[...] = jnp.zeros(l_ref.shape, F32)
-    acc_ref[...] = jnp.zeros(acc_ref.shape, F32)
-    c = math.log2(math.e) / math.sqrt(DIM)
-
-    def tile(k, masked):
-        keys = jnp.concatenate([ref[k, 0:64] for ref in own + other], axis=0)
-        values = jnp.concatenate([ref[k, 64:128] for ref in own + other], axis=0)
-        width = keys.shape[0]
-        if masked:
-            lane = lax.broadcasted_iota(jnp.int32, (128, 128), 1)
-            place = []
-            for n in range(2):
-                first = jnp.bitwise_xor(x, 2 * n) * 64
-                second = jnp.bitwise_xor(x, 2 * n + 1) * 64 - 64
-                place.append(lane + jnp.where(lane < 64, first, second))
-            far = jnp.full((128, 128), jnp.where(core == 1, 0, 1 << 20), jnp.int32)
-            place = jnp.concatenate(place + [far, far], axis=1)
-        for h in range(2):
-            for n in range(2):
-                rows = pl.ds(n * 128, 128)
-                at = pl.ds(h * 256 + n * 128, 128)
-                s = dot(q_ref[rows, pl.ds(h * DIM, DIM)], keys, 1, 1)
-                if masked:
-                    spot = lax.broadcasted_iota(jnp.int32, (128, width), 0) + n * 128
-                    s = jnp.where(place <= spot, s, NEG)
-                old = m_ref[at]
-                peak = jnp.max(s, axis=1, keepdims=True)
-                new = jnp.maximum(old, peak)
-                fade = jnp.exp2((old - new) * c)
-                m_ref[at] = new
-                p = jnp.concatenate(
-                    [jnp.exp2((s[:, i : i + 128] - new) * c) for i in range(0, width, 128)], axis=1
-                )
-                part = p[:, 0:128]
-                for i in range(128, width, 128):
-                    part = part + p[:, i : i + 128]
-                l_ref[at] = l_ref[at] * fade + part
-                acc_ref[at] = acc_ref[at] * fade + dot(p.astype(BF16), values)
-
-    def full(k, _):
-        tile(k, False)
-        return 0
-
-    lax.fori_loop(0, zl, full, 0)
-    tile(zl, True)
+    scan_keys(kv_ref, lax.axis_index("core"), scaled_ref, scores_ref, m_ref, l_ref, acc_ref, True)
+
+
+def attend_other_kernel(
+    scaled_ref, kv_ref, m_in, l_in, acc_in, readout_ref, o_ref, a_ref, m_ref, l_ref, acc_ref, scores_ref
+):
+    m_ref[...] = m_in[...]
+    l_ref[...] = l_in[...]
+    acc_ref[...] = acc_in[...]
+    other = 1 - lax.axis_index("core")
+    scan_keys(kv_ref, other, scaled_ref, scores_ref, m_ref, l_ref, acc_ref, False)
     parts = []
     for h in range(2):
         at = pl.ds(h * 256, 256)
         parts.append(acc_ref[at] / jnp.sum(l_ref[at], axis=1, keepdims=True))
     attended = jnp.concatenate(parts, axis=1).astype(BF16)
     o_ref[...] = attended
-    a = to_lanes(attended.astype(F32) * readout_ref[...])
-    stats = jnp.concatenate([stat_ref[...]] + a + [jnp.zeros((2, DIM), F32)], axis=0)
-    for n in range(send_ref.shape[0]):
-        send_ref[n] = stats
+    a_ref[...] = jnp.concatenate(to_lanes(attended.astype(F32) * readout_ref[...]), axis=0)
 
 
 def segment_row(values):
@@ -355,50 +397,61 @@
     chips, wide = lax.axis_size("zl"), lax.axis_size("x")
     ctx = chips * lax.axis_size("core")
 
-    packed = call(
-        pack_kernel,
-        shape((chips, DIM, DIM), BF16),
-        [ANY, ANY],
-        [pltpu.VMEM((DIM, DIM), BF16), pltpu.SemaphoreType.DMA((2,))],
-    )(key_rows, value_rows)
-    quarter = lax.all_to_all(packed, "zl", 0, 0)
-
+    together = lax.optimization_barrier
     state_shapes = (shape((FADE + 8, DIM)), shape((STATE_ROWS, DIM), BF16))
     own, send = call(states_kernel, state_shapes, [VMEM, VMEM, VMEM, SMEM])(
         state_input, state_write, codes, decay_rates
     )
+    packed = call(
+        pack_kernel,
+        shape((chips, DIM, DIM), BF16),
+        [HBM, HBM],
+        [pltpu.VMEM((DIM, DIM), BF16), pltpu.SemaphoreType.DMA((2,))],
+        mib=60,
+    )(key_rows, value_rows)
+    send, packed = together((send, packed))
 
     def shifted(v, by):
         return lax.ppermute(v, CTX, [(i, i + by) for i in range(ctx - by)])
 
+    got = shifted(send, 1)
+    quarter = lax.all_to_all(packed, "zl", 0, 0)
+    got, quarter = together((got, quarter))
     merged = (shape((FADE + 8, DIM)), shape((FADE + 8, DIM)), shape((STATE_ROWS, DIM), BF16))
-    got = shifted(send, 1)
-    t, before, send = call(first_kernel, merged, [VMEM] * 2)(got, own)
+    fan_shape = shape((wide, chips, DIM, DIM), BF16)
+    t, before, send, fan = call(first_kernel, merged + (fan_shape,), [VMEM] * 3)(got, own, quarter)
+
     got = shifted(send, 2)
+    mine = lax.all_to_all(fan, "x", 0, 0)
+    got, mine = together((got, mine))
+    t, before, send = call(middle_kernel, merged, [VMEM] * 3)(got, t, before)
+    send, mine = together((send, mine))
+
+    got = shifted(send, 4)
+    theirs = lax.ppermute(mine, "core", [(0, 1), (1, 0)])
+    running = (shape((512, 256), BF16),) + (shape((512, DIM)),) * 3
+    scores = pltpu.VMEM((chips // 2, 512, 512), F32)
+    attention = call(attend_own_kernel, running, [VMEM] * 2, [scores], flops=10**9)(queries, mine)
+    got, attention = together((got, attention))
+    t, before, send = call(middle_kernel, merged, [VMEM] * 3)(got, t, before)
+    send, theirs, attention, codes = together((send, theirs, attention, codes))
+
+    got = shifted(send, 8)
+    attended, a = call(
+        attend_other_kernel,
+        (shape((tokens, 256), BF16), shape((2, DIM))),
+        [VMEM] * 6,
+        [pltpu.VMEM((512, DIM), F32) for _ in range(3)] + [scores],
+        flops=10**9,
+    )(attention[0], theirs, *attention[1:], attend_out)
     base, carry = call(
         local_kernel, (shape((tokens, 256)), shape((tokens, 256))), [VMEM] * 5 + [SMEM] * 2
     )(state_input, state_write, state_read, gate_input, codes, decay_rates, skip_gain)
-    t, before, send = call(middle_kernel, merged, [VMEM] * 3)(got, t, before)
-    got = shifted(send, 4)
-    t, before, send = call(middle_kernel, merged, [VMEM] * 3)(got, t, before)
-    got = shifted(send, 8)
-
-    pieces = [quarter] + [
-        lax.ppermute(quarter, "x", [(i, i ^ k) for i in range(wide)]) for k in range(1, wide)
-    ]
-    others = [lax.ppermute(p, "core", [(0, 1), (1, 0)]) for p in pieces]
-
-    gated, stats = call(
-        carried_kernel, (shape((tokens, 256)), shape((4, DIM))), [VMEM] * 7
-    )(got, before, state_read, base, carry, gain, state_out)
-
+    got, a, base = together((got, a, base))
     head_plane = lax.axis_size("y") * wide
-    attended, send = call(
-        attend_kernel,
-        (shape((tokens, 256), BF16), shape((head_plane, 8, DIM))),
-        [VMEM] * 11,
-        [pltpu.VMEM((512, DIM), F32) for _ in range(3)],
-    )(queries, *pieces, *others, attend_out, stats)
+    gated, send = call(
+        carried_kernel, (shape((tokens, 256)), shape((head_plane, 8, DIM))), [VMEM] * 8
+    )(got, before, state_read, base, carry, gain, state_out, a)
     summed = lax.all_to_all(send, ("y", "x"), 0, 0)
     line = ctx * lax.axis_size("zh")
     send = call(middle_sums_kernel, shape((line, 8, DIM), BF16), [VMEM] * 2)(summed, seg)

time: 131 us -> 113 us (0.86)
  blocking collectives: 74.3 us -> 37.4 us
  waiting for transfers between devices: 2.72 us -> 15.1 us
  starting transfers between devices: 41.4 us -> 46.8 us
  Pallas kernels: 6.58 us -> 9.71 us
  local copies, waits for them, and re-layouts: 4.15 us -> 2.68 us
    all_to_all x1 -> x0, blocking collectives: 25.2 us -> none  [per_device(): quarter = lax.all_to_all(packed, 'zl', 0, 0)]
    all_to_all x0 -> x2, starting transfers between devices: none -> 17.1 us  [the longest x1 13.1 us: per_device(): quarter = lax.all_to_all(packed, 'zl', 0, 0)]
    all_to_all x0 -> x2, waiting for transfers between devices: none -> 11.1 us  [the longest x1 5.73 us: per_device(): quarter = lax.all_to_all(packed, 'zl', 0, 0)]
    all_to_all x1, blocking collectives: 36.4 us -> 26.2 us  [per_device(): summed = lax.all_to_all(send, ('zl', 'core', 'zh'), 0, 0)]
    ppermute x7 -> x1, starting transfers between devices: 18.4 us -> 8.91 us  [per_device(): theirs = lax.ppermute(mine, 'core', [(0, 1), (1, 0)])]
    pallas_call x4 -> x5, Pallas kernels: 2.42 us -> 5.56 us  [the longest x1 1.66 us: per_device(): call(attend_other_kernel, (shape((tokens, 256), BF16), shape((2, DIM))),...]
    ppermute x4, starting transfers between devices: 23.1 us -> 20.8 us  [shifted(): return lax.ppermute(v, CTX, [(i, i + by) for i in range(ctx - by)])]
    all_to_all x1, blocking collectives: 12.7 us -> 11.2 us  [per_device(): summed = lax.all_to_all(send, ('y', 'x'), 0, 0)]
  transfers between devices with their start and end apart: 11 -> 7, of which waited for: 2 -> 5; matrix products, arithmetic and copies ran while one was open for 0% -> 0% of each run, Pallas kernels for 3% -> 4%
where the time goes in v2:
time: 113 us
  starting transfers between devices  46.8 us (41%)
  blocking collectives  37.4 us (33%)
  waiting for transfers between devices  15.1 us (13%)
  Pallas kernels  9.71 us (9%)
  local copies, waits for them, and re-layouts  2.68 us (2%)
    all_to_all x1, blocking collectives, per_device(): summed = lax.all_to_all(send, ('zl', 'core', 'zh'), 0, 0)  26.2 us
    ppermute x4, starting transfers between devices, shifted(): return lax.ppermute(v, CTX, [(i, i + by) for i in range(ctx - by)])  20.8 us
    all_to_all x1, starting transfers between devices, per_device(): quarter = lax.all_to_all(packed, 'zl', 0, 0)  13.1 us
    all_to_all x1, blocking collectives, per_device(): summed = lax.all_to_all(send, ('y', 'x'), 0, 0)  11.2 us
    ppermute x1, starting transfers between devices, per_device(): theirs = lax.ppermute(mine, 'core', [(0, 1), (1, 0)])  8.91 us
    all_to_all x1, waiting for transfers between devices, per_device(): quarter = lax.all_to_all(packed, 'zl', 0, 0)  5.73 us
    all_to_all x1, waiting for transfers between devices, per_device(): mine = lax.all_to_all(fan, 'x', 0, 0)  5.34 us
    ppermute x4, waiting for transfers between devices, shifted(): return lax.ppermute(v, CTX, [(i, i + by) for i in range(ctx - by)])  4.04 us
  transfers between devices with their start and end apart: 7, of which 5 were waited for; matrix products, arithmetic and copies ran while one was open for 0% of the time, Pallas kernels for 4%

profile of v2, /device:TPU:1, one launch (start us, length us, event | category | flops | bytes accessed | tf_op | source)
XLA Modules:
  0.0 112.5 jit_solution(14468360963650852924)
XLA Ops:
  0.7 1.6 %shard_map.158 = bf16[8,128,128]{2,1,0:T(8,128)(2,1)} custom-call(bf16[256,1024]{1,0:T(8,128)(2,1)} %k_ref.1, bf16[256,1024]{1,0:T(8,128)(2,1)} %v_ref.1), custom_call_target="tpu_custom_call" | custom-call | flops 1000000 | bytes 1000000 | tf_op jit(solution)/shard_map/pallas_call | solution.py:405
  2.2 0.0 copy-start.6
  2.3 0.6 copy-done.6
  2.9 1.0 shard_map.157
  3.9 13.1 %all-to-all-start = ((bf16[8,128,128]{2,1,0:T(8,128)(2,1)}), bf16[8,128,128]{2,1,0:T(8,128)(2,1)S(1)}, u32[]{:S(2)}, u32[]{:S(2)}) async-start(bf16[8,128,128]{2,1,0:T(8,128)(2,1)} %shard_map.158), calls=%async_computation | async-start | bytes 524288 | tf_op jit(solution)/shard_map/all_to_all | solution.py:418
  17.0 4.5 %collective-permute-start = (bf16[272,128]{1,0:T(8,128)(2,1)S(1)}, bf16[272,128]{1,0:T(8,128)(2,1)S(1)}, u32[]{:S(2)}, u32[]{:S(2)}) collective-permute-start(bf16[272,128]{1,0:T(8,128)(2,1)S(1)} %get-tuple-element.50), channel_id=1, source_target_pairs={{0,32},{32,64},{64,96},{96,128},{128,160},{160,192},{192,224},{224... | collective-permute-start | bytes 208904 | tf_op jit(solution)/shard_map/ppermute | solution.py:415
  21.5 2.0 %collective-permute-done.got_ref = bf16[272,128]{1,0:T(8,128)(2,1)S(1)} collective-permute-done((bf16[272,128]{1,0:T(8,128)(2,1)S(1)}, bf16[272,128]{1,0:T(8,128)(2,1)S(1)}, u32[]{:S(2)}, u32[]{:S(2)}) %collective-permute-start) | collective-permute-done | bytes 69664 | tf_op jit(solution)/shard_map/ppermute | solution.py:415
  23.5 5.7 %all-to-all-done.quarter_ref = bf16[8,128,128]{2,1,0:T(8,128)(2,1)S(1)} async-done(((bf16[8,128,128]{2,1,0:T(8,128)(2,1)}), bf16[8,128,128]{2,1,0:T(8,128)(2,1)S(1)}, u32[]{:S(2)}, u32[]{:S(2)}) %all-to-all-start) | async-done | bytes 262176 | tf_op jit(solution)/shard_map/all_to_all | solution.py:418
  29.2 1.1 shard_map.159
  30.3 4.0 %all-to-all-start.1 = ((bf16[4,8,128,128]{3,2,1,0:T(8,128)(2,1)}), bf16[4,8,128,128]{3,2,1,0:T(8,128)(2,1)S(1)}, u32[]{:S(2)}, u32[]{:S(2)}) async-start(bf16[4,8,128,128]{3,2,1,0:T(8,128)(2,1)} %get-tuple-element.56), calls=%async_computation.1 | async-start | bytes 2097152 | tf_op jit(solution)/shard_map/all_to_all | solution.py:425
  34.3 3.0 %collective-permute-start.1 = (bf16[272,128]{1,0:T(8,128)(2,1)S(1)}, bf16[272,128]{1,0:T(8,128)(2,1)S(1)}, u32[]{:S(2)}, u32[]{:S(2)}) collective-permute-start(bf16[272,128]{1,0:T(8,128)(2,1)S(1)} %get-tuple-element.55), channel_id=1, source_target_pairs={{0,64},{32,96},{64,128},{96,160},{128,192},{160,224},{192,256},{22... | collective-permute-start | bytes 208904 | tf_op jit(solution)/shard_map/ppermute | solution.py:415
  37.4 1.3 %collective-permute-done.1.got_ref = bf16[272,128]{1,0:T(8,128)(2,1)S(1)} collective-permute-done((bf16[272,128]{1,0:T(8,128)(2,1)S(1)}, bf16[272,128]{1,0:T(8,128)(2,1)S(1)}, u32[]{:S(2)}, u32[]{:S(2)}) %collective-permute-start.1) | collective-permute-done | bytes 69664 | tf_op jit(solution)/shard_map/ppermute | solution.py:415
  38.7 5.3 %all-to-all-done.1.kv_ref = bf16[4,8,128,128]{3,2,1,0:T(8,128)(2,1)S(1)} async-done(((bf16[4,8,128,128]{3,2,1,0:T(8,128)(2,1)}), bf16[4,8,128,128]{3,2,1,0:T(8,128)(2,1)S(1)}, u32[]{:S(2)}, u32[]{:S(2)}) %all-to-all-start.1) | async-done | bytes 1048608 | tf_op jit(solution)/shard_map/all_to_all | solution.py:425
  44.1 8.9 %collective-permute-start.3 = (bf16[4,8,128,128]{3,2,1,0:T(8,128)(2,1)S(1)}, bf16[4,8,128,128]{3,2,1,0:T(8,128)(2,1)S(1)}, u32[]{:S(2)}, u32[]{:S(2)}) collective-permute-start(bf16[4,8,128,128]{3,2,1,0:T(8,128)(2,1)S(1)} %all-to-all-done.1.kv_ref), channel_id=1, source_target_pairs={{0,32},{32,0},{1,33},{33,1},{2,34},{34,2},{3,35},{35,3},{4,36},{36... | collective-permute-start | bytes 3145736 | tf_op jit(solution)/shard_map/ppermute | solution.py:431
  53.0 4.9 %collective-permute-start.2 = (bf16[272,128]{1,0:T(8,128)(2,1)S(1)}, bf16[272,128]{1,0:T(8,128)(2,1)S(1)}, u32[]{:S(2)}, u32[]{:S(2)}) collective-permute-start(bf16[272,128]{1,0:T(8,128)(2,1)S(1)} %get-tuple-element.62), channel_id=1, source_target_pairs={{0,128},{32,160},{64,192},{96,224},{128,256},{160,288},{192,320},{... | collective-permute-start | bytes 208904 | tf_op jit(solution)/shard_map/ppermute | solution.py:415
  58.0 0.9 shard_map.161
  58.8 0.7 collective-permute-done.2.got_ref
  59.5 0.7 shard_map.162
  60.2 0.0 collective-permute-done.3.kv_ref
  60.2 8.4 %collective-permute-start.4 = (bf16[272,128]{1,0:T(8,128)(2,1)S(1)}, bf16[272,128]{1,0:T(8,128)(2,1)S(1)}, u32[]{:S(2)}, u32[]{:S(2)}) collective-permute-start(bf16[272,128]{1,0:T(8,128)(2,1)S(1)} %get-tuple-element.82), channel_id=1, source_target_pairs={{0,256},{32,288},{64,320},{96,352},{128,384},{160,416},{192,448},{... | collective-permute-start | bytes 208904 | tf_op jit(solution)/shard_map/ppermute | solution.py:415
  68.6 1.4 %shard_map.164 = (f32[256,256]{1,0:T(8,128)S(1)}, f32[256,256]{1,0:T(8,128)S(1)}) custom-call(bf16[256,256]{1,0:T(8,128)(2,1)S(1)} %copy-done, bf16[256,256]{1,0:T(8,128)(2,1)S(1)} %copy-done.1, bf16[256,256]{1,0:T(8,128)(2,1)S(1)} %copy-done.2, bf16[256,256]{1,0:T(8,128)(2,1)S(1)} %copy-done.3, s32[2,256]{1,0:T(2,128)S(1)} %bitcast.7, f32[2]{0:T(128)S(1)} %copy-done.6, ...), custom_call_target="tpu_custom_call" | custom-call | flops 1000000 | bytes 1000000 | tf_op jit(solution)/shard_map/pallas_call | solution.py:447
  70.0 0.0 copy-start.11
  70.0 0.7 copy-done.11
  70.7 1.7 %shard_map.163 = (bf16[256,256]{1,0:T(8,128)(2,1)}, f32[2,128]{1,0:T(2,128)S(1)}) custom-call(bf16[512,256]{1,0:T(8,128)(2,1)S(1)} %get-tuple-element.76.scaled_ref, bf16[4,8,128,128]{3,2,1,0:T(8,128)(2,1)S(1)} %collective-permute-done.3.kv_ref, f32[512,128]{1,0:T(8,128)S(1)} %get-tuple-element.78.m_in, f32[512,128]{1,0:T(8,128)S(1)} %get-tuple-element.79.l_in, ...), custom_call_target="tpu_custom_call" | custom-call | flops 1000000000 | bytes 1000000 | tf_op jit(solution)/shard_map/pallas_call | solution.py:440
  72.3 0.0 collective-permute-done.4.got_ref
  72.4 0.7 copy-done.5
  73.0 0.4 shard_map.165
  73.4 11.2 %all_to_all.20.got_ref = f32[16,8,128]{2,1,0:T(8,128)S(1)} all-to-all(f32[16,8,128]{2,1,0:T(8,128)S(1)} %get-tuple-element.91), channel_id=1, replica_groups=mesh['zl'=8,'core'=2,'zh'=2,'y'=4,'x'=4] {'y','x'}, dimensions={0} | all-to-all | bytes 131072 | tf_op jit(solution)/shard_map/all_to_all | solution.py:455
  84.6 0.7 copy-done.8
  85.3 0.1 shard_map.166
  85.4 26.2 %all_to_all.21.got_ref = bf16[32,8,128]{2,1,0:T(8,128)(2,1)S(1)} all-to-all(bf16[32,8,128]{2,1,0:T(8,128)(2,1)S(1)} %shard_map.166), channel_id=1, replica_groups=mesh['zl'=8,'core'=2,'zh'=2,'y'=4,'x'=4] {'zl','core','zh'}, dimensions={0} | all-to-all | bytes 131072 | tf_op jit(solution)/shard_map/all_to_all | solution.py:458
  111.6 0.9 shard_map.167
  (19 shorter events, 0.1 us)
Async XLA Ops:
  0.6 1.6 %copy-start.1 = (bf16[256,256]{1,0:T(8,128)(2,1)S(1)}, bf16[256,256]{1,0:T(8,128)(2,1)}, u32[]{:S(2)}) copy-start(bf16[256,256]{1,0:T(8,128)(2,1)} %w_ref.3) | copy-start | bytes 393220
  0.6 1.6 %copy-start = (bf16[256,256]{1,0:T(8,128)(2,1)S(1)}, bf16[256,256]{1,0:T(8,128)(2,1)}, u32[]{:S(2)}) copy-start(bf16[256,256]{1,0:T(8,128)(2,1)} %x_ref.3) | copy-start | bytes 393220
  0.7 1.6 %copy-start.4 = (s32[256,2]{0,1:T(2,128)S(1)}, s32[256,2]{0,1:T(2,128)}, u32[]{:S(2)}) copy-start(s32[256,2]{0,1:T(2,128)} %param.21) | copy-start | bytes 6148
  2.2 0.7 copy-start.6
  3.9 25.3 %all-to-all-start = ((bf16[8,128,128]{2,1,0:T(8,128)(2,1)}), bf16[8,128,128]{2,1,0:T(8,128)(2,1)S(1)}, u32[]{:S(2)}, u32[]{:S(2)}) async-start(bf16[8,128,128]{2,1,0:T(8,128)(2,1)} %shard_map.158), calls=%async_computation | async-start | bytes 524288 | tf_op jit(solution)/shard_map/all_to_all | solution.py:418
  17.0 6.5 %collective-permute-start = (bf16[272,128]{1,0:T(8,128)(2,1)S(1)}, bf16[272,128]{1,0:T(8,128)(2,1)S(1)}, u32[]{:S(2)}, u32[]{:S(2)}) collective-permute-start(bf16[272,128]{1,0:T(8,128)(2,1)S(1)} %get-tuple-element.50), channel_id=1, source_target_pairs={{0,32},{32,64},{64,96},{96,128},{128,160},{160,192},{192,224},{224... | collective-permute-start | bytes 208904 | tf_op jit(solution)/shard_map/ppermute | solution.py:415
  30.3 13.8 %all-to-all-start.1 = ((bf16[4,8,128,128]{3,2,1,0:T(8,128)(2,1)}), bf16[4,8,128,128]{3,2,1,0:T(8,128)(2,1)S(1)}, u32[]{:S(2)}, u32[]{:S(2)}) async-start(bf16[4,8,128,128]{3,2,1,0:T(8,128)(2,1)} %get-tuple-element.56), calls=%async_computation.1 | async-start | bytes 2097152 | tf_op jit(solution)/shard_map/all_to_all | solution.py:425
  34.3 4.4 %collective-permute-start.1 = (bf16[272,128]{1,0:T(8,128)(2,1)S(1)}, bf16[272,128]{1,0:T(8,128)(2,1)S(1)}, u32[]{:S(2)}, u32[]{:S(2)}) collective-permute-start(bf16[272,128]{1,0:T(8,128)(2,1)S(1)} %get-tuple-element.55), channel_id=1, source_target_pairs={{0,64},{32,96},{64,128},{96,160},{128,192},{160,224},{192,256},{22... | collective-permute-start | bytes 208904 | tf_op jit(solution)/shard_map/ppermute | solution.py:415
  44.1 13.9 %copy-start.10 = (bf16[256,256]{1,0:T(8,128)(2,1)S(1)}, bf16[256,256]{1,0:T(8,128)(2,1)}, u32[]{:S(2)}) copy-start(bf16[256,256]{1,0:T(8,128)(2,1)} %q_ref.1) | copy-start | bytes 393220
  44.1 16.1 %collective-permute-start.3 = (bf16[4,8,128,128]{3,2,1,0:T(8,128)(2,1)S(1)}, bf16[4,8,128,128]{3,2,1,0:T(8,128)(2,1)S(1)}, u32[]{:S(2)}, u32[]{:S(2)}) collective-permute-start(bf16[4,8,128,128]{3,2,1,0:T(8,128)(2,1)S(1)} %all-to-all-done.1.kv_ref), channel_id=1, source_target_pairs={{0,32},{32,0},{1,33},{33,1},{2,34},{34,2},{3,35},{35,3},{4,36},{36... | collective-permute-start | bytes 3145736 | tf_op jit(solution)/shard_map/ppermute | solution.py:431
  53.0 6.5 %collective-permute-start.2 = (bf16[272,128]{1,0:T(8,128)(2,1)S(1)}, bf16[272,128]{1,0:T(8,128)(2,1)S(1)}, u32[]{:S(2)}, u32[]{:S(2)}) collective-permute-start(bf16[272,128]{1,0:T(8,128)(2,1)S(1)} %get-tuple-element.62), channel_id=1, source_target_pairs={{0,128},{32,160},{64,192},{96,224},{128,256},{160,288},{192,320},{... | collective-permute-start | bytes 208904 | tf_op jit(solution)/shard_map/ppermute | solution.py:415
  59.5 9.1 %copy-start.2 = (bf16[256,256]{1,0:T(8,128)(2,1)S(1)}, bf16[256,256]{1,0:T(8,128)(2,1)}, u32[]{:S(2)}) copy-start(bf16[256,256]{1,0:T(8,128)(2,1)} %r_ref.3) | copy-start | bytes 393220
  59.5 9.1 %copy-start.3 = (bf16[256,256]{1,0:T(8,128)(2,1)S(1)}, bf16[256,256]{1,0:T(8,128)(2,1)}, u32[]{:S(2)}) copy-start(bf16[256,256]{1,0:T(8,128)(2,1)} %g_ref.1) | copy-start | bytes 393220
  60.2 8.4 %copy-start.9 = (f32[2]{0:T(128)S(1)}, f32[2]{0:T(128)}, u32[]{:S(2)}) copy-start(f32[2]{0:T(128)} %skip_ref.1) | copy-start | bytes 28
  60.2 12.1 %collective-permute-start.4 = (bf16[272,128]{1,0:T(8,128)(2,1)S(1)}, bf16[272,128]{1,0:T(8,128)(2,1)S(1)}, u32[]{:S(2)}, u32[]{:S(2)}) collective-permute-start(bf16[272,128]{1,0:T(8,128)(2,1)S(1)} %get-tuple-element.82), channel_id=1, source_target_pairs={{0,256},{32,288},{64,320},{96,352},{128,384},{160,416},{192,448},{... | collective-permute-start | bytes 208904 | tf_op jit(solution)/shard_map/ppermute | solution.py:415
  70.0 0.7 copy-start.11
  70.7 1.7 %copy-start.7 = (f32[256]{0:T(256)S(1)}, f32[256]{0:T(256)}, u32[]{:S(2)}) copy-start(f32[256]{0:T(256)} %param.26) | copy-start | bytes 3076
  72.3 0.7 copy-start.5
  84.6 0.7 copy-start.8

commit v3 on v2

--- a/solution.py
+++ b/solution.py
@@ -38,7 +38,7 @@
         out_specs=[VMEM] * len(outs) if many else VMEM,
         scratch_shapes=scratch,
         cost_estimate=pl.CostEstimate(flops=flops, bytes_accessed=moved, transcendentals=0),
-        compiler_params=pltpu.CompilerParams(vmem_limit_bytes=mib * 2**20),
+        compiler_params=pltpu.CompilerParams(vmem_limit_bytes=int(mib * 2**20)),
     )
 
 
@@ -53,23 +53,6 @@
 def split(v):
     high = v.astype(BF16)
     return high, (v - high.astype(F32)).astype(BF16)
-
-
-def pack_kernel(k_ref, v_ref, o_ref, piece, sems):
-    group = lax.axis_index("zh") * 4 + lax.axis_index("y")
-    rows = pl.ds(pl.multiple_of(lax.axis_index("x") * 64, 64), 64)
-    cols = pl.ds(pl.multiple_of(group * DIM, DIM), DIM)
-    copies = [
-        pltpu.make_async_copy(ref.at[rows, cols], piece.at[pl.ds(64 * n, 64)], sems.at[n])
-        for n, ref in enumerate((k_ref, v_ref))
-    ]
-    for c in copies:
-        c.start()
-    for c in copies:
-        c.wait()
-    both = piece[...]
-    for n in range(o_ref.shape[0]):
-        o_ref[n] = both
 
 
 def code_sums(codes_ref):
@@ -94,7 +77,24 @@
     return lanes, jnp.transpose(lanes)
 
 
-def states_kernel(x_ref, w_ref, codes_ref, rates_ref, own_ref, send_ref):
+def entry_kernel(
+    x_ref, w_ref, codes_ref, rates_ref, k_ref, v_ref, gain_ref, state_out_ref, attend_out_ref, seg_ref,
+    own_ref, send_ref, packed_ref, rows_ref, seg_out, piece, sems,
+):
+    group = lax.axis_index("zh") * 4 + lax.axis_index("y")
+    quarter = pl.ds(pl.multiple_of(lax.axis_index("x") * 64, 64), 64)
+    columns = pl.ds(pl.multiple_of(group * DIM, DIM), DIM)
+    copies = [
+        pltpu.make_async_copy(ref.at[quarter, columns], piece.at[pl.ds(64 * n, 64)], sems.at[n])
+        for n, ref in enumerate((k_ref, v_ref))
+    ]
+    for c in copies:
+        c.start()
+    gain = gain_ref[...]
+    rows_ref[...] = jnp.concatenate(
+        [gain, gain * state_out_ref[...], attend_out_ref[...], jnp.zeros((5, 256), F32)], axis=0
+    )
+    seg_out[...] = seg_ref[...]
     sums = code_sums(codes_ref)
     row = lax.broadcasted_iota(jnp.int32, (8, DIM), 0)
     fades, marks = jnp.zeros((8, DIM), F32), jnp.zeros((8, DIM), F32)
@@ -121,12 +121,21 @@
         fades = jnp.where(row == 2 * h, high, jnp.where(row == 2 * h + 1, fade - high, fades))
     own_ref[pl.ds(FADE, 8)] = marks
     send_ref[pl.ds(FADE, 16)] = jnp.concatenate([fades, jnp.zeros((8, DIM), F32)], axis=0).astype(BF16)
-
-
-def first_kernel(got_ref, t_ref, quarter_ref, t_out, x_out, send_ref, fan_ref):
+    for c in copies:
+        c.wait()
+    both = piece[...]
+    for n in range(packed_ref.shape[0]):
+        packed_ref[n] = both
+
+
+def first_kernel(got_ref, t_ref, t_out, x_out, send_ref):
+    merge(got_ref, t_ref, None, t_out, x_out, send_ref)
+
+
+def fan_kernel(got_ref, t_ref, x_ref, quarter_ref, t_out, x_out, send_ref, fan_ref):
     for n in range(fan_ref.shape[0]):
         fan_ref[n] = quarter_ref[...]
-    merge(got_ref, t_ref, None, t_out, x_out, send_ref)
+    merge(got_ref, t_ref, x_ref, t_out, x_out, send_ref)
 
 
 def middle_kernel(got_ref, t_ref, x_ref, t_out, x_out, send_ref):
@@ -204,7 +213,7 @@
 
 
 def carried_kernel(
-    got_ref, x_ref, r_ref, base_ref, carry_ref, gain_ref, readout_ref, a_ref, gated_ref, send_ref
+    got_ref, x_ref, r_ref, base_ref, carry_ref, rows_ref, a_ref, gated_ref, send_ref
 ):
     parts = []
     for h in range(2):
@@ -216,7 +225,7 @@
         parts.append(base_ref[:, cols] + carry_ref[:, cols] * (dot(r, high) + dot(r, low)))
     gated = jnp.concatenate(parts, axis=1)
     gated_ref[...] = gated
-    weight = gain_ref[...] * readout_ref[...]
+    weight = rows_ref[1:2, :]
     stats = to_lanes(gated * gated) + to_lanes(gated * weight)
     stats = jnp.concatenate(stats + [a_ref[...], jnp.zeros((2, DIM), F32)], axis=0)
     for n in range(send_ref.shape[0]):
@@ -304,7 +313,7 @@
 
 
 def attend_other_kernel(
-    scaled_ref, kv_ref, m_in, l_in, acc_in, readout_ref, o_ref, a_ref, m_ref, l_ref, acc_ref, scores_ref
+    scaled_ref, kv_ref, m_in, l_in, acc_in, rows_ref, o_ref, a_ref, m_ref, l_ref, acc_ref, scores_ref
 ):
     m_ref[...] = m_in[...]
     l_ref[...] = l_in[...]
@@ -317,7 +326,7 @@
         parts.append(acc_ref[at] / jnp.sum(l_ref[at], axis=1, keepdims=True))
     attended = jnp.concatenate(parts, axis=1).astype(BF16)
     o_ref[...] = attended
-    a_ref[...] = jnp.concatenate(to_lanes(attended.astype(F32) * readout_ref[...]), axis=0)
+    a_ref[...] = jnp.concatenate(to_lanes(attended.astype(F32) * rows_ref[2:3, :]), axis=0)
 
 
 def segment_row(values):
@@ -341,10 +350,10 @@
         send_ref[n] = out
 
 
-def final_kernel(got_ref, gated_ref, gain_ref, o_ref, values_ref):
+def final_kernel(got_ref, gated_ref, rows_ref, o_ref, values_ref):
     index = lax.axis_index("zl") * 2 + lax.axis_index("core")
     mine = got_ref[2 * index].astype(F32) + got_ref[2 * index + 1].astype(F32)
-    gain = gain_ref[...]
+    gain = rows_ref[0:1, :]
     for b in range(2):
         rows = pl.ds(b * DIM, DIM)
         scale = lax.rsqrt(mine[b : b + 1] * (1.0 / COLUMNS) + EPS)
@@ -398,67 +407,67 @@
     ctx = chips * lax.axis_size("core")
 
     together = lax.optimization_barrier
-    state_shapes = (shape((FADE + 8, DIM)), shape((STATE_ROWS, DIM), BF16))
-    own, send = call(states_kernel, state_shapes, [VMEM, VMEM, VMEM, SMEM])(
-        state_input, state_write, codes, decay_rates
-    )
-    packed = call(
-        pack_kernel,
-        shape((chips, DIM, DIM), BF16),
-        [HBM, HBM],
+    own, send, packed, rows, seg = call(
+        entry_kernel,
+        (
+            shape((FADE + 8, DIM)),
+            shape((STATE_ROWS, DIM), BF16),
+            shape((chips, DIM, DIM), BF16),
+            shape((8, 256)),
+            shape((2, DIM), jnp.int32),
+        ),
+        [VMEM] * 3 + [SMEM] + [HBM] * 2 + [VMEM] * 4,
         [pltpu.VMEM((DIM, DIM), BF16), pltpu.SemaphoreType.DMA((2,))],
-        mib=60,
-    )(key_rows, value_rows)
-    send, packed = together((send, packed))
+        mib=53,
+    )(
+        state_input, state_write, codes, decay_rates, key_rows, value_rows, gain, state_out, attend_out, seg
+    )
 
     def shifted(v, by):
         return lax.ppermute(v, CTX, [(i, i + by) for i in range(ctx - by)])
 
+    merged = (shape((FADE + 8, DIM)), shape((FADE + 8, DIM)), shape((STATE_ROWS, DIM), BF16))
     got = shifted(send, 1)
     quarter = lax.all_to_all(packed, "zl", 0, 0)
+    t, before, send = call(first_kernel, merged, [VMEM] * 2)(got, own)
+    got = shifted(send, 2)
     got, quarter = together((got, quarter))
-    merged = (shape((FADE + 8, DIM)), shape((FADE + 8, DIM)), shape((STATE_ROWS, DIM), BF16))
     fan_shape = shape((wide, chips, DIM, DIM), BF16)
-    t, before, send, fan = call(first_kernel, merged + (fan_shape,), [VMEM] * 3)(got, own, quarter)
-
-    got = shifted(send, 2)
+    t, before, send, fan = call(fan_kernel, merged + (fan_shape,), [VMEM] * 4)(got, t, before, quarter)
+
     mine = lax.all_to_all(fan, "x", 0, 0)
-    got, mine = together((got, mine))
+    got = shifted(send, 4)
     t, before, send = call(middle_kernel, merged, [VMEM] * 3)(got, t, before)
-    send, mine = together((send, mine))
-
-    got = shifted(send, 4)
+    base, carry = call(
+        local_kernel, (shape((tokens, 256)), shape((tokens, 256))), [VMEM] * 5 + [SMEM] * 2
+    )(state_input, state_write, state_read, gate_input, codes, decay_rates, skip_gain)
+    send, base, mine = together((send, base, mine))
+
+    got = shifted(send, 8)
     theirs = lax.ppermute(mine, "core", [(0, 1), (1, 0)])
     running = (shape((512, 256), BF16),) + (shape((512, DIM)),) * 3
     scores = pltpu.VMEM((chips // 2, 512, 512), F32)
     attention = call(attend_own_kernel, running, [VMEM] * 2, [scores], flops=10**9)(queries, mine)
-    got, attention = together((got, attention))
-    t, before, send = call(middle_kernel, merged, [VMEM] * 3)(got, t, before)
-    send, theirs, attention, codes = together((send, theirs, attention, codes))
-
-    got = shifted(send, 8)
+    theirs, attention = together((theirs, attention))
     attended, a = call(
         attend_other_kernel,
         (shape((tokens, 256), BF16), shape((2, DIM))),
         [VMEM] * 6,
         [pltpu.VMEM((512, DIM), F32) for _ in range(3)] + [scores],
         flops=10**9,
-    )(attention[0], theirs, *attention[1:], attend_out)
-    base, carry = call(
-        local_kernel, (shape((tokens, 256)), shape((tokens, 256))), [VMEM] * 5 + [SMEM] * 2
-    )(state_input, state_write, state_read, gate_input, codes, decay_rates, skip_gain)
-    got, a, base = together((got, a, base))
+    )(attention[0], theirs, *attention[1:], rows)
+    got, a = together((got, a))
     head_plane = lax.axis_size("y") * wide
     gated, send = call(
-        carried_kernel, (shape((tokens, 256)), shape((head_plane, 8, DIM))), [VMEM] * 8
-    )(got, before, state_read, base, carry, gain, state_out, a)
+        carried_kernel, (shape((tokens, 256)), shape((head_plane, 8, DIM))), [VMEM] * 7
+    )(got, before, state_read, base, carry, rows, a)
     summed = lax.all_to_all(send, ("y", "x"), 0, 0)
     line = ctx * lax.axis_size("zh")
     send = call(middle_sums_kernel, shape((line, 8, DIM), BF16), [VMEM] * 2)(summed, seg)
     summed = lax.all_to_all(send, ("zl", "core", "zh"), 0, 0)
     state_mixed, values = call(
         final_kernel, (shape((tokens, 256), BF16), shape((1, SEGMENTS))), [VMEM] * 3
-    )(summed, gated, gain)
+    )(summed, gated, rows)
     return attended, state_mixed, values.reshape(SEGMENTS)
 
 

time: 113 us -> 105 us (0.929)
  waiting for transfers between devices: 15.1 us -> 5.13 us
  starting transfers between devices: 46.8 us -> 52.6 us
  blocking collectives: 37.4 us -> 33.7 us
    ppermute x4, starting transfers between devices: 20.8 us -> 28.7 us  [shifted(): return lax.ppermute(v, CTX, [(i, i + by) for i in range(ctx - by)])]
    all_to_all x1, waiting for transfers between devices: 5.73 us -> 0.01 us  [per_device(): quarter = lax.all_to_all(packed, 'zl', 0, 0)]
    all_to_all x1, blocking collectives: 26.2 us -> 22.4 us  [per_device(): summed = lax.all_to_all(send, ('zl', 'core', 'zh'), 0, 0)]
    all_to_all x1, waiting for transfers between devices: 5.34 us -> 1.77 us  [per_device(): mine = lax.all_to_all(fan, 'x', 0, 0)]
    ppermute x1, starting transfers between devices: 8.91 us -> 6.66 us  [per_device(): theirs = lax.ppermute(mine, 'core', [(0, 1), (1, 0)])]
    unnamed x24 -> x28, local copies, waits for them, and re-layouts: 2.68 us -> 2.54 us
  transfers between devices with their start and end apart: 7 -> 7, of which waited for: 5 -> 3; matrix products, arithmetic and copies ran while one was open for 0% -> 0% of each run, Pallas kernels for 4% -> 4%
where the time goes in v3:
time: 105 us; the launch traced here: 104 us
  starting transfers between devices  52.6 us (50%)
  blocking collectives  33.7 us (32%)
  Pallas kernels  9.49 us (9%)
  waiting for transfers between devices  5.13 us (5%)
  local copies, waits for them, and re-layouts  2.54 us (2%)
    ppermute x4, starting transfers between devices, shifted(): return lax.ppermute(v, CTX, [(i, i + by) for i in range(ctx - by)])  28.7 us
    all_to_all x1, blocking collectives, per_device(): summed = lax.all_to_all(send, ('zl', 'core', 'zh'), 0, 0)  22.4 us
    all_to_all x1, starting transfers between devices, per_device(): quarter = lax.all_to_all(packed, 'zl', 0, 0)  13.1 us
    all_to_all x1, blocking collectives, per_device(): summed = lax.all_to_all(send, ('y', 'x'), 0, 0)  11.3 us
    ppermute x1, starting transfers between devices, per_device(): theirs = lax.ppermute(mine, 'core', [(0, 1), (1, 0)])  6.66 us
    all_to_all x1, starting transfers between devices, per_device(): mine = lax.all_to_all(fan, 'x', 0, 0)  4.16 us
    ppermute x4, waiting for transfers between devices, shifted(): return lax.ppermute(v, CTX, [(i, i + by) for i in range(ctx - by)])  3.36 us
    unnamed x28, local copies, waits for them, and re-layouts  2.54 us
  transfers between devices with their start and end apart: 7, of which 3 were waited for; matrix products, arithmetic and copies ran while one was open for 0% of the time, Pallas kernels for 4%

profile of v3, /device:TPU:1, one launch (start us, length us, event | category | flops | bytes accessed | tf_op | source)
XLA Modules:
  0.0 104.3 jit_solution(12744474660096909385)
XLA Ops:
  0.7 0.6 copy-done.11
  1.3 0.0 copy-done.9
  1.3 0.0 copy-done.10
  1.3 0.0 copy-done.6
  1.4 0.0 copy-done.8
  1.4 0.9 copy-done
  2.3 0.9 copy-done.2
  3.2 2.4 %shard_map.157 = (f32[264,128]{1,0:T(8,128)S(1)}, bf16[272,128]{1,0:T(8,128)(2,1)S(1)}, bf16[8,128,128]{2,1,0:T(8,128)(2,1)}, f32[8,256]{1,0:T(8,128)S(1)}, s32[2,128]{1,0:T(2,128)S(1)}) custom-call(bf16[256,256]{1,0:T(8,128)(2,1)S(1)} %copy-done, bf16[256,256]{1,0:T(8,128)(2,1)S(1)} %copy-done.2, s32[2,256]{1,0:T(2,128)S(1)} %bitcast.6, f32[2]{0:T(128)S(1)} %copy-done.7, ...), custom_call_target="tpu_custom_call" | custom-call | flops 1000000 | bytes 1000000 | tf_op jit(solution)/shard_map/pallas_call | solution.py:410
  5.6 13.1 %all-to-all-start = ((bf16[8,128,128]{2,1,0:T(8,128)(2,1)}), bf16[8,128,128]{2,1,0:T(8,128)(2,1)S(1)}, u32[]{:S(2)}, u32[]{:S(2)}) async-start(bf16[8,128,128]{2,1,0:T(8,128)(2,1)} %get-tuple-element.44), calls=%async_computation | async-start | bytes 524288 | tf_op jit(solution)/shard_map/all_to_all | solution.py:431
  18.7 4.5 %collective-permute-start = (bf16[272,128]{1,0:T(8,128)(2,1)S(1)}, bf16[272,128]{1,0:T(8,128)(2,1)S(1)}, u32[]{:S(2)}, u32[]{:S(2)}) collective-permute-start(bf16[272,128]{1,0:T(8,128)(2,1)S(1)} %get-tuple-element.41), channel_id=1, source_target_pairs={{0,32},{32,64},{64,96},{96,128},{128,160},{160,192},{192,224},{224... | collective-permute-start | bytes 208904 | tf_op jit(solution)/shard_map/ppermute | solution.py:427
  23.1 2.0 %collective-permute-done.got_ref = bf16[272,128]{1,0:T(8,128)(2,1)S(1)} collective-permute-done((bf16[272,128]{1,0:T(8,128)(2,1)S(1)}, bf16[272,128]{1,0:T(8,128)(2,1)S(1)}, u32[]{:S(2)}, u32[]{:S(2)}) %collective-permute-start) | collective-permute-done | bytes 69664 | tf_op jit(solution)/shard_map/ppermute | solution.py:427
  25.2 6.5 %collective-permute-start.1 = (bf16[272,128]{1,0:T(8,128)(2,1)S(1)}, bf16[272,128]{1,0:T(8,128)(2,1)S(1)}, u32[]{:S(2)}, u32[]{:S(2)}) collective-permute-start(bf16[272,128]{1,0:T(8,128)(2,1)S(1)} %get-tuple-element.43), channel_id=1, source_target_pairs={{0,64},{32,96},{64,128},{96,160},{128,192},{160,224},{192,256},{22... | collective-permute-start | bytes 208904 | tf_op jit(solution)/shard_map/ppermute | solution.py:427
  31.7 1.3 %collective-permute-done.1.got_ref = bf16[272,128]{1,0:T(8,128)(2,1)S(1)} collective-permute-done((bf16[272,128]{1,0:T(8,128)(2,1)S(1)}, bf16[272,128]{1,0:T(8,128)(2,1)S(1)}, u32[]{:S(2)}, u32[]{:S(2)}) %collective-permute-start.1) | collective-permute-done | bytes 69664 | tf_op jit(solution)/shard_map/ppermute | solution.py:427
  33.0 1.1 %shard_map.159 = (f32[264,128]{1,0:T(8,128)S(1)}, f32[264,128]{1,0:T(8,128)S(1)}, bf16[272,128]{1,0:T(8,128)(2,1)S(1)}, bf16[4,8,128,128]{3,2,1,0:T(8,128)(2,1)}) custom-call(bf16[272,128]{1,0:T(8,128)(2,1)S(1)} %collective-permute-done.1.got_ref, f32[264,128]{1,0:T(8,128)S(1)} %get-tuple-element.46.t_ref, f32[264,128]{1,0:T(8,128)S(1)} %get-tuple-element.47.x_ref, ...), custom_call_target="tpu_custom_call" | custom-call | flops 1000000 | bytes 1000000 | tf_op jit(solution)/shard_map/pallas_call | solution.py:436
  34.2 4.2 %all-to-all-start.1 = ((bf16[4,8,128,128]{3,2,1,0:T(8,128)(2,1)}), bf16[4,8,128,128]{3,2,1,0:T(8,128)(2,1)S(1)}, u32[]{:S(2)}, u32[]{:S(2)}) async-start(bf16[4,8,128,128]{3,2,1,0:T(8,128)(2,1)} %get-tuple-element.54), calls=%async_computation.1 | async-start | bytes 2097152 | tf_op jit(solution)/shard_map/all_to_all | solution.py:438
  38.3 7.4 %collective-permute-start.2 = (bf16[272,128]{1,0:T(8,128)(2,1)S(1)}, bf16[272,128]{1,0:T(8,128)(2,1)S(1)}, u32[]{:S(2)}, u32[]{:S(2)}) collective-permute-start(bf16[272,128]{1,0:T(8,128)(2,1)S(1)} %get-tuple-element.49), channel_id=1, source_target_pairs={{0,128},{32,160},{64,192},{96,224},{128,256},{160,288},{192,320},{... | collective-permute-start | bytes 208904 | tf_op jit(solution)/shard_map/ppermute | solution.py:427
  45.8 1.4 %shard_map.161 = (f32[256,256]{1,0:T(8,128)S(1)}, f32[256,256]{1,0:T(8,128)S(1)}) custom-call(bf16[256,256]{1,0:T(8,128)(2,1)S(1)} %copy-done.1, bf16[256,256]{1,0:T(8,128)(2,1)S(1)} %copy-done.3, bf16[256,256]{1,0:T(8,128)(2,1)S(1)} %copy-done.4, bf16[256,256]{1,0:T(8,128)(2,1)S(1)} %copy-done.5, s32[2,256]{1,0:T(2,128)S(1)} %bitcast.7, f32[2]{0:T(128)S(1)} %copy-done.7, ...), custom_call_target="tpu_custom_call" | custom-call | flops 1000000 | bytes 1000000 | tf_op jit(solution)/shard_map/pallas_call | solution.py:441
  47.1 0.0 collective-permute-done.2.got_ref
  47.1 0.0 copy-start.13
  47.2 0.7 shard_map.160
  47.8 1.8 %all-to-all-done.1.kv_ref = bf16[4,8,128,128]{3,2,1,0:T(8,128)(2,1)S(1)} async-done(((bf16[4,8,128,128]{3,2,1,0:T(8,128)(2,1)}), bf16[4,8,128,128]{3,2,1,0:T(8,128)(2,1)S(1)}, u32[]{:S(2)}, u32[]{:S(2)}) %all-to-all-start.1) | async-done | bytes 1048608 | tf_op jit(solution)/shard_map/all_to_all | solution.py:438
  49.6 6.7 %collective-permute-start.3 = (bf16[4,8,128,128]{3,2,1,0:T(8,128)(2,1)S(1)}, bf16[4,8,128,128]{3,2,1,0:T(8,128)(2,1)S(1)}, u32[]{:S(2)}, u32[]{:S(2)}) collective-permute-start(bf16[4,8,128,128]{3,2,1,0:T(8,128)(2,1)S(1)} %all-to-all-done.1.kv_ref), channel_id=1, source_target_pairs={{0,32},{32,0},{1,33},{33,1},{2,34},{34,2},{3,35},{35,3},{4,36},{36... | collective-permute-start | bytes 3145736 | tf_op jit(solution)/shard_map/ppermute | solution.py:447
  56.3 10.3 %collective-permute-start.4 = (bf16[272,128]{1,0:T(8,128)(2,1)S(1)}, bf16[272,128]{1,0:T(8,128)(2,1)S(1)}, u32[]{:S(2)}, u32[]{:S(2)}) collective-permute-start(bf16[272,128]{1,0:T(8,128)(2,1)S(1)} %get-tuple-element.67), channel_id=1, source_target_pairs={{0,256},{32,288},{64,320},{96,352},{128,384},{160,416},{192,448},{... | collective-permute-start | bytes 208904 | tf_op jit(solution)/shard_map/ppermute | solution.py:427
  66.6 0.9 shard_map.162
  67.5 0.0 collective-permute-done.3.kv_ref
  67.5 1.7 %shard_map.163 = (bf16[256,256]{1,0:T(8,128)(2,1)}, f32[2,128]{1,0:T(2,128)S(1)}) custom-call(bf16[512,256]{1,0:T(8,128)(2,1)S(1)} %get-tuple-element.60.scaled_ref, bf16[4,8,128,128]{3,2,1,0:T(8,128)(2,1)S(1)} %collective-permute-done.3.kv_ref, f32[512,128]{1,0:T(8,128)S(1)} %get-tuple-element.62.m_in, f32[512,128]{1,0:T(8,128)S(1)} %get-tuple-element.63.l_in, ...), custom_call_target="tpu_custom_call" | custom-call | flops 1000000000 | bytes 1000000 | tf_op jit(solution)/shard_map/pallas_call | solution.py:452
  69.2 0.0 collective-permute-done.4.got_ref
  69.2 0.4 shard_map.164
  69.5 11.3 %all_to_all.20.got_ref = f32[16,8,128]{2,1,0:T(8,128)S(1)} all-to-all(f32[16,8,128]{2,1,0:T(8,128)S(1)} %get-tuple-element.74), channel_id=1, replica_groups=mesh['zl'=8,'core'=2,'zh'=2,'y'=4,'x'=4] {'y','x'}, dimensions={0} | all-to-all | bytes 131072 | tf_op jit(solution)/shard_map/all_to_all | solution.py:464
  80.9 0.1 shard_map.165
  81.0 22.4 %all_to_all.21.got_ref = bf16[32,8,128]{2,1,0:T(8,128)(2,1)S(1)} all-to-all(bf16[32,8,128]{2,1,0:T(8,128)(2,1)S(1)} %shard_map.165), channel_id=1, replica_groups=mesh['zl'=8,'core'=2,'zh'=2,'y'=4,'x'=4] {'zl','core','zh'}, dimensions={0} | all-to-all | bytes 131072 | tf_op jit(solution)/shard_map/all_to_all | solution.py:467
  103.4 0.9 shard_map.166
  (22 shorter events, 0.1 us)
Async XLA Ops:
  0.6 0.7 copy-start.11
  0.6 0.7 copy-start.9
  0.7 0.7 copy-start.10
  0.7 0.7 copy-start.6
  0.7 0.7 copy-start.7
  0.7 0.7 copy-start.8
  1.4 0.9 copy-start
  2.3 0.9 copy-start.2
  5.6 27.5 %all-to-all-start = ((bf16[8,128,128]{2,1,0:T(8,128)(2,1)}), bf16[8,128,128]{2,1,0:T(8,128)(2,1)S(1)}, u32[]{:S(2)}, u32[]{:S(2)}) async-start(bf16[8,128,128]{2,1,0:T(8,128)(2,1)} %get-tuple-element.44), calls=%async_computation | async-start | bytes 524288 | tf_op jit(solution)/shard_map/all_to_all | solution.py:431
  18.7 6.5 %collective-permute-start = (bf16[272,128]{1,0:T(8,128)(2,1)S(1)}, bf16[272,128]{1,0:T(8,128)(2,1)S(1)}, u32[]{:S(2)}, u32[]{:S(2)}) collective-permute-start(bf16[272,128]{1,0:T(8,128)(2,1)S(1)} %get-tuple-element.41), channel_id=1, source_target_pairs={{0,32},{32,64},{64,96},{96,128},{128,160},{160,192},{192,224},{224... | collective-permute-start | bytes 208904 | tf_op jit(solution)/shard_map/ppermute | solution.py:427
  25.2 7.8 %collective-permute-start.1 = (bf16[272,128]{1,0:T(8,128)(2,1)S(1)}, bf16[272,128]{1,0:T(8,128)(2,1)S(1)}, u32[]{:S(2)}, u32[]{:S(2)}) collective-permute-start(bf16[272,128]{1,0:T(8,128)(2,1)S(1)} %get-tuple-element.43), channel_id=1, source_target_pairs={{0,64},{32,96},{64,128},{96,160},{128,192},{160,224},{192,256},{22... | collective-permute-start | bytes 208904 | tf_op jit(solution)/shard_map/ppermute | solution.py:427
  34.1 11.6 %copy-start.1 = (bf16[256,256]{1,0:T(8,128)(2,1)S(1)}, bf16[256,256]{1,0:T(8,128)(2,1)}, u32[]{:S(2)}) copy-start(bf16[256,256]{1,0:T(8,128)(2,1)} %x_ref.3) | copy-start | bytes 393220
  34.2 11.6 %copy-start.3 = (bf16[256,256]{1,0:T(8,128)(2,1)S(1)}, bf16[256,256]{1,0:T(8,128)(2,1)}, u32[]{:S(2)}) copy-start(bf16[256,256]{1,0:T(8,128)(2,1)} %w_ref.3) | copy-start | bytes 393220
  34.2 11.6 %copy-start.4 = (bf16[256,256]{1,0:T(8,128)(2,1)S(1)}, bf16[256,256]{1,0:T(8,128)(2,1)}, u32[]{:S(2)}) copy-start(bf16[256,256]{1,0:T(8,128)(2,1)} %r_ref.3) | copy-start | bytes 393220
  34.2 11.6 %copy-start.5 = (bf16[256,256]{1,0:T(8,128)(2,1)S(1)}, bf16[256,256]{1,0:T(8,128)(2,1)}, u32[]{:S(2)}) copy-start(bf16[256,256]{1,0:T(8,128)(2,1)} %g_ref.1) | copy-start | bytes 393220
  34.2 15.4 %all-to-all-start.1 = ((bf16[4,8,128,128]{3,2,1,0:T(8,128)(2,1)}), bf16[4,8,128,128]{3,2,1,0:T(8,128)(2,1)S(1)}, u32[]{:S(2)}, u32[]{:S(2)}) async-start(bf16[4,8,128,128]{3,2,1,0:T(8,128)(2,1)} %get-tuple-element.54), calls=%async_computation.1 | async-start | bytes 2097152 | tf_op jit(solution)/shard_map/all_to_all | solution.py:438
  38.3 7.4 %copy-start.12 = (f32[2]{0:T(128)S(1)}, f32[2]{0:T(128)}, u32[]{:S(2)}) copy-start(f32[2]{0:T(128)} %skip_ref.1) | copy-start | bytes 28
  38.3 8.8 %collective-permute-start.2 = (bf16[272,128]{1,0:T(8,128)(2,1)S(1)}, bf16[272,128]{1,0:T(8,128)(2,1)S(1)}, u32[]{:S(2)}, u32[]{:S(2)}) collective-permute-start(bf16[272,128]{1,0:T(8,128)(2,1)S(1)} %get-tuple-element.49), channel_id=1, source_target_pairs={{0,128},{32,160},{64,192},{96,224},{128,256},{160,288},{192,320},{... | collective-permute-start | bytes 208904 | tf_op jit(solution)/shard_map/ppermute | solution.py:427
  47.1 19.5 %copy-start.13 = (bf16[256,256]{1,0:T(8,128)(2,1)S(1)}, bf16[256,256]{1,0:T(8,128)(2,1)}, u32[]{:S(2)}) copy-start(bf16[256,256]{1,0:T(8,128)(2,1)} %q_ref.1) | copy-start | bytes 393220
  49.6 17.9 %collective-permute-start.3 = (bf16[4,8,128,128]{3,2,1,0:T(8,128)(2,1)S(1)}, bf16[4,8,128,128]{3,2,1,0:T(8,128)(2,1)S(1)}, u32[]{:S(2)}, u32[]{:S(2)}) collective-permute-start(bf16[4,8,128,128]{3,2,1,0:T(8,128)(2,1)S(1)} %all-to-all-done.1.kv_ref), channel_id=1, source_target_pairs={{0,32},{32,0},{1,33},{33,1},{2,34},{34,2},{3,35},{35,3},{4,36},{36... | collective-permute-start | bytes 3145736 | tf_op jit(solution)/shard_map/ppermute | solution.py:447
  56.3 12.9 %collective-permute-start.4 = (bf16[272,128]{1,0:T(8,128)(2,1)S(1)}, bf16[272,128]{1,0:T(8,128)(2,1)S(1)}, u32[]{:S(2)}, u32[]{:S(2)}) collective-permute-start(bf16[272,128]{1,0:T(8,128)(2,1)S(1)} %get-tuple-element.67), channel_id=1, source_target_pairs={{0,256},{32,288},{64,320},{96,352},{128,384},{160,416},{192,448},{... | collective-permute-start | bytes 208904 | tf_op jit(solution)/shard_map/ppermute | solution.py:427

commit v4 on v3

--- a/solution.py
+++ b/solution.py
@@ -25,6 +25,8 @@
 SMEM = pl.BlockSpec(memory_space=pltpu.SMEM)
 HBM = pl.BlockSpec(memory_space=pltpu.HBM)
 NEG = -1e30
+CARRIED_FLOPS = 10_800_000_000
+ENTRY_MIB = 58
 FADE = 2 * DIM
 STATE_ROWS = FADE + 16
 
@@ -78,23 +80,26 @@
 
 
 def entry_kernel(
-    x_ref, w_ref, codes_ref, rates_ref, k_ref, v_ref, gain_ref, state_out_ref, attend_out_ref, seg_ref,
-    own_ref, send_ref, packed_ref, rows_ref, seg_out, piece, sems,
+    rates_ref, k_hbm, v_hbm, x_hbm, w_hbm, codes_hbm, gain_hbm, state_out_hbm, attend_out_hbm, seg_hbm,
+    own_ref, send_ref, packed_ref, rows_ref,
+    piece, x_ref, w_ref, codes_ref, gain_ref, state_out_ref, attend_out_ref, seg_ref, sems,
 ):
     group = lax.axis_index("zh") * 4 + lax.axis_index("y")
     quarter = pl.ds(pl.multiple_of(lax.axis_index("x") * 64, 64), 64)
     columns = pl.ds(pl.multiple_of(group * DIM, DIM), DIM)
-    copies = [
-        pltpu.make_async_copy(ref.at[quarter, columns], piece.at[pl.ds(64 * n, 64)], sems.at[n])
-        for n, ref in enumerate((k_ref, v_ref))
+    pairs = [(codes_hbm, codes_ref), (x_hbm, x_ref), (w_hbm, w_ref)]
+    pairs += [(ref.at[quarter, columns], piece.at[pl.ds(64 * n, 64)]) for n, ref in enumerate((k_hbm, v_hbm))]
+    pairs += [
+        (gain_hbm, gain_ref),
+        (state_out_hbm, state_out_ref),
+        (attend_out_hbm, attend_out_ref),
+        (seg_hbm, seg_ref),
     ]
+    copies = [pltpu.make_async_copy(*pair, sems.at[n]) for n, pair in enumerate(pairs)]
     for c in copies:
         c.start()
-    gain = gain_ref[...]
-    rows_ref[...] = jnp.concatenate(
-        [gain, gain * state_out_ref[...], attend_out_ref[...], jnp.zeros((5, 256), F32)], axis=0
-    )
-    seg_out[...] = seg_ref[...]
+    for c in copies[:3]:
+        c.wait()
     sums = code_sums(codes_ref)
     row = lax.broadcasted_iota(jnp.int32, (8, DIM), 0)
     fades, marks = jnp.zeros((8, DIM), F32), jnp.zeros((8, DIM), F32)
@@ -121,53 +126,42 @@
         fades = jnp.where(row == 2 * h, high, jnp.where(row == 2 * h + 1, fade - high, fades))
     own_ref[pl.ds(FADE, 8)] = marks
     send_ref[pl.ds(FADE, 16)] = jnp.concatenate([fades, jnp.zeros((8, DIM), F32)], axis=0).astype(BF16)
-    for c in copies:
+    for c in copies[3:]:
         c.wait()
     both = piece[...]
     for n in range(packed_ref.shape[0]):
         packed_ref[n] = both
-
-
-def first_kernel(got_ref, t_ref, t_out, x_out, send_ref):
-    merge(got_ref, t_ref, None, t_out, x_out, send_ref)
-
-
-def fan_kernel(got_ref, t_ref, x_ref, quarter_ref, t_out, x_out, send_ref, fan_ref):
+    gain = gain_ref[...]
+    rows_ref[...] = jnp.concatenate(
+        [gain, gain * state_out_ref[...], attend_out_ref[...], seg_ref[...].astype(F32), jnp.zeros((4, 256), F32)],
+        axis=0,
+    )
+
+
+def fan_kernel(
+    got1_ref, got2_ref, got3_ref, own_ref, quarter_ref, rows_ref, x_out, send_ref, fan_ref, rows_out
+):
+    rows_out[...] = rows_ref[...]
     for n in range(fan_ref.shape[0]):
         fan_ref[n] = quarter_ref[...]
-    merge(got_ref, t_ref, x_ref, t_out, x_out, send_ref)
-
-
-def middle_kernel(got_ref, t_ref, x_ref, t_out, x_out, send_ref):
-    merge(got_ref, t_ref, x_ref, t_out, x_out, send_ref)
-
-
-def merge(got_ref, t_ref, x_ref, t_out, x_out, send_ref):
-    got_fades = got_ref[pl.ds(FADE, 16)].astype(F32)
+    refs = (got1_ref, got2_ref, got3_ref)
+    sent = [ref[pl.ds(FADE, 16)].astype(F32) for ref in refs]
     row = lax.broadcasted_iota(jnp.int32, (8, DIM), 0)
-    fades, marks_t, marks_x = (jnp.zeros((8, DIM), F32) for _ in range(3))
+    fades, marks = jnp.zeros((8, DIM), F32), jnp.zeros((8, DIM), F32)
     for h in range(2):
         rows = pl.ds(h * DIM, DIM)
-        got = got_ref[rows].astype(F32)
-        got_fade = got_fades[2 * h : 2 * h + 1] + got_fades[2 * h + 1 : 2 * h + 2]
-        mine = t_ref[pl.ds(FADE, 8)][h : h + 1]
-        state = mine * got + t_ref[rows]
-        t_out[rows] = state
-        send_ref[rows] = state.astype(BF16)
-        fade = mine * got_fade
-        if x_ref is None:
-            x_out[rows] = got
-            x_fade = got_fade
-        else:
-            before = x_ref[pl.ds(FADE, 8)][h : h + 1]
-            x_out[rows] = before * got + x_ref[rows]
-            x_fade = before * got_fade
+        f1, f2, f3 = (v[2 * h : 2 * h + 1] + v[2 * h + 1 : 2 * h + 2] for v in sent)
+        g1, g2, g3 = (ref[rows].astype(F32) for ref in refs)
+        before = g1 + f1 * (g2 + f2 * g3)
+        x_out[rows] = before
+        own = own_ref[pl.ds(FADE, 8)][h : h + 1]
+        send_ref[rows] = (own * before + own_ref[rows]).astype(BF16)
+        past = f1 * f2 * f3
+        marks = jnp.where(row == h, past, marks)
+        fade = own * past
         high = fade.astype(BF16).astype(F32)
-        marks_t = jnp.where(row == h, fade, marks_t)
-        marks_x = jnp.where(row == h, x_fade, marks_x)
         fades = jnp.where(row == 2 * h, high, jnp.where(row == 2 * h + 1, fade - high, fades))
-    t_out[pl.ds(FADE, 8)] = marks_t
-    x_out[pl.ds(FADE, 8)] = marks_x
+    x_out[pl.ds(FADE, 8)] = marks
     send_ref[pl.ds(FADE, 16)] = jnp.concatenate([fades, jnp.zeros((8, DIM), F32)], axis=0).astype(BF16)
 
 
@@ -213,23 +207,24 @@
 
 
 def carried_kernel(
-    got_ref, x_ref, r_ref, base_ref, carry_ref, rows_ref, a_ref, gated_ref, send_ref
+    near_ref, mid_ref, far_ref, x_ref, r_ref, base_ref, carry_ref, rows_ref, gated_ref, stats_ref
 ):
     parts = []
+    near, mid = near_ref[pl.ds(FADE, 16)].astype(F32), mid_ref[pl.ds(FADE, 16)].astype(F32)
     for h in range(2):
         rows, cols = pl.ds(h * DIM, DIM), pl.ds(h * DIM, DIM)
-        before = x_ref[pl.ds(FADE, 8)][h : h + 1]
-        entering = before * got_ref[rows].astype(F32) + x_ref[rows]
+        entering = far_ref[rows].astype(F32)
+        for ref, fades in ((mid_ref, mid), (near_ref, near)):
+            fade = fades[2 * h : 2 * h + 1] + fades[2 * h + 1 : 2 * h + 2]
+            entering = fade * entering + ref[rows].astype(F32)
+        entering = x_ref[pl.ds(FADE, 8)][h : h + 1] * entering + x_ref[rows]
         high, low = split(entering)
         r = r_ref[:, cols]
         parts.append(base_ref[:, cols] + carry_ref[:, cols] * (dot(r, high) + dot(r, low)))
     gated = jnp.concatenate(parts, axis=1)
     gated_ref[...] = gated
     weight = rows_ref[1:2, :]
-    stats = to_lanes(gated * gated) + to_lanes(gated * weight)
-    stats = jnp.concatenate(stats + [a_ref[...], jnp.zeros((2, DIM), F32)], axis=0)
-    for n in range(send_ref.shape[0]):
-        send_ref[n] = stats
+    stats_ref[...] = jnp.concatenate(to_lanes(gated * gated) + to_lanes(gated * weight), axis=0)
 
 
 def keys_of(ref, k):
@@ -313,7 +308,8 @@
 
 
 def attend_other_kernel(
-    scaled_ref, kv_ref, m_in, l_in, acc_in, rows_ref, o_ref, a_ref, m_ref, l_ref, acc_ref, scores_ref
+    scaled_ref, kv_ref, m_in, l_in, acc_in, rows_ref, stats_ref,
+    o_ref, send_ref, m_ref, l_ref, acc_ref, scores_ref,
 ):
     m_ref[...] = m_in[...]
     l_ref[...] = l_in[...]
@@ -326,7 +322,10 @@
         parts.append(acc_ref[at] / jnp.sum(l_ref[at], axis=1, keepdims=True))
     attended = jnp.concatenate(parts, axis=1).astype(BF16)
     o_ref[...] = attended
-    a_ref[...] = jnp.concatenate(to_lanes(attended.astype(F32) * rows_ref[2:3, :]), axis=0)
+    a = to_lanes(attended.astype(F32) * rows_ref[2:3, :])
+    stats = jnp.concatenate([stats_ref[...]] + a + [jnp.zeros((2, DIM), F32)], axis=0)
+    for n in range(send_ref.shape[0]):
+        send_ref[n] = stats
 
 
 def segment_row(values):
@@ -334,18 +333,19 @@
     return jnp.sum(jnp.transpose(full), axis=0, keepdims=True)
 
 
-def middle_sums_kernel(got_ref, seg_ref, send_ref):
+def middle_sums_kernel(got_ref, rows_ref, send_ref):
     total = got_ref[0]
     for n in range(1, got_ref.shape[0]):
         total = total + got_ref[n]
     segment = lax.broadcasted_iota(jnp.int32, (SEGMENTS, DIM), 0)
-    seg = seg_ref[...]
+    seg = jnp.concatenate([rows_ref[3:4, :DIM], rows_ref[3:4, DIM:]], axis=0)
+    held = seg.astype(jnp.int32)
     part = jnp.zeros((SEGMENTS, DIM), F32)
     for j in range(2):
-        part = part + jnp.where(seg[j : j + 1] == segment, total[4 + j : 5 + j], 0.0)
+        part = part + jnp.where(held[j : j + 1] == segment, total[4 + j : 5 + j], 0.0)
     part = segment_row(part)
     high = part.astype(BF16).astype(F32)
-    out = jnp.concatenate([total[0:4], high, part - high, seg.astype(F32)], axis=0).astype(BF16)
+    out = jnp.concatenate([total[0:4], high, part - high, seg], axis=0).astype(BF16)
     for n in range(send_ref.shape[0]):
         send_ref[n] = out
 
@@ -399,7 +399,7 @@
 ):
     tokens = queries.shape[0]
     codes = decay_codes.T
-    seg = segment_index.reshape(2, DIM)
+    seg = segment_index.reshape(1, 256)
     gain = norm_gain.reshape(1, 256)
     state_out = state_readout.reshape(1, 256)
     attend_out = attend_readout.reshape(1, 256)
@@ -407,63 +407,72 @@
     ctx = chips * lax.axis_size("core")
 
     together = lax.optimization_barrier
-    own, send, packed, rows, seg = call(
+    own, send, packed, rows = call(
         entry_kernel,
         (
             shape((FADE + 8, DIM)),
             shape((STATE_ROWS, DIM), BF16),
             shape((chips, DIM, DIM), BF16),
             shape((8, 256)),
-            shape((2, DIM), jnp.int32),
         ),
-        [VMEM] * 3 + [SMEM] + [HBM] * 2 + [VMEM] * 4,
-        [pltpu.VMEM((DIM, DIM), BF16), pltpu.SemaphoreType.DMA((2,))],
-        mib=53,
-    )(
-        state_input, state_write, codes, decay_rates, key_rows, value_rows, gain, state_out, attend_out, seg
-    )
+        [SMEM] + [HBM] * 9,
+        [
+            pltpu.VMEM((DIM, DIM), BF16),
+            pltpu.VMEM((tokens, 256), BF16),
+            pltpu.VMEM((tokens, 256), BF16),
+            pltpu.VMEM((2, tokens), jnp.int32),
+            pltpu.VMEM((1, 256), F32),
+            pltpu.VMEM((1, 256), F32),
+            pltpu.VMEM((1, 256), F32),
+            pltpu.VMEM((1, 256), jnp.int32),
+            pltpu.SemaphoreType.DMA((9,)),
+        ],
+        mib=ENTRY_MIB,
+    )(decay_rates, key_rows, value_rows, state_input, state_write, codes, gain, state_out, attend_out, seg)
 
     def shifted(v, by):
         return lax.ppermute(v, CTX, [(i, i + by) for i in range(ctx - by)])
 
-    merged = (shape((FADE + 8, DIM)), shape((FADE + 8, DIM)), shape((STATE_ROWS, DIM), BF16))
-    got = shifted(send, 1)
     quarter = lax.all_to_all(packed, "zl", 0, 0)
-    t, before, send = call(first_kernel, merged, [VMEM] * 2)(got, own)
-    got = shifted(send, 2)
-    got, quarter = together((got, quarter))
-    fan_shape = shape((wide, chips, DIM, DIM), BF16)
-    t, before, send, fan = call(fan_kernel, merged + (fan_shape,), [VMEM] * 4)(got, t, before, quarter)
-
-    mine = lax.all_to_all(fan, "x", 0, 0)
-    got = shifted(send, 4)
-    t, before, send = call(middle_kernel, merged, [VMEM] * 3)(got, t, before)
+    got = tuple(shifted(send, by) for by in (3, 2, 1))
     base, carry = call(
         local_kernel, (shape((tokens, 256)), shape((tokens, 256))), [VMEM] * 5 + [SMEM] * 2
     )(state_input, state_write, state_read, gate_input, codes, decay_rates, skip_gain)
-    send, base, mine = together((send, base, mine))
-
-    got = shifted(send, 8)
+    got, quarter, base = together((got, quarter, base))
+    before, send, fan, rows = call(
+        fan_kernel,
+        (
+            shape((FADE + 8, DIM)),
+            shape((STATE_ROWS, DIM), BF16),
+            shape((wide, chips, DIM, DIM), BF16),
+            shape((8, 256)),
+        ),
+        [VMEM] * 6,
+    )(*got[::-1], own, quarter, rows)
+
+    mine = lax.all_to_all(fan, "x", 0, 0)
+    arrived = tuple(shifted(send, by) for by in (4, 8, 12))
     theirs = lax.ppermute(mine, "core", [(0, 1), (1, 0)])
     running = (shape((512, 256), BF16),) + (shape((512, DIM)),) * 3
     scores = pltpu.VMEM((chips // 2, 512, 512), F32)
     attention = call(attend_own_kernel, running, [VMEM] * 2, [scores], flops=10**9)(queries, mine)
-    theirs, attention = together((theirs, attention))
-    attended, a = call(
+    arrived, attention = together((arrived, attention))
+    near, mid, far = arrived
+    gated, stats = call(
+        carried_kernel, (shape((tokens, 256)), shape((4, DIM))), [VMEM] * 8, flops=CARRIED_FLOPS
+    )(near, mid, far, before, state_read, base, carry, rows)
+    theirs, attention, stats = together((theirs, attention, stats))
+    head_plane = lax.axis_size("y") * wide
+    attended, send = call(
         attend_other_kernel,
-        (shape((tokens, 256), BF16), shape((2, DIM))),
-        [VMEM] * 6,
+        (shape((tokens, 256), BF16), shape((head_plane, 8, DIM))),
+        [VMEM] * 7,
         [pltpu.VMEM((512, DIM), F32) for _ in range(3)] + [scores],
         flops=10**9,
-    )(attention[0], theirs, *attention[1:], rows)
-    got, a = together((got, a))
-    head_plane = lax.axis_size("y") * wide
-    gated, send = call(
-        carried_kernel, (shape((tokens, 256)), shape((head_plane, 8, DIM))), [VMEM] * 7
-    )(got, before, state_read, base, carry, rows, a)
+    )(attention[0], theirs, *attention[1:], rows, stats)
     summed = lax.all_to_all(send, ("y", "x"), 0, 0)
     line = ctx * lax.axis_size("zh")
-    send = call(middle_sums_kernel, shape((line, 8, DIM), BF16), [VMEM] * 2)(summed, seg)
+    send = call(middle_sums_kernel, shape((line, 8, DIM), BF16), [VMEM] * 2)(summed, rows)
     summed = lax.all_to_all(send, ("zl", "core", "zh"), 0, 0)
     state_mixed, values = call(
         final_kernel, (shape((tokens, 256), BF16), shape((1, SEGMENTS))), [VMEM] * 3

time: 105 us -> 96.7 us (0.921)
  starting transfers between devices: 52.6 us -> 47.1 us
  waiting for transfers between devices: 5.13 us -> 1.3 us
  blocking collectives: 33.7 us -> 37.2 us
  local copies, waits for them, and re-layouts: 2.54 us -> 0.05 us
    ppermute x4 -> x6, starting transfers between devices: 28.7 us -> 24.3 us  [shifted(): return lax.ppermute(v, CTX, [(i, i + by) for i in range(ctx - by)])]
    ppermute x4 -> x6, waiting for transfers between devices: 3.36 us -> 0.32 us  [shifted(): return lax.ppermute(v, CTX, [(i, i + by) for i in range(ctx - by)])]
    unnamed x28 -> x20, local copies, waits for them, and re-layouts: 2.54 us -> 0.05 us
    all_to_all x1, blocking collectives: 11.3 us -> 13.6 us  [per_device(): summed = lax.all_to_all(send, ('y', 'x'), 0, 0)]
    all_to_all x1, waiting for transfers between devices: 1.77 us -> 0.01 us  [per_device(): mine = lax.all_to_all(fan, 'x', 0, 0)]
    all_to_all x1, blocking collectives: 22.4 us -> 23.6 us  [per_device(): summed = lax.all_to_all(send, ('zl', 'core', 'zh'), 0, 0)]
    ppermute x1, starting transfers between devices: 6.66 us -> 5.49 us  [per_device(): theirs = lax.ppermute(mine, 'core', [(0, 1), (1, 0)])]
    pallas_call x5 -> x3, Pallas kernels: 3.85 us -> 3.19 us  [the longest x1 1.66 us: per_device(): call(attend_other_kernel, (shape((tokens, 256), BF16), shape((head_plane,...]
  transfers between devices with their start and end apart: 7 -> 9, of which waited for: 3 -> 2; matrix products, arithmetic and copies ran while one was open for 0% -> 0% of each run, Pallas kernels for 4% -> 3%
where the time goes in v4:
time: 96.7 us; the launch traced here: 96.1 us
  starting transfers between devices  47.1 us (49%)
  blocking collectives  37.2 us (38%)
  Pallas kernels  9.58 us (10%)
  waiting for transfers between devices  1.3 us (1%)
    ppermute x6, starting transfers between devices, shifted(): return lax.ppermute(v, CTX, [(i, i + by) for i in range(ctx - by)])  24.3 us
    all_to_all x1, blocking collectives, per_device(): summed = lax.all_to_all(send, ('zl', 'core', 'zh'), 0, 0)  23.6 us
    all_to_all x1, blocking collectives, per_device(): summed = lax.all_to_all(send, ('y', 'x'), 0, 0)  13.6 us
    all_to_all x1, starting transfers between devices, per_device(): quarter = lax.all_to_all(packed, 'zl', 0, 0)  13.2 us
    ppermute x1, starting transfers between devices, per_device(): theirs = lax.ppermute(mine, 'core', [(0, 1), (1, 0)])  5.49 us
    all_to_all x1, starting transfers between devices, per_device(): mine = lax.all_to_all(fan, 'x', 0, 0)  4.15 us
    pallas_call x1, Pallas kernels, per_device(): call(entry_kernel, (shape((FADE + 8, DIM)), shape((STATE_ROWS, DIM), BF16...  3.12 us
  transfers between devices with their start and end apart: 9, of which 2 were waited for; matrix products, arithmetic and copies ran while one was open for 0% of the time, Pallas kernels for 3%

profile of v4, /device:TPU:1, one launch (start us, length us, event | category | flops | bytes accessed | tf_op | source)
XLA Modules:
  0.0 96.1 jit_solution(15116983079228834181)
XLA Ops:
  0.6 3.1 %shard_map.157 = (f32[264,128]{1,0:T(8,128)}, bf16[272,128]{1,0:T(8,128)(2,1)}, bf16[8,128,128]{2,1,0:T(8,128)(2,1)}, f32[8,256]{1,0:T(8,128)}) custom-call(f32[2]{0:T(128)} %rates_ref.3, bf16[256,1024]{1,0:T(8,128)(2,1)} %k_hbm.1, bf16[256,1024]{1,0:T(8,128)(2,1)} %v_hbm.1, bf16[256,256]{1,0:T(8,128)(2,1)} %x_ref.1, bf16[256,256]{1,0:T(8,128)(2,1)} %w_ref.1, ...), custom_call_target="tpu_custom_call" | custom-call | flops 1000000 | bytes 1000000 | tf_op jit(solution)/shard_map/pallas_call | solution.py:410
  3.8 0.0 copy-start
  3.8 0.0 copy-start.1
  3.8 0.0 copy-start.3
  3.8 0.0 copy-start.4
  3.8 13.2 %all-to-all-start = ((bf16[8,128,128]{2,1,0:T(8,128)(2,1)}), bf16[8,128,128]{2,1,0:T(8,128)(2,1)S(1)}, u32[]{:S(2)}, u32[]{:S(2)}) async-start(bf16[8,128,128]{2,1,0:T(8,128)(2,1)} %get-tuple-element.42), calls=%async_computation | async-start | bytes 524288 | tf_op jit(solution)/shard_map/all_to_all | solution.py:436
  17.0 0.0 copy-start.8
  17.1 4.6 %collective-permute-start.2 = (bf16[272,128]{1,0:T(8,128)(2,1)}, bf16[272,128]{1,0:T(8,128)(2,1)S(1)}, u32[]{:S(2)}, u32[]{:S(2)}) collective-permute-start(bf16[272,128]{1,0:T(8,128)(2,1)} %get-tuple-element.41), channel_id=1, source_target_pairs={{0,32},{32,64},{64,96},{96,128},{128,160},{160,192},{192,224},{224... | collective-permute-start | bytes 208904 | tf_op jit(solution)/shard_map/ppermute | solution.py:434
  21.7 3.1 %collective-permute-start.1 = (bf16[272,128]{1,0:T(8,128)(2,1)}, bf16[272,128]{1,0:T(8,128)(2,1)S(1)}, u32[]{:S(2)}, u32[]{:S(2)}) collective-permute-start(bf16[272,128]{1,0:T(8,128)(2,1)} %get-tuple-element.41), channel_id=1, source_target_pairs={{0,64},{32,96},{64,128},{96,160},{128,192},{160,224},{192,256},{22... | collective-permute-start | bytes 208904 | tf_op jit(solution)/shard_map/ppermute | solution.py:434
  24.8 3.1 %collective-permute-start = (bf16[272,128]{1,0:T(8,128)(2,1)}, bf16[272,128]{1,0:T(8,128)(2,1)S(1)}, u32[]{:S(2)}, u32[]{:S(2)}) collective-permute-start(bf16[272,128]{1,0:T(8,128)(2,1)} %get-tuple-element.41), channel_id=1, source_target_pairs={{0,96},{32,128},{64,160},{96,192},{128,224},{160,256},{192,288},{2... | collective-permute-start | bytes 208904 | tf_op jit(solution)/shard_map/ppermute | solution.py:434
  27.9 0.0 copy-start.5
  28.0 1.4 %shard_map.158 = (f32[256,256]{1,0:T(8,128)S(1)}, f32[256,256]{1,0:T(8,128)S(1)}) custom-call(bf16[256,256]{1,0:T(8,128)(2,1)S(1)} %copy-done, bf16[256,256]{1,0:T(8,128)(2,1)S(1)} %copy-done.1, bf16[256,256]{1,0:T(8,128)(2,1)S(1)} %copy-done.4, bf16[256,256]{1,0:T(8,128)(2,1)S(1)} %copy-done.3, s32[2,256]{1,0:T(2,128)S(1)} %bitcast.7, f32[2]{0:T(128)S(1)} %copy-done.7, ...), custom_call_target="tpu_custom_call" | custom-call | flops 1000000 | bytes 1000000 | tf_op jit(solution)/shard_map/pallas_call | solution.py:438
  29.3 0.0 collective-permute-done.2.got1_ref
  29.3 0.0 collective-permute-done.1.got2_ref
  29.4 0.3 collective-permute-done.got3_ref
  29.7 1.1 %shard_map.159 = (f32[264,128]{1,0:T(8,128)S(1)}, bf16[272,128]{1,0:T(8,128)(2,1)S(1)}, bf16[4,8,128,128]{3,2,1,0:T(8,128)(2,1)}, f32[8,256]{1,0:T(8,128)S(1)}) custom-call(bf16[272,128]{1,0:T(8,128)(2,1)S(1)} %collective-permute-done.2.got1_ref, bf16[272,128]{1,0:T(8,128)(2,1)S(1)} %collective-permute-done.1.got2_ref, ...), custom_call_target="tpu_custom_call" | custom-call | flops 1000000 | bytes 1000000 | tf_op jit(solution)/shard_map/pallas_call | solution.py:442
  30.8 4.1 %all-to-all-start.1 = ((bf16[4,8,128,128]{3,2,1,0:T(8,128)(2,1)}), bf16[4,8,128,128]{3,2,1,0:T(8,128)(2,1)S(1)}, u32[]{:S(2)}, u32[]{:S(2)}) async-start(bf16[4,8,128,128]{3,2,1,0:T(8,128)(2,1)} %get-tuple-element.50), calls=%async_computation.1 | async-start | bytes 2097152 | tf_op jit(solution)/shard_map/all_to_all | solution.py:453
  35.0 10.0 %collective-permute-start.6 = (bf16[272,128]{1,0:T(8,128)(2,1)S(1)}, bf16[272,128]{1,0:T(8,128)(2,1)S(1)}, u32[]{:S(2)}, u32[]{:S(2)}) collective-permute-start(bf16[272,128]{1,0:T(8,128)(2,1)S(1)} %get-tuple-element.51), channel_id=1, source_target_pairs={{0,384},{32,416},{64,448},{96,480},{1,385},{33,417},{65,449},{97,4... | collective-permute-start | bytes 208904 | tf_op jit(solution)/shard_map/ppermute | solution.py:434
  45.0 1.8 %collective-permute-start.5 = (bf16[272,128]{1,0:T(8,128)(2,1)S(1)}, bf16[272,128]{1,0:T(8,128)(2,1)S(1)}, u32[]{:S(2)}, u32[]{:S(2)}) collective-permute-start(bf16[272,128]{1,0:T(8,128)(2,1)S(1)} %get-tuple-element.51), channel_id=1, source_target_pairs={{0,256},{32,288},{64,320},{96,352},{128,384},{160,416},{192,448},{... | collective-permute-start | bytes 208904 | tf_op jit(solution)/shard_map/ppermute | solution.py:434
  46.8 1.7 %collective-permute-start.4 = (bf16[272,128]{1,0:T(8,128)(2,1)S(1)}, bf16[272,128]{1,0:T(8,128)(2,1)S(1)}, u32[]{:S(2)}, u32[]{:S(2)}) collective-permute-start(bf16[272,128]{1,0:T(8,128)(2,1)S(1)} %get-tuple-element.51), channel_id=1, source_target_pairs={{0,128},{32,160},{64,192},{96,224},{128,256},{160,288},{192,320},{... | collective-permute-start | bytes 208904 | tf_op jit(solution)/shard_map/ppermute | solution.py:434
  48.5 0.0 all-to-all-done.1.kv_ref
  48.5 5.5 %collective-permute-start.3 = (bf16[4,8,128,128]{3,2,1,0:T(8,128)(2,1)S(1)}, bf16[4,8,128,128]{3,2,1,0:T(8,128)(2,1)S(1)}, u32[]{:S(2)}, u32[]{:S(2)}) collective-permute-start(bf16[4,8,128,128]{3,2,1,0:T(8,128)(2,1)S(1)} %all-to-all-done.1.kv_ref), channel_id=1, source_target_pairs={{0,32},{32,0},{1,33},{33,1},{2,34},{34,2},{3,35},{35,3},{4,36},{36... | collective-permute-start | bytes 3145736 | tf_op jit(solution)/shard_map/ppermute | solution.py:455
  54.0 0.9 shard_map.160
  54.9 0.0 collective-permute-done.5.mid_ref
  54.9 0.0 collective-permute-done.4.near_ref
  54.9 0.4 shard_map.161
  55.3 1.0 %collective-permute-done.3.kv_ref = bf16[4,8,128,128]{3,2,1,0:T(8,128)(2,1)S(1)} collective-permute-done((bf16[4,8,128,128]{3,2,1,0:T(8,128)(2,1)S(1)}, bf16[4,8,128,128]{3,2,1,0:T(8,128)(2,1)S(1)}, u32[]{:S(2)}, u32[]{:S(2)}) %collective-permute-start.3) | collective-permute-done | bytes 1048608 | tf_op jit(solution)/shard_map/ppermute | solution.py:455
  56.2 1.7 %shard_map.162 = (bf16[256,256]{1,0:T(8,128)(2,1)}, f32[16,8,128]{2,1,0:T(8,128)S(1)}) custom-call(bf16[512,256]{1,0:T(8,128)(2,1)S(1)} %get-tuple-element.68.scaled_ref, bf16[4,8,128,128]{3,2,1,0:T(8,128)(2,1)S(1)} %collective-permute-done.3.kv_ref, f32[512,128]{1,0:T(8,128)S(1)} %get-tuple-element.70.m_in, f32[512,128]{1,0:T(8,128)S(1)} %get-tuple-element.71.l_in, ...), custom_call_target="tpu_custom_call" | custom-call | flops 1000000000 | bytes 1000000 | tf_op jit(solution)/shard_map/pallas_call | solution.py:466
  57.9 13.6 %all_to_all.20.got_ref = f32[16,8,128]{2,1,0:T(8,128)S(1)} all-to-all(f32[16,8,128]{2,1,0:T(8,128)S(1)} %get-tuple-element.75), channel_id=1, replica_groups=mesh['zl'=8,'core'=2,'zh'=2,'y'=4,'x'=4] {'y','x'}, dimensions={0} | all-to-all | bytes 131072 | tf_op jit(solution)/shard_map/all_to_all | solution.py:473
  71.5 0.1 shard_map.163
  71.6 23.6 %all_to_all.21.got_ref = bf16[32,8,128]{2,1,0:T(8,128)(2,1)S(1)} all-to-all(bf16[32,8,128]{2,1,0:T(8,128)(2,1)S(1)} %shard_map.163), channel_id=1, replica_groups=mesh['zl'=8,'core'=2,'zh'=2,'y'=4,'x'=4] {'zl','core','zh'}, dimensions={0} | all-to-all | bytes 131072 | tf_op jit(solution)/shard_map/all_to_all | solution.py:476
  95.2 0.9 shard_map.164
  (16 shorter events, 0.0 us)
Async XLA Ops:
  0.6 27.2 %copy-start.6 = (s32[256,2]{0,1:T(2,128)S(1)}, s32[256,2]{0,1:T(2,128)}, u32[]{:S(2)}) copy-start(s32[256,2]{0,1:T(2,128)} %param.21) | copy-start | bytes 6148
  3.8 24.1 %copy-start = (bf16[256,256]{1,0:T(8,128)(2,1)S(1)}, bf16[256,256]{1,0:T(8,128)(2,1)}, u32[]{:S(2)}) copy-start(bf16[256,256]{1,0:T(8,128)(2,1)} %x_ref.1) | copy-start | bytes 393220
  3.8 24.1 %copy-start.1 = (bf16[256,256]{1,0:T(8,128)(2,1)S(1)}, bf16[256,256]{1,0:T(8,128)(2,1)}, u32[]{:S(2)}) copy-start(bf16[256,256]{1,0:T(8,128)(2,1)} %w_ref.1) | copy-start | bytes 393220
  3.8 24.1 %copy-start.3 = (bf16[256,256]{1,0:T(8,128)(2,1)S(1)}, bf16[256,256]{1,0:T(8,128)(2,1)}, u32[]{:S(2)}) copy-start(bf16[256,256]{1,0:T(8,128)(2,1)} %g_ref.1) | copy-start | bytes 393220
  3.8 24.1 %copy-start.4 = (bf16[256,256]{1,0:T(8,128)(2,1)S(1)}, bf16[256,256]{1,0:T(8,128)(2,1)}, u32[]{:S(2)}) copy-start(bf16[256,256]{1,0:T(8,128)(2,1)} %r_ref.3) | copy-start | bytes 393220
  3.8 25.9 %all-to-all-start = ((bf16[8,128,128]{2,1,0:T(8,128)(2,1)}), bf16[8,128,128]{2,1,0:T(8,128)(2,1)S(1)}, u32[]{:S(2)}, u32[]{:S(2)}) async-start(bf16[8,128,128]{2,1,0:T(8,128)(2,1)} %get-tuple-element.42), calls=%async_computation | async-start | bytes 524288 | tf_op jit(solution)/shard_map/all_to_all | solution.py:436
  17.0 10.9 %copy-start.7 = (f32[2]{0:T(128)S(1)}, f32[2]{0:T(128)}, u32[]{:S(2)}) copy-start(f32[2]{0:T(128)} %rates_ref.3) | copy-start | bytes 28
  17.0 10.9 %copy-start.8 = (f32[2]{0:T(128)S(1)}, f32[2]{0:T(128)}, u32[]{:S(2)}) copy-start(f32[2]{0:T(128)} %skip_ref.1) | copy-start | bytes 28
  17.1 12.6 %copy-start.2 = (f32[264,128]{1,0:T(8,128)S(1)}, f32[264,128]{1,0:T(8,128)}, u32[]{:S(2)}) copy-start(f32[264,128]{1,0:T(8,128)} %get-tuple-element.47.own_ref) | copy-start | bytes 405508
  17.1 12.3 %collective-permute-start.2 = (bf16[272,128]{1,0:T(8,128)(2,1)}, bf16[272,128]{1,0:T(8,128)(2,1)S(1)}, u32[]{:S(2)}, u32[]{:S(2)}) collective-permute-start(bf16[272,128]{1,0:T(8,128)(2,1)} %get-tuple-element.41), channel_id=1, source_target_pairs={{0,32},{32,64},{64,96},{96,128},{128,160},{160,192},{192,224},{224... | collective-permute-start | bytes 208904 | tf_op jit(solution)/shard_map/ppermute | solution.py:434
  21.7 7.7 %collective-permute-start.1 = (bf16[272,128]{1,0:T(8,128)(2,1)}, bf16[272,128]{1,0:T(8,128)(2,1)S(1)}, u32[]{:S(2)}, u32[]{:S(2)}) collective-permute-start(bf16[272,128]{1,0:T(8,128)(2,1)} %get-tuple-element.41), channel_id=1, source_target_pairs={{0,64},{32,96},{64,128},{96,160},{128,192},{160,224},{192,256},{22... | collective-permute-start | bytes 208904 | tf_op jit(solution)/shard_map/ppermute | solution.py:434
  24.8 4.9 %collective-permute-start = (bf16[272,128]{1,0:T(8,128)(2,1)}, bf16[272,128]{1,0:T(8,128)(2,1)S(1)}, u32[]{:S(2)}, u32[]{:S(2)}) collective-permute-start(bf16[272,128]{1,0:T(8,128)(2,1)} %get-tuple-element.41), channel_id=1, source_target_pairs={{0,96},{32,128},{64,160},{96,192},{128,224},{160,256},{192,288},{2... | collective-permute-start | bytes 208904 | tf_op jit(solution)/shard_map/ppermute | solution.py:434
  27.9 1.7 %copy-start.5 = (f32[8,256]{1,0:T(8,128)S(1)}, f32[8,256]{1,0:T(8,128)}, u32[]{:S(2)}) copy-start(f32[8,256]{1,0:T(8,128)} %get-tuple-element.49.rows_ref) | copy-start | bytes 24580
  30.8 23.2 %copy-start.9 = (bf16[256,256]{1,0:T(8,128)(2,1)S(1)}, bf16[256,256]{1,0:T(8,128)(2,1)}, u32[]{:S(2)}) copy-start(bf16[256,256]{1,0:T(8,128)(2,1)} %q_ref.1) | copy-start | bytes 393220
  30.8 17.7 %all-to-all-start.1 = ((bf16[4,8,128,128]{3,2,1,0:T(8,128)(2,1)}), bf16[4,8,128,128]{3,2,1,0:T(8,128)(2,1)S(1)}, u32[]{:S(2)}, u32[]{:S(2)}) async-start(bf16[4,8,128,128]{3,2,1,0:T(8,128)(2,1)} %get-tuple-element.50), calls=%async_computation.1 | async-start | bytes 2097152 | tf_op jit(solution)/shard_map/all_to_all | solution.py:453
  35.0 19.9 %collective-permute-start.6 = (bf16[272,128]{1,0:T(8,128)(2,1)S(1)}, bf16[272,128]{1,0:T(8,128)(2,1)S(1)}, u32[]{:S(2)}, u32[]{:S(2)}) collective-permute-start(bf16[272,128]{1,0:T(8,128)(2,1)S(1)} %get-tuple-element.51), channel_id=1, source_target_pairs={{0,384},{32,416},{64,448},{96,480},{1,385},{33,417},{65,449},{97,4... | collective-permute-start | bytes 208904 | tf_op jit(solution)/shard_map/ppermute | solution.py:434
  45.0 9.9 %collective-permute-start.5 = (bf16[272,128]{1,0:T(8,128)(2,1)S(1)}, bf16[272,128]{1,0:T(8,128)(2,1)S(1)}, u32[]{:S(2)}, u32[]{:S(2)}) collective-permute-start(bf16[272,128]{1,0:T(8,128)(2,1)S(1)} %get-tuple-element.51), channel_id=1, source_target_pairs={{0,256},{32,288},{64,320},{96,352},{128,384},{160,416},{192,448},{... | collective-permute-start | bytes 208904 | tf_op jit(solution)/shard_map/ppermute | solution.py:434
  46.8 8.1 %collective-permute-start.4 = (bf16[272,128]{1,0:T(8,128)(2,1)S(1)}, bf16[272,128]{1,0:T(8,128)(2,1)S(1)}, u32[]{:S(2)}, u32[]{:S(2)}) collective-permute-start(bf16[272,128]{1,0:T(8,128)(2,1)S(1)} %get-tuple-element.51), channel_id=1, source_target_pairs={{0,128},{32,160},{64,192},{96,224},{128,256},{160,288},{192,320},{... | collective-permute-start | bytes 208904 | tf_op jit(solution)/shard_map/ppermute | solution.py:434
  48.5 7.8 %collective-permute-start.3 = (bf16[4,8,128,128]{3,2,1,0:T(8,128)(2,1)S(1)}, bf16[4,8,128,128]{3,2,1,0:T(8,128)(2,1)S(1)}, u32[]{:S(2)}, u32[]{:S(2)}) collective-permute-start(bf16[4,8,128,128]{3,2,1,0:T(8,128)(2,1)S(1)} %all-to-all-done.1.kv_ref), channel_id=1, source_target_pairs={{0,32},{32,0},{1,33},{33,1},{2,34},{34,2},{3,35},{35,3},{4,36},{36... | collective-permute-start | bytes 3145736 | tf_op jit(solution)/shard_map/ppermute | solution.py:455

commit v5 on v4

--- a/solution.py
+++ b/solution.py
@@ -26,7 +26,8 @@
 HBM = pl.BlockSpec(memory_space=pltpu.HBM)
 NEG = -1e30
 CARRIED_FLOPS = 10_800_000_000
-ENTRY_MIB = 58
+MERGE_FLOPS = 20_000_000_000
+PACK_MIB = 58
 FADE = 2 * DIM
 STATE_ROWS = FADE + 16
 
@@ -79,27 +80,27 @@
     return lanes, jnp.transpose(lanes)
 
 
-def entry_kernel(
-    rates_ref, k_hbm, v_hbm, x_hbm, w_hbm, codes_hbm, gain_hbm, state_out_hbm, attend_out_hbm, seg_hbm,
-    own_ref, send_ref, packed_ref, rows_ref,
-    piece, x_ref, w_ref, codes_ref, gain_ref, state_out_ref, attend_out_ref, seg_ref, sems,
-):
+def pack_kernel(k_hbm, v_hbm, packed_ref, piece, sems):
     group = lax.axis_index("zh") * 4 + lax.axis_index("y")
     quarter = pl.ds(pl.multiple_of(lax.axis_index("x") * 64, 64), 64)
     columns = pl.ds(pl.multiple_of(group * DIM, DIM), DIM)
-    pairs = [(codes_hbm, codes_ref), (x_hbm, x_ref), (w_hbm, w_ref)]
-    pairs += [(ref.at[quarter, columns], piece.at[pl.ds(64 * n, 64)]) for n, ref in enumerate((k_hbm, v_hbm))]
-    pairs += [
-        (gain_hbm, gain_ref),
-        (state_out_hbm, state_out_ref),
-        (attend_out_hbm, attend_out_ref),
-        (seg_hbm, seg_ref),
+    copies = [
+        pltpu.make_async_copy(ref.at[quarter, columns], piece.at[pl.ds(64 * n, 64)], sems.at[n])
+        for n, ref in enumerate((k_hbm, v_hbm))
     ]
-    copies = [pltpu.make_async_copy(*pair, sems.at[n]) for n, pair in enumerate(pairs)]
     for c in copies:
         c.start()
-    for c in copies[:3]:
+    for c in copies:
         c.wait()
+    both = piece[...]
+    for n in range(packed_ref.shape[0]):
+        packed_ref[n] = both
+
+
+def states_kernel(
+    rates_ref, x_ref, w_ref, codes_ref, gain_ref, state_out_ref, attend_out_ref, seg_ref,
+    own_ref, send_ref, rows_ref,
+):
     sums = code_sums(codes_ref)
     row = lax.broadcasted_iota(jnp.int32, (8, DIM), 0)
     fades, marks = jnp.zeros((8, DIM), F32), jnp.zeros((8, DIM), F32)
@@ -126,11 +127,6 @@
         fades = jnp.where(row == 2 * h, high, jnp.where(row == 2 * h + 1, fade - high, fades))
     own_ref[pl.ds(FADE, 8)] = marks
     send_ref[pl.ds(FADE, 16)] = jnp.concatenate([fades, jnp.zeros((8, DIM), F32)], axis=0).astype(BF16)
-    for c in copies[3:]:
-        c.wait()
-    both = piece[...]
-    for n in range(packed_ref.shape[0]):
-        packed_ref[n] = both
     gain = gain_ref[...]
     rows_ref[...] = jnp.concatenate(
         [gain, gain * state_out_ref[...], attend_out_ref[...], seg_ref[...].astype(F32), jnp.zeros((4, 256), F32)],
@@ -138,12 +134,12 @@
     )
 
 
-def fan_kernel(
-    got1_ref, got2_ref, got3_ref, own_ref, quarter_ref, rows_ref, x_out, send_ref, fan_ref, rows_out
-):
-    rows_out[...] = rows_ref[...]
+def fan_kernel(quarter_ref, fan_ref):
     for n in range(fan_ref.shape[0]):
         fan_ref[n] = quarter_ref[...]
+
+
+def merge_kernel(got1_ref, got2_ref, got3_ref, own_ref, x_out, send_ref):
     refs = (got1_ref, got2_ref, got3_ref)
     sent = [ref[pl.ds(FADE, 16)].astype(F32) for ref in refs]
     row = lax.broadcasted_iota(jnp.int32, (8, DIM), 0)
@@ -407,48 +403,34 @@
     ctx = chips * lax.axis_size("core")
 
     together = lax.optimization_barrier
-    own, send, packed, rows = call(
-        entry_kernel,
-        (
-            shape((FADE + 8, DIM)),
-            shape((STATE_ROWS, DIM), BF16),
-            shape((chips, DIM, DIM), BF16),
-            shape((8, 256)),
-        ),
-        [SMEM] + [HBM] * 9,
-        [
-            pltpu.VMEM((DIM, DIM), BF16),
-            pltpu.VMEM((tokens, 256), BF16),
-            pltpu.VMEM((tokens, 256), BF16),
-            pltpu.VMEM((2, tokens), jnp.int32),
-            pltpu.VMEM((1, 256), F32),
-            pltpu.VMEM((1, 256), F32),
-            pltpu.VMEM((1, 256), F32),
-            pltpu.VMEM((1, 256), jnp.int32),
-            pltpu.SemaphoreType.DMA((9,)),
-        ],
-        mib=ENTRY_MIB,
-    )(decay_rates, key_rows, value_rows, state_input, state_write, codes, gain, state_out, attend_out, seg)
+    packed = call(
+        pack_kernel,
+        shape((chips, DIM, DIM), BF16),
+        [HBM] * 2,
+        [pltpu.VMEM((DIM, DIM), BF16), pltpu.SemaphoreType.DMA((2,))],
+        mib=PACK_MIB,
+    )(key_rows, value_rows)
+    packed, codes = together((packed, codes))
+    quarter = lax.all_to_all(packed, "zl", 0, 0)
+    own, send, rows = call(
+        states_kernel,
+        (shape((FADE + 8, DIM)), shape((STATE_ROWS, DIM), BF16), shape((8, 256))),
+        [SMEM] + [VMEM] * 7,
+    )(decay_rates, state_input, state_write, codes, gain, state_out, attend_out, seg)
 
     def shifted(v, by):
         return lax.ppermute(v, CTX, [(i, i + by) for i in range(ctx - by)])
 
-    quarter = lax.all_to_all(packed, "zl", 0, 0)
     got = tuple(shifted(send, by) for by in (3, 2, 1))
     base, carry = call(
         local_kernel, (shape((tokens, 256)), shape((tokens, 256))), [VMEM] * 5 + [SMEM] * 2
     )(state_input, state_write, state_read, gate_input, codes, decay_rates, skip_gain)
-    got, quarter, base = together((got, quarter, base))
-    before, send, fan, rows = call(
-        fan_kernel,
-        (
-            shape((FADE + 8, DIM)),
-            shape((STATE_ROWS, DIM), BF16),
-            shape((wide, chips, DIM, DIM), BF16),
-            shape((8, 256)),
-        ),
-        [VMEM] * 6,
-    )(*got[::-1], own, quarter, rows)
+    quarter, base = together((quarter, base))
+    fan = call(fan_kernel, shape((wide, chips, DIM, DIM), BF16), [VMEM])(quarter)
+    got, _ = together((got, fan))
+    before, send = call(
+        merge_kernel, (shape((FADE + 8, DIM)), shape((STATE_ROWS, DIM), BF16)), [VMEM] * 4, flops=MERGE_FLOPS
+    )(*got[::-1], own)
 
     mine = lax.all_to_all(fan, "x", 0, 0)
     arrived = tuple(shifted(send, by) for by in (4, 8, 12))

time: 96.7 us -> 95.7 us (0.990)
  starting transfers between devices: 47.1 us -> 45.4 us
    ppermute x6, starting transfers between devices: 24.3 us -> 21 us  [shifted(): return lax.ppermute(v, CTX, [(i, i + by) for i in range(ctx - by)])]
    all_to_all x1, blocking collectives: 23.6 us -> 26.3 us  [per_device(): summed = lax.all_to_all(send, ('zl', 'core', 'zh'), 0, 0)]
    all_to_all x1, blocking collectives: 13.6 us -> 11.5 us  [per_device(): summed = lax.all_to_all(send, ('y', 'x'), 0, 0)]
    ppermute x1, starting transfers between devices: 5.49 us -> 7.16 us  [per_device(): theirs = lax.ppermute(mine, 'core', [(0, 1), (1, 0)])]
    pallas_call x2 -> x4, Pallas kernels: 4.26 us -> 3.69 us  [the longest x1 1.5 us: per_device(): call(pack_kernel, shape((chips, DIM, DIM), BF16), [HBM] * 2, [pltpu.VMEM(...]
  transfers between devices with their start and end apart: 9 -> 9, of which waited for: 2 -> 2; matrix products, arithmetic and copies ran while one was open for 0% -> 0% of each run, Pallas kernels for 3% -> 5%
where the time goes in v5:
time: 95.7 us; the launch traced here: 95.1 us
  starting transfers between devices  45.4 us (47%)
  blocking collectives  37.7 us (39%)
  Pallas kernels  9.02 us (9%)
  waiting for transfers between devices  1.3 us (1%)
    all_to_all x1, blocking collectives, per_device(): summed = lax.all_to_all(send, ('zl', 'core', 'zh'), 0, 0)  26.3 us
    ppermute x6, starting transfers between devices, shifted(): return lax.ppermute(v, CTX, [(i, i + by) for i in range(ctx - by)])  21 us
    all_to_all x1, starting transfers between devices, per_device(): quarter = lax.all_to_all(packed, 'zl', 0, 0)  13.2 us
    all_to_all x1, blocking collectives, per_device(): summed = lax.all_to_all(send, ('y', 'x'), 0, 0)  11.5 us
    ppermute x1, starting transfers between devices, per_device(): theirs = lax.ppermute(mine, 'core', [(0, 1), (1, 0)])  7.16 us
    all_to_all x1, starting transfers between devices, per_device(): mine = lax.all_to_all(fan, 'x', 0, 0)  4.01 us
  transfers between devices with their start and end apart: 9, of which 2 were waited for; matrix products, arithmetic and copies ran while one was open for 0% of the time, Pallas kernels for 5%

profile of v5, /device:TPU:1, one launch (start us, length us, event | category | flops | bytes accessed | tf_op | source)
XLA Modules:
  0.0 95.1 jit_solution(15828087355026659256)
XLA Ops:
  0.6 1.5 %shard_map.157 = bf16[8,128,128]{2,1,0:T(8,128)(2,1)} custom-call(bf16[256,1024]{1,0:T(8,128)(2,1)} %k_hbm.1, bf16[256,1024]{1,0:T(8,128)(2,1)} %v_hbm.1), custom_call_target="tpu_custom_call" | custom-call | flops 1000000 | bytes 1000000 | tf_op jit(solution)/shard_map/pallas_call | solution.py:406
  2.1 0.0 copy-start
  2.1 0.0 copy-start.1
  2.2 0.0 copy-start.7
  2.2 0.0 copy-start.8
  2.2 0.0 copy-start.9
  2.2 13.2 %all-to-all-start = ((bf16[8,128,128]{2,1,0:T(8,128)(2,1)}), bf16[8,128,128]{2,1,0:T(8,128)(2,1)S(1)}, u32[]{:S(2)}, u32[]{:S(2)}) async-start(bf16[8,128,128]{2,1,0:T(8,128)(2,1)} %shard_map.157), calls=%async_computation | async-start | bytes 524288 | tf_op jit(solution)/shard_map/all_to_all | solution.py:414
  15.4 0.0 copy-start.5
  15.5 0.6 copy-done.4
  16.1 0.0 copy-done.6
  16.1 1.0 %shard_map.160 = (f32[264,128]{1,0:T(8,128)S(1)}, bf16[272,128]{1,0:T(8,128)(2,1)S(1)}, f32[8,256]{1,0:T(8,128)S(1)}) custom-call(f32[2]{0:T(128)S(1)} %copy-done.5, bf16[256,256]{1,0:T(8,128)(2,1)S(1)} %copy-done, bf16[256,256]{1,0:T(8,128)(2,1)S(1)} %copy-done.1, s32[2,256]{1,0:T(2,128)S(1)} %bitcast.6, f32[1,256]{1,0:T(1,128)S(1)} %bitcast.8, ...), custom_call_target="tpu_custom_call" | custom-call | flops 1000000 | bytes 1000000 | tf_op jit(solution)/shard_map/pallas_call | solution.py:415
  17.2 0.0 copy-start.10
  17.2 4.5 %collective-permute-start.3 = (bf16[272,128]{1,0:T(8,128)(2,1)S(1)}, bf16[272,128]{1,0:T(8,128)(2,1)S(1)}, u32[]{:S(2)}, u32[]{:S(2)}) collective-permute-start(bf16[272,128]{1,0:T(8,128)(2,1)S(1)} %get-tuple-element.44), channel_id=1, source_target_pairs={{0,32},{32,64},{64,96},{96,128},{128,160},{160,192},{192,224},{224... | collective-permute-start | bytes 208904 | tf_op jit(solution)/shard_map/ppermute | solution.py:422
  21.7 3.1 %collective-permute-start.2 = (bf16[272,128]{1,0:T(8,128)(2,1)S(1)}, bf16[272,128]{1,0:T(8,128)(2,1)S(1)}, u32[]{:S(2)}, u32[]{:S(2)}) collective-permute-start(bf16[272,128]{1,0:T(8,128)(2,1)S(1)} %get-tuple-element.44), channel_id=1, source_target_pairs={{0,64},{32,96},{64,128},{96,160},{128,192},{160,224},{192,256},{22... | collective-permute-start | bytes 208904 | tf_op jit(solution)/shard_map/ppermute | solution.py:422
  24.8 3.1 %collective-permute-start.1 = (bf16[272,128]{1,0:T(8,128)(2,1)S(1)}, bf16[272,128]{1,0:T(8,128)(2,1)S(1)}, u32[]{:S(2)}, u32[]{:S(2)}) collective-permute-start(bf16[272,128]{1,0:T(8,128)(2,1)S(1)} %get-tuple-element.44), channel_id=1, source_target_pairs={{0,96},{32,128},{64,160},{96,192},{128,224},{160,256},{192,288},{2... | collective-permute-start | bytes 208904 | tf_op jit(solution)/shard_map/ppermute | solution.py:422
  27.9 1.4 %shard_map.158 = (f32[256,256]{1,0:T(8,128)S(1)}, f32[256,256]{1,0:T(8,128)S(1)}) custom-call(bf16[256,256]{1,0:T(8,128)(2,1)S(1)} %copy-done, bf16[256,256]{1,0:T(8,128)(2,1)S(1)} %copy-done.1, bf16[256,256]{1,0:T(8,128)(2,1)S(1)} %copy-done.3, bf16[256,256]{1,0:T(8,128)(2,1)S(1)} %copy-done.2, s32[2,256]{1,0:T(2,128)S(1)} %bitcast.7, f32[2]{0:T(128)S(1)} %copy-done.5, ...), custom_call_target="tpu_custom_call" | custom-call | flops 1000000 | bytes 1000000 | tf_op jit(solution)/shard_map/pallas_call | solution.py:425
  29.3 1.1 %shard_map.159 = bf16[4,8,128,128]{3,2,1,0:T(8,128)(2,1)} custom-call(bf16[8,128,128]{2,1,0:T(8,128)(2,1)S(1)} %all-to-all-done.quarter_ref), custom_call_target="tpu_custom_call" | custom-call | flops 1000000 | bytes 1000000 | tf_op jit(solution)/shard_map/pallas_call | solution.py:429
  30.4 4.0 %all-to-all-start.1 = ((bf16[4,8,128,128]{3,2,1,0:T(8,128)(2,1)}), bf16[4,8,128,128]{3,2,1,0:T(8,128)(2,1)S(1)}, u32[]{:S(2)}, u32[]{:S(2)}) async-start(bf16[4,8,128,128]{3,2,1,0:T(8,128)(2,1)} %shard_map.159), calls=%async_computation.1 | async-start | bytes 2097152 | tf_op jit(solution)/shard_map/all_to_all | solution.py:435
  34.4 0.1 shard_map.161
  34.5 6.9 %collective-permute-start.6 = (bf16[272,128]{1,0:T(8,128)(2,1)S(1)}, bf16[272,128]{1,0:T(8,128)(2,1)S(1)}, u32[]{:S(2)}, u32[]{:S(2)}) collective-permute-start(bf16[272,128]{1,0:T(8,128)(2,1)S(1)} %get-tuple-element.49), channel_id=1, source_target_pairs={{0,384},{32,416},{64,448},{96,480},{1,385},{33,417},{65,449},{97,4... | collective-permute-start | bytes 208904 | tf_op jit(solution)/shard_map/ppermute | solution.py:422
  41.4 1.3 %collective-permute-start.5 = (bf16[272,128]{1,0:T(8,128)(2,1)S(1)}, bf16[272,128]{1,0:T(8,128)(2,1)S(1)}, u32[]{:S(2)}, u32[]{:S(2)}) collective-permute-start(bf16[272,128]{1,0:T(8,128)(2,1)S(1)} %get-tuple-element.49), channel_id=1, source_target_pairs={{0,256},{32,288},{64,320},{96,352},{128,384},{160,416},{192,448},{... | collective-permute-start | bytes 208904 | tf_op jit(solution)/shard_map/ppermute | solution.py:422
  42.7 2.2 %collective-permute-start.4 = (bf16[272,128]{1,0:T(8,128)(2,1)S(1)}, bf16[272,128]{1,0:T(8,128)(2,1)S(1)}, u32[]{:S(2)}, u32[]{:S(2)}) collective-permute-start(bf16[272,128]{1,0:T(8,128)(2,1)S(1)} %get-tuple-element.49), channel_id=1, source_target_pairs={{0,128},{32,160},{64,192},{96,224},{128,256},{160,288},{192,320},{... | collective-permute-start | bytes 208904 | tf_op jit(solution)/shard_map/ppermute | solution.py:422
  44.9 0.3 all-to-all-done.1.kv_ref
  45.2 7.2 %collective-permute-start = (bf16[4,8,128,128]{3,2,1,0:T(8,128)(2,1)S(1)}, bf16[4,8,128,128]{3,2,1,0:T(8,128)(2,1)S(1)}, u32[]{:S(2)}, u32[]{:S(2)}) collective-permute-start(bf16[4,8,128,128]{3,2,1,0:T(8,128)(2,1)S(1)} %all-to-all-done.1.kv_ref), channel_id=1, source_target_pairs={{0,32},{32,0},{1,33},{33,1},{2,34},{34,2},{3,35},{35,3},{4,36},{36... | collective-permute-start | bytes 3145736 | tf_op jit(solution)/shard_map/ppermute | solution.py:437
  52.4 0.8 shard_map.162
  53.3 0.4 shard_map.163
  53.7 1.0 %collective-permute-done.kv_ref = bf16[4,8,128,128]{3,2,1,0:T(8,128)(2,1)S(1)} collective-permute-done((bf16[4,8,128,128]{3,2,1,0:T(8,128)(2,1)S(1)}, bf16[4,8,128,128]{3,2,1,0:T(8,128)(2,1)S(1)}, u32[]{:S(2)}, u32[]{:S(2)}) %collective-permute-start) | collective-permute-done | bytes 1048608 | tf_op jit(solution)/shard_map/ppermute | solution.py:437
  54.6 1.7 %shard_map.164 = (bf16[256,256]{1,0:T(8,128)(2,1)}, f32[16,8,128]{2,1,0:T(8,128)S(1)}) custom-call(bf16[512,256]{1,0:T(8,128)(2,1)S(1)} %get-tuple-element.66.scaled_ref, bf16[4,8,128,128]{3,2,1,0:T(8,128)(2,1)S(1)} %collective-permute-done.kv_ref, f32[512,128]{1,0:T(8,128)S(1)} %get-tuple-element.68.m_in, f32[512,128]{1,0:T(8,128)S(1)} %get-tuple-element.69.l_in, ...), custom_call_target="tpu_custom_call" | custom-call | flops 1000000000 | bytes 1000000 | tf_op jit(solution)/shard_map/pallas_call | solution.py:448
  56.3 11.5 %all_to_all.20.got_ref = f32[16,8,128]{2,1,0:T(8,128)S(1)} all-to-all(f32[16,8,128]{2,1,0:T(8,128)S(1)} %get-tuple-element.73), channel_id=1, replica_groups=mesh['zl'=8,'core'=2,'zh'=2,'y'=4,'x'=4] {'y','x'}, dimensions={0} | all-to-all | bytes 131072 | tf_op jit(solution)/shard_map/all_to_all | solution.py:455
  67.8 0.1 shard_map.165
  67.9 26.3 %all_to_all.21.got_ref = bf16[32,8,128]{2,1,0:T(8,128)(2,1)S(1)} all-to-all(bf16[32,8,128]{2,1,0:T(8,128)(2,1)S(1)} %shard_map.165), channel_id=1, replica_groups=mesh['zl'=8,'core'=2,'zh'=2,'y'=4,'x'=4] {'zl','core','zh'}, dimensions={0} | all-to-all | bytes 131072 | tf_op jit(solution)/shard_map/all_to_all | solution.py:458
  94.2 0.9 shard_map.166
  (22 shorter events, 0.1 us)
Async XLA Ops:
  2.1 13.3 %copy-start = (bf16[256,256]{1,0:T(8,128)(2,1)S(1)}, bf16[256,256]{1,0:T(8,128)(2,1)}, u32[]{:S(2)}) copy-start(bf16[256,256]{1,0:T(8,128)(2,1)} %x_ref.3) | copy-start | bytes 393220
  2.1 13.3 %copy-start.1 = (bf16[256,256]{1,0:T(8,128)(2,1)S(1)}, bf16[256,256]{1,0:T(8,128)(2,1)}, u32[]{:S(2)}) copy-start(bf16[256,256]{1,0:T(8,128)(2,1)} %w_ref.3) | copy-start | bytes 393220
  2.2 13.3 %copy-start.7 = (f32[256]{0:T(256)S(1)}, f32[256]{0:T(256)}, u32[]{:S(2)}) copy-start(f32[256]{0:T(256)} %param.26) | copy-start | bytes 3076
  2.2 13.3 %copy-start.8 = (f32[256]{0:T(256)S(1)}, f32[256]{0:T(256)}, u32[]{:S(2)}) copy-start(f32[256]{0:T(256)} %param.25) | copy-start | bytes 3076
  2.2 13.3 %copy-start.9 = (s32[256]{0:T(256)S(1)}, s32[256]{0:T(256)}, u32[]{:S(2)}) copy-start(s32[256]{0:T(256)} %param.27) | copy-start | bytes 3076
  2.2 27.1 %all-to-all-start = ((bf16[8,128,128]{2,1,0:T(8,128)(2,1)}), bf16[8,128,128]{2,1,0:T(8,128)(2,1)S(1)}, u32[]{:S(2)}, u32[]{:S(2)}) async-start(bf16[8,128,128]{2,1,0:T(8,128)(2,1)} %shard_map.157), calls=%async_computation | async-start | bytes 524288 | tf_op jit(solution)/shard_map/all_to_all | solution.py:414
  15.4 0.7 copy-start.4
  15.4 0.7 copy-start.5
  15.4 0.7 copy-start.6
  16.1 11.8 %copy-start.2 = (bf16[256,256]{1,0:T(8,128)(2,1)S(1)}, bf16[256,256]{1,0:T(8,128)(2,1)}, u32[]{:S(2)}) copy-start(bf16[256,256]{1,0:T(8,128)(2,1)} %g_ref.1) | copy-start | bytes 393220
  16.1 11.8 %copy-start.3 = (bf16[256,256]{1,0:T(8,128)(2,1)S(1)}, bf16[256,256]{1,0:T(8,128)(2,1)}, u32[]{:S(2)}) copy-start(bf16[256,256]{1,0:T(8,128)(2,1)} %r_ref.3) | copy-start | bytes 393220
  17.2 10.7 %copy-start.10 = (f32[2]{0:T(128)S(1)}, f32[2]{0:T(128)}, u32[]{:S(2)}) copy-start(f32[2]{0:T(128)} %skip_ref.1) | copy-start | bytes 28
  17.2 17.2 %collective-permute-start.3 = (bf16[272,128]{1,0:T(8,128)(2,1)S(1)}, bf16[272,128]{1,0:T(8,128)(2,1)S(1)}, u32[]{:S(2)}, u32[]{:S(2)}) collective-permute-start(bf16[272,128]{1,0:T(8,128)(2,1)S(1)} %get-tuple-element.44), channel_id=1, source_target_pairs={{0,32},{32,64},{64,96},{96,128},{128,160},{160,192},{192,224},{224... | collective-permute-start | bytes 208904 | tf_op jit(solution)/shard_map/ppermute | solution.py:422
  21.7 12.7 %collective-permute-start.2 = (bf16[272,128]{1,0:T(8,128)(2,1)S(1)}, bf16[272,128]{1,0:T(8,128)(2,1)S(1)}, u32[]{:S(2)}, u32[]{:S(2)}) collective-permute-start(bf16[272,128]{1,0:T(8,128)(2,1)S(1)} %get-tuple-element.44), channel_id=1, source_target_pairs={{0,64},{32,96},{64,128},{96,160},{128,192},{160,224},{192,256},{22... | collective-permute-start | bytes 208904 | tf_op jit(solution)/shard_map/ppermute | solution.py:422
  24.8 9.7 %collective-permute-start.1 = (bf16[272,128]{1,0:T(8,128)(2,1)S(1)}, bf16[272,128]{1,0:T(8,128)(2,1)S(1)}, u32[]{:S(2)}, u32[]{:S(2)}) collective-permute-start(bf16[272,128]{1,0:T(8,128)(2,1)S(1)} %get-tuple-element.44), channel_id=1, source_target_pairs={{0,96},{32,128},{64,160},{96,192},{128,224},{160,256},{192,288},{2... | collective-permute-start | bytes 208904 | tf_op jit(solution)/shard_map/ppermute | solution.py:422
  30.4 14.8 %all-to-all-start.1 = ((bf16[4,8,128,128]{3,2,1,0:T(8,128)(2,1)}), bf16[4,8,128,128]{3,2,1,0:T(8,128)(2,1)S(1)}, u32[]{:S(2)}, u32[]{:S(2)}) async-start(bf16[4,8,128,128]{3,2,1,0:T(8,128)(2,1)} %shard_map.159), calls=%async_computation.1 | async-start | bytes 2097152 | tf_op jit(solution)/shard_map/all_to_all | solution.py:435
  34.4 17.9 %copy-start.11 = (bf16[256,256]{1,0:T(8,128)(2,1)S(1)}, bf16[256,256]{1,0:T(8,128)(2,1)}, u32[]{:S(2)}) copy-start(bf16[256,256]{1,0:T(8,128)(2,1)} %q_ref.1) | copy-start | bytes 393220
  34.5 18.7 %collective-permute-start.6 = (bf16[272,128]{1,0:T(8,128)(2,1)S(1)}, bf16[272,128]{1,0:T(8,128)(2,1)S(1)}, u32[]{:S(2)}, u32[]{:S(2)}) collective-permute-start(bf16[272,128]{1,0:T(8,128)(2,1)S(1)} %get-tuple-element.49), channel_id=1, source_target_pairs={{0,384},{32,416},{64,448},{96,480},{1,385},{33,417},{65,449},{97,4... | collective-permute-start | bytes 208904 | tf_op jit(solution)/shard_map/ppermute | solution.py:422
  41.4 11.9 %collective-permute-start.5 = (bf16[272,128]{1,0:T(8,128)(2,1)S(1)}, bf16[272,128]{1,0:T(8,128)(2,1)S(1)}, u32[]{:S(2)}, u32[]{:S(2)}) collective-permute-start(bf16[272,128]{1,0:T(8,128)(2,1)S(1)} %get-tuple-element.49), channel_id=1, source_target_pairs={{0,256},{32,288},{64,320},{96,352},{128,384},{160,416},{192,448},{... | collective-permute-start | bytes 208904 | tf_op jit(solution)/shard_map/ppermute | solution.py:422
  42.7 10.6 %collective-permute-start.4 = (bf16[272,128]{1,0:T(8,128)(2,1)S(1)}, bf16[272,128]{1,0:T(8,128)(2,1)S(1)}, u32[]{:S(2)}, u32[]{:S(2)}) collective-permute-start(bf16[272,128]{1,0:T(8,128)(2,1)S(1)} %get-tuple-element.49), channel_id=1, source_target_pairs={{0,128},{32,160},{64,192},{96,224},{128,256},{160,288},{192,320},{... | collective-permute-start | bytes 208904 | tf_op jit(solution)/shard_map/ppermute | solution.py:422
  45.2 9.4 %collective-permute-start = (bf16[4,8,128,128]{3,2,1,0:T(8,128)(2,1)S(1)}, bf16[4,8,128,128]{3,2,1,0:T(8,128)(2,1)S(1)}, u32[]{:S(2)}, u32[]{:S(2)}) collective-permute-start(bf16[4,8,128,128]{3,2,1,0:T(8,128)(2,1)S(1)} %all-to-all-done.1.kv_ref), channel_id=1, source_target_pairs={{0,32},{32,0},{1,33},{33,1},{2,34},{34,2},{3,35},{35,3},{4,36},{36... | collective-permute-start | bytes 3145736 | tf_op jit(solution)/shard_map/ppermute | solution.py:437

commit v6 on v5

--- a/solution.py
+++ b/solution.py
@@ -319,7 +319,8 @@
     attended = jnp.concatenate(parts, axis=1).astype(BF16)
     o_ref[...] = attended
     a = to_lanes(attended.astype(F32) * rows_ref[2:3, :])
-    stats = jnp.concatenate([stats_ref[...]] + a + [jnp.zeros((2, DIM), F32)], axis=0)
+    seg = [rows_ref[3:4, :DIM], rows_ref[3:4, DIM:]]
+    stats = jnp.concatenate([stats_ref[...]] + a + seg, axis=0).astype(BF16)
     for n in range(send_ref.shape[0]):
         send_ref[n] = stats
 
@@ -329,26 +330,32 @@
     return jnp.sum(jnp.transpose(full), axis=0, keepdims=True)
 
 
-def middle_sums_kernel(got_ref, rows_ref, send_ref):
-    total = got_ref[0]
-    for n in range(1, got_ref.shape[0]):
-        total = total + got_ref[n]
+def middle_sums_kernel(got_ref, send_ref):
     segment = lax.broadcasted_iota(jnp.int32, (SEGMENTS, DIM), 0)
-    seg = jnp.concatenate([rows_ref[3:4, :DIM], rows_ref[3:4, DIM:]], axis=0)
-    held = seg.astype(jnp.int32)
-    part = jnp.zeros((SEGMENTS, DIM), F32)
-    for j in range(2):
-        part = part + jnp.where(held[j : j + 1] == segment, total[4 + j : 5 + j], 0.0)
-    part = segment_row(part)
-    high = part.astype(BF16).astype(F32)
-    out = jnp.concatenate([total[0:4], high, part - high, seg], axis=0).astype(BF16)
+    plane = got_ref.shape[0] // 2
+    rows = []
+    for core in range(2):
+        low = got_ref[core * plane].astype(F32)
+        total = low
+        for n in range(1, plane):
+            total = total + got_ref[core * plane + n].astype(F32)
+        seg = low[6:8]
+        held = seg.astype(jnp.int32)
+        part = jnp.zeros((SEGMENTS, DIM), F32)
+        for j in range(2):
+            part = part + jnp.where(held[j : j + 1] == segment, total[4 + j : 5 + j], 0.0)
+        part = segment_row(part)
+        high = part.astype(BF16).astype(F32)
+        rows += [total[0:4], high, part - high, seg]
+    out = jnp.concatenate(rows, axis=0).astype(BF16)
     for n in range(send_ref.shape[0]):
         send_ref[n] = out
 
 
 def final_kernel(got_ref, gated_ref, rows_ref, o_ref, values_ref):
-    index = lax.axis_index("zl") * 2 + lax.axis_index("core")
-    mine = got_ref[2 * index].astype(F32) + got_ref[2 * index + 1].astype(F32)
+    zl, core = lax.axis_index("zl"), lax.axis_index("core")
+    mine = got_ref[2 * zl].astype(F32) + got_ref[2 * zl + 1].astype(F32)
+    mine = jnp.where(core == 0, mine[0:8], mine[8:16])
     gain = rows_ref[0:1, :]
     for b in range(2):
         rows = pl.ds(b * DIM, DIM)
@@ -363,15 +370,17 @@
     extra = jnp.zeros((8, DIM), F32)
     for s in range(got_ref.shape[0] // 2):
         low = got_ref[2 * s].astype(F32)
-        both = low + got_ref[2 * s + 1].astype(F32)
-        extra = extra + both
-        scale = lax.rsqrt(both[0:2] * (1.0 / COLUMNS) + EPS)
-        score = scale * both[2:4]
-        seg = low[6:8].astype(jnp.int32)
-        for j in range(2):
-            member = seg[j : j + 1] == segment
-            part = part + jnp.where(member, score[j : j + 1], 0.0)
-            count = count + jnp.where(member, 1.0, 0.0)
+        pair = low + got_ref[2 * s + 1].astype(F32)
+        for c in range(2):
+            both = pair[8 * c : 8 * c + 8]
+            extra = extra + both
+            scale = lax.rsqrt(both[0:2] * (1.0 / COLUMNS) + EPS)
+            score = scale * both[2:4]
+            seg = low[8 * c + 6 : 8 * c + 8].astype(jnp.int32)
+            for j in range(2):
+                member = seg[j : j + 1] == segment
+                part = part + jnp.where(member, score[j : j + 1], 0.0)
+                count = count + jnp.where(member, 1.0, 0.0)
     total = segment_row(part) + extra[4:5] + extra[5:6]
     held = segment_row(count)
     values_ref[...] = (total / jnp.maximum(held, 1.0))[:, :SEGMENTS]
@@ -447,15 +456,15 @@
     head_plane = lax.axis_size("y") * wide
     attended, send = call(
         attend_other_kernel,
-        (shape((tokens, 256), BF16), shape((head_plane, 8, DIM))),
+        (shape((tokens, 256), BF16), shape((2 * head_plane, 8, DIM), BF16)),
         [VMEM] * 7,
         [pltpu.VMEM((512, DIM), F32) for _ in range(3)] + [scores],
         flops=10**9,
     )(attention[0], theirs, *attention[1:], rows, stats)
-    summed = lax.all_to_all(send, ("y", "x"), 0, 0)
-    line = ctx * lax.axis_size("zh")
-    send = call(middle_sums_kernel, shape((line, 8, DIM), BF16), [VMEM] * 2)(summed, rows)
-    summed = lax.all_to_all(send, ("zl", "core", "zh"), 0, 0)
+    summed = lax.all_to_all(send, ("core", "y", "x"), 0, 0)
+    line = chips * lax.axis_size("zh")
+    send = call(middle_sums_kernel, shape((line, 16, DIM), BF16), [VMEM])(summed)
+    summed = lax.all_to_all(send, ("zl", "zh"), 0, 0)
     state_mixed, values = call(
         final_kernel, (shape((tokens, 256), BF16), shape((1, SEGMENTS))), [VMEM] * 3
     )(summed, gated, rows)

time: 95.7 us -> 94.3 us (0.985)
  blocking collectives: 37.7 us -> 36.4 us
    all_to_all x2, blocking collectives: 37.7 us -> 36.4 us  [the longest x1 24.1 us: per_device(): summed = lax.all_to_all(send, ('zl', 'zh'), 0, 0)]
where the time goes in v6:
time: 94.3 us; the launch traced here: 93.7 us
  starting transfers between devices  45.4 us (48%)
  blocking collectives  36.4 us (39%)
  Pallas kernels  9.02 us (10%)
  waiting for transfers between devices  1.3 us (1%)
    all_to_all x1, blocking collectives, per_device(): summed = lax.all_to_all(send, ('zl', 'zh'), 0, 0)  24.1 us
    ppermute x6, starting transfers between devices, shifted(): return lax.ppermute(v, CTX, [(i, i + by) for i in range(ctx - by)])  21 us
    all_to_all x1, starting transfers between devices, per_device(): quarter = lax.all_to_all(packed, 'zl', 0, 0)  13.2 us
    all_to_all x1, blocking collectives, per_device(): summed = lax.all_to_all(send, ('core', 'y', 'x'), 0, 0)  12.2 us
    ppermute x1, starting transfers between devices, per_device(): theirs = lax.ppermute(mine, 'core', [(0, 1), (1, 0)])  7.16 us
    all_to_all x1, starting transfers between devices, per_device(): mine = lax.all_to_all(fan, 'x', 0, 0)  4.01 us
  transfers between devices with their start and end apart: 9, of which 2 were waited for; matrix products, arithmetic and copies ran while one was open for 0% of the time, Pallas kernels for 5%

profile of v6, /device:TPU:1, one launch (start us, length us, event | category | flops | bytes accessed | tf_op | source)
XLA Modules:
  0.0 93.7 jit_solution(16262307388704034448)
XLA Ops:
  0.6 1.5 %shard_map.157 = bf16[8,128,128]{2,1,0:T(8,128)(2,1)} custom-call(bf16[256,1024]{1,0:T(8,128)(2,1)} %k_hbm.1, bf16[256,1024]{1,0:T(8,128)(2,1)} %v_hbm.1), custom_call_target="tpu_custom_call" | custom-call | flops 1000000 | bytes 1000000 | tf_op jit(solution)/shard_map/pallas_call | solution.py:415
  2.1 0.0 copy-start
  2.1 0.0 copy-start.1
  2.2 0.0 copy-start.7
  2.2 0.0 copy-start.8
  2.2 0.0 copy-start.9
  2.2 13.2 %all-to-all-start = ((bf16[8,128,128]{2,1,0:T(8,128)(2,1)}), bf16[8,128,128]{2,1,0:T(8,128)(2,1)S(1)}, u32[]{:S(2)}, u32[]{:S(2)}) async-start(bf16[8,128,128]{2,1,0:T(8,128)(2,1)} %shard_map.157), calls=%async_computation | async-start | bytes 524288 | tf_op jit(solution)/shard_map/all_to_all | solution.py:423
  15.4 0.0 copy-start.5
  15.5 0.6 copy-done.4
  16.1 0.0 copy-done.6
  16.1 1.0 %shard_map.160 = (f32[264,128]{1,0:T(8,128)S(1)}, bf16[272,128]{1,0:T(8,128)(2,1)S(1)}, f32[8,256]{1,0:T(8,128)S(1)}) custom-call(f32[2]{0:T(128)S(1)} %copy-done.5, bf16[256,256]{1,0:T(8,128)(2,1)S(1)} %copy-done, bf16[256,256]{1,0:T(8,128)(2,1)S(1)} %copy-done.1, s32[2,256]{1,0:T(2,128)S(1)} %bitcast.6, f32[1,256]{1,0:T(1,128)S(1)} %bitcast.8, ...), custom_call_target="tpu_custom_call" | custom-call | flops 1000000 | bytes 1000000 | tf_op jit(solution)/shard_map/pallas_call | solution.py:424
  17.2 0.0 copy-start.10
  17.2 4.5 %collective-permute-start.3 = (bf16[272,128]{1,0:T(8,128)(2,1)S(1)}, bf16[272,128]{1,0:T(8,128)(2,1)S(1)}, u32[]{:S(2)}, u32[]{:S(2)}) collective-permute-start(bf16[272,128]{1,0:T(8,128)(2,1)S(1)} %get-tuple-element.44), channel_id=1, source_target_pairs={{0,32},{32,64},{64,96},{96,128},{128,160},{160,192},{192,224},{224... | collective-permute-start | bytes 208904 | tf_op jit(solution)/shard_map/ppermute | solution.py:431
  21.7 3.1 %collective-permute-start.2 = (bf16[272,128]{1,0:T(8,128)(2,1)S(1)}, bf16[272,128]{1,0:T(8,128)(2,1)S(1)}, u32[]{:S(2)}, u32[]{:S(2)}) collective-permute-start(bf16[272,128]{1,0:T(8,128)(2,1)S(1)} %get-tuple-element.44), channel_id=1, source_target_pairs={{0,64},{32,96},{64,128},{96,160},{128,192},{160,224},{192,256},{22... | collective-permute-start | bytes 208904 | tf_op jit(solution)/shard_map/ppermute | solution.py:431
  24.8 3.1 %collective-permute-start.1 = (bf16[272,128]{1,0:T(8,128)(2,1)S(1)}, bf16[272,128]{1,0:T(8,128)(2,1)S(1)}, u32[]{:S(2)}, u32[]{:S(2)}) collective-permute-start(bf16[272,128]{1,0:T(8,128)(2,1)S(1)} %get-tuple-element.44), channel_id=1, source_target_pairs={{0,96},{32,128},{64,160},{96,192},{128,224},{160,256},{192,288},{2... | collective-permute-start | bytes 208904 | tf_op jit(solution)/shard_map/ppermute | solution.py:431
  27.9 1.4 %shard_map.158 = (f32[256,256]{1,0:T(8,128)S(1)}, f32[256,256]{1,0:T(8,128)S(1)}) custom-call(bf16[256,256]{1,0:T(8,128)(2,1)S(1)} %copy-done, bf16[256,256]{1,0:T(8,128)(2,1)S(1)} %copy-done.1, bf16[256,256]{1,0:T(8,128)(2,1)S(1)} %copy-done.3, bf16[256,256]{1,0:T(8,128)(2,1)S(1)} %copy-done.2, s32[2,256]{1,0:T(2,128)S(1)} %bitcast.7, f32[2]{0:T(128)S(1)} %copy-done.5, ...), custom_call_target="tpu_custom_call" | custom-call | flops 1000000 | bytes 1000000 | tf_op jit(solution)/shard_map/pallas_call | solution.py:434
  29.3 1.1 %shard_map.159 = bf16[4,8,128,128]{3,2,1,0:T(8,128)(2,1)} custom-call(bf16[8,128,128]{2,1,0:T(8,128)(2,1)S(1)} %all-to-all-done.quarter_ref), custom_call_target="tpu_custom_call" | custom-call | flops 1000000 | bytes 1000000 | tf_op jit(solution)/shard_map/pallas_call | solution.py:438
  30.4 4.0 %all-to-all-start.1 = ((bf16[4,8,128,128]{3,2,1,0:T(8,128)(2,1)}), bf16[4,8,128,128]{3,2,1,0:T(8,128)(2,1)S(1)}, u32[]{:S(2)}, u32[]{:S(2)}) async-start(bf16[4,8,128,128]{3,2,1,0:T(8,128)(2,1)} %shard_map.159), calls=%async_computation.1 | async-start | bytes 2097152 | tf_op jit(solution)/shard_map/all_to_all | solution.py:444
  34.4 0.1 shard_map.161
  34.5 6.9 %collective-permute-start.6 = (bf16[272,128]{1,0:T(8,128)(2,1)S(1)}, bf16[272,128]{1,0:T(8,128)(2,1)S(1)}, u32[]{:S(2)}, u32[]{:S(2)}) collective-permute-start(bf16[272,128]{1,0:T(8,128)(2,1)S(1)} %get-tuple-element.49), channel_id=1, source_target_pairs={{0,384},{32,416},{64,448},{96,480},{1,385},{33,417},{65,449},{97,4... | collective-permute-start | bytes 208904 | tf_op jit(solution)/shard_map/ppermute | solution.py:431
  41.4 1.3 %collective-permute-start.5 = (bf16[272,128]{1,0:T(8,128)(2,1)S(1)}, bf16[272,128]{1,0:T(8,128)(2,1)S(1)}, u32[]{:S(2)}, u32[]{:S(2)}) collective-permute-start(bf16[272,128]{1,0:T(8,128)(2,1)S(1)} %get-tuple-element.49), channel_id=1, source_target_pairs={{0,256},{32,288},{64,320},{96,352},{128,384},{160,416},{192,448},{... | collective-permute-start | bytes 208904 | tf_op jit(solution)/shard_map/ppermute | solution.py:431
  42.7 2.2 %collective-permute-start.4 = (bf16[272,128]{1,0:T(8,128)(2,1)S(1)}, bf16[272,128]{1,0:T(8,128)(2,1)S(1)}, u32[]{:S(2)}, u32[]{:S(2)}) collective-permute-start(bf16[272,128]{1,0:T(8,128)(2,1)S(1)} %get-tuple-element.49), channel_id=1, source_target_pairs={{0,128},{32,160},{64,192},{96,224},{128,256},{160,288},{192,320},{... | collective-permute-start | bytes 208904 | tf_op jit(solution)/shard_map/ppermute | solution.py:431
  44.9 0.3 all-to-all-done.1.kv_ref
  45.2 7.2 %collective-permute-start = (bf16[4,8,128,128]{3,2,1,0:T(8,128)(2,1)S(1)}, bf16[4,8,128,128]{3,2,1,0:T(8,128)(2,1)S(1)}, u32[]{:S(2)}, u32[]{:S(2)}) collective-permute-start(bf16[4,8,128,128]{3,2,1,0:T(8,128)(2,1)S(1)} %all-to-all-done.1.kv_ref), channel_id=1, source_target_pairs={{0,32},{32,0},{1,33},{33,1},{2,34},{34,2},{3,35},{35,3},{4,36},{36... | collective-permute-start | bytes 3145736 | tf_op jit(solution)/shard_map/ppermute | solution.py:446
  52.4 0.8 shard_map.162
  53.3 0.4 shard_map.163
  53.7 1.0 %collective-permute-done.kv_ref = bf16[4,8,128,128]{3,2,1,0:T(8,128)(2,1)S(1)} collective-permute-done((bf16[4,8,128,128]{3,2,1,0:T(8,128)(2,1)S(1)}, bf16[4,8,128,128]{3,2,1,0:T(8,128)(2,1)S(1)}, u32[]{:S(2)}, u32[]{:S(2)}) %collective-permute-start) | collective-permute-done | bytes 1048608 | tf_op jit(solution)/shard_map/ppermute | solution.py:446
  54.6 1.7 %shard_map.164 = (bf16[256,256]{1,0:T(8,128)(2,1)}, bf16[32,8,128]{2,1,0:T(8,128)(2,1)S(1)}) custom-call(bf16[512,256]{1,0:T(8,128)(2,1)S(1)} %get-tuple-element.66.scaled_ref, bf16[4,8,128,128]{3,2,1,0:T(8,128)(2,1)S(1)} %collective-permute-done.kv_ref, f32[512,128]{1,0:T(8,128)S(1)} %get-tuple-element.68.m_in, f32[512,128]{1,0:T(8,128)S(1)} %get-tuple-element.69.l_in, ...), custom_call_target="tpu_custom_call" | custom-call | flops 1000000000 | bytes 1000000 | tf_op jit(solution)/shard_map/pallas_call | solution.py:457
  56.3 12.2 %all_to_all.20.got_ref = bf16[32,8,128]{2,1,0:T(8,128)(2,1)S(1)} all-to-all(bf16[32,8,128]{2,1,0:T(8,128)(2,1)S(1)} %get-tuple-element.73), channel_id=1, replica_groups=mesh['zl'=8,'core'=2,'zh'=2,'y'=4,'x'=4] {'core','y','x'}, dimensions={0} | all-to-all | bytes 131072 | tf_op jit(solution)/shard_map/all_to_all | solution.py:464
  68.5 0.1 shard_map.165
  68.7 24.1 %all_to_all.21.got_ref = bf16[16,16,128]{2,1,0:T(8,128)(2,1)S(1)} all-to-all(bf16[16,16,128]{2,1,0:T(8,128)(2,1)S(1)} %shard_map.165), channel_id=1, replica_groups=mesh['zl'=8,'core'=2,'zh'=2,'y'=4,'x'=4] {'zl','zh'}, dimensions={0} | all-to-all | bytes 131072 | tf_op jit(solution)/shard_map/all_to_all | solution.py:467
  92.8 0.9 shard_map.166
  (22 shorter events, 0.1 us)
Async XLA Ops:
  2.1 13.3 %copy-start = (bf16[256,256]{1,0:T(8,128)(2,1)S(1)}, bf16[256,256]{1,0:T(8,128)(2,1)}, u32[]{:S(2)}) copy-start(bf16[256,256]{1,0:T(8,128)(2,1)} %x_ref.3) | copy-start | bytes 393220
  2.1 13.3 %copy-start.1 = (bf16[256,256]{1,0:T(8,128)(2,1)S(1)}, bf16[256,256]{1,0:T(8,128)(2,1)}, u32[]{:S(2)}) copy-start(bf16[256,256]{1,0:T(8,128)(2,1)} %w_ref.3) | copy-start | bytes 393220
  2.2 13.3 %copy-start.7 = (f32[256]{0:T(256)S(1)}, f32[256]{0:T(256)}, u32[]{:S(2)}) copy-start(f32[256]{0:T(256)} %param.26) | copy-start | bytes 3076
  2.2 13.3 %copy-start.8 = (f32[256]{0:T(256)S(1)}, f32[256]{0:T(256)}, u32[]{:S(2)}) copy-start(f32[256]{0:T(256)} %param.25) | copy-start | bytes 3076
  2.2 13.3 %copy-start.9 = (s32[256]{0:T(256)S(1)}, s32[256]{0:T(256)}, u32[]{:S(2)}) copy-start(s32[256]{0:T(256)} %param.27) | copy-start | bytes 3076
  2.2 27.1 %all-to-all-start = ((bf16[8,128,128]{2,1,0:T(8,128)(2,1)}), bf16[8,128,128]{2,1,0:T(8,128)(2,1)S(1)}, u32[]{:S(2)}, u32[]{:S(2)}) async-start(bf16[8,128,128]{2,1,0:T(8,128)(2,1)} %shard_map.157), calls=%async_computation | async-start | bytes 524288 | tf_op jit(solution)/shard_map/all_to_all | solution.py:423
  15.4 0.7 copy-start.4
  15.4 0.7 copy-start.5
  15.4 0.7 copy-start.6
  16.1 11.8 %copy-start.2 = (bf16[256,256]{1,0:T(8,128)(2,1)S(1)}, bf16[256,256]{1,0:T(8,128)(2,1)}, u32[]{:S(2)}) copy-start(bf16[256,256]{1,0:T(8,128)(2,1)} %g_ref.1) | copy-start | bytes 393220
  16.1 11.8 %copy-start.3 = (bf16[256,256]{1,0:T(8,128)(2,1)S(1)}, bf16[256,256]{1,0:T(8,128)(2,1)}, u32[]{:S(2)}) copy-start(bf16[256,256]{1,0:T(8,128)(2,1)} %r_ref.3) | copy-start | bytes 393220
  17.2 10.7 %copy-start.10 = (f32[2]{0:T(128)S(1)}, f32[2]{0:T(128)}, u32[]{:S(2)}) copy-start(f32[2]{0:T(128)} %skip_ref.1) | copy-start | bytes 28
  17.2 17.2 %collective-permute-start.3 = (bf16[272,128]{1,0:T(8,128)(2,1)S(1)}, bf16[272,128]{1,0:T(8,128)(2,1)S(1)}, u32[]{:S(2)}, u32[]{:S(2)}) collective-permute-start(bf16[272,128]{1,0:T(8,128)(2,1)S(1)} %get-tuple-element.44), channel_id=1, source_target_pairs={{0,32},{32,64},{64,96},{96,128},{128,160},{160,192},{192,224},{224... | collective-permute-start | bytes 208904 | tf_op jit(solution)/shard_map/ppermute | solution.py:431
  21.7 12.7 %collective-permute-start.2 = (bf16[272,128]{1,0:T(8,128)(2,1)S(1)}, bf16[272,128]{1,0:T(8,128)(2,1)S(1)}, u32[]{:S(2)}, u32[]{:S(2)}) collective-permute-start(bf16[272,128]{1,0:T(8,128)(2,1)S(1)} %get-tuple-element.44), channel_id=1, source_target_pairs={{0,64},{32,96},{64,128},{96,160},{128,192},{160,224},{192,256},{22... | collective-permute-start | bytes 208904 | tf_op jit(solution)/shard_map/ppermute | solution.py:431
  24.8 9.7 %collective-permute-start.1 = (bf16[272,128]{1,0:T(8,128)(2,1)S(1)}, bf16[272,128]{1,0:T(8,128)(2,1)S(1)}, u32[]{:S(2)}, u32[]{:S(2)}) collective-permute-start(bf16[272,128]{1,0:T(8,128)(2,1)S(1)} %get-tuple-element.44), channel_id=1, source_target_pairs={{0,96},{32,128},{64,160},{96,192},{128,224},{160,256},{192,288},{2... | collective-permute-start | bytes 208904 | tf_op jit(solution)/shard_map/ppermute | solution.py:431
  30.4 14.8 %all-to-all-start.1 = ((bf16[4,8,128,128]{3,2,1,0:T(8,128)(2,1)}), bf16[4,8,128,128]{3,2,1,0:T(8,128)(2,1)S(1)}, u32[]{:S(2)}, u32[]{:S(2)}) async-start(bf16[4,8,128,128]{3,2,1,0:T(8,128)(2,1)} %shard_map.159), calls=%async_computation.1 | async-start | bytes 2097152 | tf_op jit(solution)/shard_map/all_to_all | solution.py:444
  34.4 17.9 %copy-start.11 = (bf16[256,256]{1,0:T(8,128)(2,1)S(1)}, bf16[256,256]{1,0:T(8,128)(2,1)}, u32[]{:S(2)}) copy-start(bf16[256,256]{1,0:T(8,128)(2,1)} %q_ref.1) | copy-start | bytes 393220
  34.5 18.7 %collective-permute-start.6 = (bf16[272,128]{1,0:T(8,128)(2,1)S(1)}, bf16[272,128]{1,0:T(8,128)(2,1)S(1)}, u32[]{:S(2)}, u32[]{:S(2)}) collective-permute-start(bf16[272,128]{1,0:T(8,128)(2,1)S(1)} %get-tuple-element.49), channel_id=1, source_target_pairs={{0,384},{32,416},{64,448},{96,480},{1,385},{33,417},{65,449},{97,4... | collective-permute-start | bytes 208904 | tf_op jit(solution)/shard_map/ppermute | solution.py:431
  41.4 11.9 %collective-permute-start.5 = (bf16[272,128]{1,0:T(8,128)(2,1)S(1)}, bf16[272,128]{1,0:T(8,128)(2,1)S(1)}, u32[]{:S(2)}, u32[]{:S(2)}) collective-permute-start(bf16[272,128]{1,0:T(8,128)(2,1)S(1)} %get-tuple-element.49), channel_id=1, source_target_pairs={{0,256},{32,288},{64,320},{96,352},{128,384},{160,416},{192,448},{... | collective-permute-start | bytes 208904 | tf_op jit(solution)/shard_map/ppermute | solution.py:431
  42.7 10.6 %collective-permute-start.4 = (bf16[272,128]{1,0:T(8,128)(2,1)S(1)}, bf16[272,128]{1,0:T(8,128)(2,1)S(1)}, u32[]{:S(2)}, u32[]{:S(2)}) collective-permute-start(bf16[272,128]{1,0:T(8,128)(2,1)S(1)} %get-tuple-element.49), channel_id=1, source_target_pairs={{0,128},{32,160},{64,192},{96,224},{128,256},{160,288},{192,320},{... | collective-permute-start | bytes 208904 | tf_op jit(solution)/shard_map/ppermute | solution.py:431
  45.2 9.4 %collective-permute-start = (bf16[4,8,128,128]{3,2,1,0:T(8,128)(2,1)S(1)}, bf16[4,8,128,128]{3,2,1,0:T(8,128)(2,1)S(1)}, u32[]{:S(2)}, u32[]{:S(2)}) collective-permute-start(bf16[4,8,128,128]{3,2,1,0:T(8,128)(2,1)S(1)} %all-to-all-done.1.kv_ref), channel_id=1, source_target_pairs={{0,32},{32,0},{1,33},{33,1},{2,34},{34,2},{3,35},{35,3},{4,36},{36... | collective-permute-start | bytes 3145736 | tf_op jit(solution)/shard_map/ppermute | solution.py:446

commit v7 on v6

--- a/solution.py
+++ b/solution.py
@@ -442,13 +442,13 @@
     )(*got[::-1], own)
 
     mine = lax.all_to_all(fan, "x", 0, 0)
-    arrived = tuple(shifted(send, by) for by in (4, 8, 12))
+    arrived = tuple(shifted(send, by) for by in (4, 12, 8))
     theirs = lax.ppermute(mine, "core", [(0, 1), (1, 0)])
     running = (shape((512, 256), BF16),) + (shape((512, DIM)),) * 3
     scores = pltpu.VMEM((chips // 2, 512, 512), F32)
     attention = call(attend_own_kernel, running, [VMEM] * 2, [scores], flops=10**9)(queries, mine)
     arrived, attention = together((arrived, attention))
-    near, mid, far = arrived
+    near, far, mid = arrived
     gated, stats = call(
         carried_kernel, (shape((tokens, 256)), shape((4, DIM))), [VMEM] * 8, flops=CARRIED_FLOPS
     )(near, mid, far, before, state_read, base, carry, rows)

time: 94.3 us -> 92.8 us (0.984)
  blocking collectives: 36.4 us -> 34.9 us
    all_to_all x1, blocking collectives: 24.1 us -> 22.6 us  [per_device(): summed = lax.all_to_all(send, ('zl', 'zh'), 0, 0)]
where the time goes in v7:
time: 92.8 us; the launch traced here: 92.2 us
  starting transfers between devices  44.8 us (48%)
  blocking collectives  34.9 us (38%)
  Pallas kernels  9.02 us (10%)
  waiting for transfers between devices  1.93 us (2%)
    all_to_all x1, blocking collectives, per_device(): summed = lax.all_to_all(send, ('zl', 'zh'), 0, 0)  22.6 us
    ppermute x6, starting transfers between devices, shifted(): return lax.ppermute(v, CTX, [(i, i + by) for i in range(ctx - by)])  20.4 us
    all_to_all x1, starting transfers between devices, per_device(): quarter = lax.all_to_all(packed, 'zl', 0, 0)  13.2 us
    all_to_all x1, blocking collectives, per_device(): summed = lax.all_to_all(send, ('core', 'y', 'x'), 0, 0)  12.2 us
    ppermute x1, starting transfers between devices, per_device(): theirs = lax.ppermute(mine, 'core', [(0, 1), (1, 0)])  7.16 us
    all_to_all x1, starting transfers between devices, per_device(): mine = lax.all_to_all(fan, 'x', 0, 0)  4.01 us
  transfers between devices with their start and end apart: 9, of which 2 were waited for; matrix products, arithmetic and copies ran while one was open for 0% of the time, Pallas kernels for 5%

profile of v7, /device:TPU:1, one launch (start us, length us, event | category | flops | bytes accessed | tf_op | source)
XLA Modules:
  0.0 92.2 jit_solution(17756950340095965098)
XLA Ops:
  0.6 1.5 %shard_map.157 = bf16[8,128,128]{2,1,0:T(8,128)(2,1)} custom-call(bf16[256,1024]{1,0:T(8,128)(2,1)} %k_hbm.1, bf16[256,1024]{1,0:T(8,128)(2,1)} %v_hbm.1), custom_call_target="tpu_custom_call" | custom-call | flops 1000000 | bytes 1000000 | tf_op jit(solution)/shard_map/pallas_call | solution.py:415
  2.1 0.0 copy-start
  2.1 0.0 copy-start.1
  2.2 0.0 copy-start.7
  2.2 0.0 copy-start.8
  2.2 13.2 %all-to-all-start = ((bf16[8,128,128]{2,1,0:T(8,128)(2,1)}), bf16[8,128,128]{2,1,0:T(8,128)(2,1)S(1)}, u32[]{:S(2)}, u32[]{:S(2)}) async-start(bf16[8,128,128]{2,1,0:T(8,128)(2,1)} %shard_map.157), calls=%async_computation | async-start | bytes 524288 | tf_op jit(solution)/shard_map/all_to_all | solution.py:423
  15.4 0.0 copy-start.6
  15.5 0.6 copy-done.4
  16.1 0.0 copy-done.6
  16.1 1.0 %shard_map.160 = (f32[264,128]{1,0:T(8,128)S(1)}, bf16[272,128]{1,0:T(8,128)(2,1)S(1)}, f32[8,256]{1,0:T(8,128)S(1)}) custom-call(f32[2]{0:T(128)S(1)} %copy-done.5, bf16[256,256]{1,0:T(8,128)(2,1)S(1)} %copy-done, bf16[256,256]{1,0:T(8,128)(2,1)S(1)} %copy-done.1, s32[2,256]{1,0:T(2,128)S(1)} %bitcast.6, f32[1,256]{1,0:T(1,128)S(1)} %bitcast.8, ...), custom_call_target="tpu_custom_call" | custom-call | flops 1000000 | bytes 1000000 | tf_op jit(solution)/shard_map/pallas_call | solution.py:424
  17.2 0.0 copy-start.10
  17.2 4.5 %collective-permute-start.3 = (bf16[272,128]{1,0:T(8,128)(2,1)S(1)}, bf16[272,128]{1,0:T(8,128)(2,1)S(1)}, u32[]{:S(2)}, u32[]{:S(2)}) collective-permute-start(bf16[272,128]{1,0:T(8,128)(2,1)S(1)} %get-tuple-element.44), channel_id=1, source_target_pairs={{0,32},{32,64},{64,96},{96,128},{128,160},{160,192},{192,224},{224... | collective-permute-start | bytes 208904 | tf_op jit(solution)/shard_map/ppermute | solution.py:431
  21.7 3.1 %collective-permute-start.2 = (bf16[272,128]{1,0:T(8,128)(2,1)S(1)}, bf16[272,128]{1,0:T(8,128)(2,1)S(1)}, u32[]{:S(2)}, u32[]{:S(2)}) collective-permute-start(bf16[272,128]{1,0:T(8,128)(2,1)S(1)} %get-tuple-element.44), channel_id=1, source_target_pairs={{0,64},{32,96},{64,128},{96,160},{128,192},{160,224},{192,256},{22... | collective-permute-start | bytes 208904 | tf_op jit(solution)/shard_map/ppermute | solution.py:431
  24.8 3.1 %collective-permute-start.1 = (bf16[272,128]{1,0:T(8,128)(2,1)S(1)}, bf16[272,128]{1,0:T(8,128)(2,1)S(1)}, u32[]{:S(2)}, u32[]{:S(2)}) collective-permute-start(bf16[272,128]{1,0:T(8,128)(2,1)S(1)} %get-tuple-element.44), channel_id=1, source_target_pairs={{0,96},{32,128},{64,160},{96,192},{128,224},{160,256},{192,288},{2... | collective-permute-start | bytes 208904 | tf_op jit(solution)/shard_map/ppermute | solution.py:431
  27.9 1.4 %shard_map.158 = (f32[256,256]{1,0:T(8,128)S(1)}, f32[256,256]{1,0:T(8,128)S(1)}) custom-call(bf16[256,256]{1,0:T(8,128)(2,1)S(1)} %copy-done, bf16[256,256]{1,0:T(8,128)(2,1)S(1)} %copy-done.1, bf16[256,256]{1,0:T(8,128)(2,1)S(1)} %copy-done.3, bf16[256,256]{1,0:T(8,128)(2,1)S(1)} %copy-done.2, s32[2,256]{1,0:T(2,128)S(1)} %bitcast.7, f32[2]{0:T(128)S(1)} %copy-done.5, ...), custom_call_target="tpu_custom_call" | custom-call | flops 1000000 | bytes 1000000 | tf_op jit(solution)/shard_map/pallas_call | solution.py:434
  29.3 1.1 %shard_map.159 = bf16[4,8,128,128]{3,2,1,0:T(8,128)(2,1)} custom-call(bf16[8,128,128]{2,1,0:T(8,128)(2,1)S(1)} %all-to-all-done.quarter_ref), custom_call_target="tpu_custom_call" | custom-call | flops 1000000 | bytes 1000000 | tf_op jit(solution)/shard_map/pallas_call | solution.py:438
  30.4 4.0 %all-to-all-start.1 = ((bf16[4,8,128,128]{3,2,1,0:T(8,128)(2,1)}), bf16[4,8,128,128]{3,2,1,0:T(8,128)(2,1)S(1)}, u32[]{:S(2)}, u32[]{:S(2)}) async-start(bf16[4,8,128,128]{3,2,1,0:T(8,128)(2,1)} %shard_map.159), calls=%async_computation.1 | async-start | bytes 2097152 | tf_op jit(solution)/shard_map/all_to_all | solution.py:444
  34.4 0.0 copy-start.11
  34.4 0.1 shard_map.161
  34.5 7.0 %collective-permute-start.6 = (bf16[272,128]{1,0:T(8,128)(2,1)S(1)}, bf16[272,128]{1,0:T(8,128)(2,1)S(1)}, u32[]{:S(2)}, u32[]{:S(2)}) collective-permute-start(bf16[272,128]{1,0:T(8,128)(2,1)S(1)} %get-tuple-element.49), channel_id=1, source_target_pairs={{0,256},{32,288},{64,320},{96,352},{128,384},{160,416},{192,448},{... | collective-permute-start | bytes 208904 | tf_op jit(solution)/shard_map/ppermute | solution.py:431
  41.5 1.3 %collective-permute-start.5 = (bf16[272,128]{1,0:T(8,128)(2,1)S(1)}, bf16[272,128]{1,0:T(8,128)(2,1)S(1)}, u32[]{:S(2)}, u32[]{:S(2)}) collective-permute-start(bf16[272,128]{1,0:T(8,128)(2,1)S(1)} %get-tuple-element.49), channel_id=1, source_target_pairs={{0,384},{32,416},{64,448},{96,480},{1,385},{33,417},{65,449},{97,4... | collective-permute-start | bytes 208904 | tf_op jit(solution)/shard_map/ppermute | solution.py:431
  42.8 1.4 %collective-permute-start.4 = (bf16[272,128]{1,0:T(8,128)(2,1)S(1)}, bf16[272,128]{1,0:T(8,128)(2,1)S(1)}, u32[]{:S(2)}, u32[]{:S(2)}) collective-permute-start(bf16[272,128]{1,0:T(8,128)(2,1)S(1)} %get-tuple-element.49), channel_id=1, source_target_pairs={{0,128},{32,160},{64,192},{96,224},{128,256},{160,288},{192,320},{... | collective-permute-start | bytes 208904 | tf_op jit(solution)/shard_map/ppermute | solution.py:431
  44.3 0.9 %all-to-all-done.1.kv_ref = bf16[4,8,128,128]{3,2,1,0:T(8,128)(2,1)S(1)} async-done(((bf16[4,8,128,128]{3,2,1,0:T(8,128)(2,1)}), bf16[4,8,128,128]{3,2,1,0:T(8,128)(2,1)S(1)}, u32[]{:S(2)}, u32[]{:S(2)}) %all-to-all-start.1) | async-done | bytes 1048608 | tf_op jit(solution)/shard_map/all_to_all | solution.py:444
  45.2 7.2 %collective-permute-start = (bf16[4,8,128,128]{3,2,1,0:T(8,128)(2,1)S(1)}, bf16[4,8,128,128]{3,2,1,0:T(8,128)(2,1)S(1)}, u32[]{:S(2)}, u32[]{:S(2)}) collective-permute-start(bf16[4,8,128,128]{3,2,1,0:T(8,128)(2,1)S(1)} %all-to-all-done.1.kv_ref), channel_id=1, source_target_pairs={{0,32},{32,0},{1,33},{33,1},{2,34},{34,2},{3,35},{35,3},{4,36},{36... | collective-permute-start | bytes 3145736 | tf_op jit(solution)/shard_map/ppermute | solution.py:446
  52.4 0.8 shard_map.162
  53.3 0.4 shard_map.163
  53.7 1.0 %collective-permute-done.kv_ref = bf16[4,8,128,128]{3,2,1,0:T(8,128)(2,1)S(1)} collective-permute-done((bf16[4,8,128,128]{3,2,1,0:T(8,128)(2,1)S(1)}, bf16[4,8,128,128]{3,2,1,0:T(8,128)(2,1)S(1)}, u32[]{:S(2)}, u32[]{:S(2)}) %collective-permute-start) | collective-permute-done | bytes 1048608 | tf_op jit(solution)/shard_map/ppermute | solution.py:446
  54.6 1.7 %shard_map.164 = (bf16[256,256]{1,0:T(8,128)(2,1)}, bf16[32,8,128]{2,1,0:T(8,128)(2,1)S(1)}) custom-call(bf16[512,256]{1,0:T(8,128)(2,1)S(1)} %get-tuple-element.66.scaled_ref, bf16[4,8,128,128]{3,2,1,0:T(8,128)(2,1)S(1)} %collective-permute-done.kv_ref, f32[512,128]{1,0:T(8,128)S(1)} %get-tuple-element.68.m_in, f32[512,128]{1,0:T(8,128)S(1)} %get-tuple-element.69.l_in, ...), custom_call_target="tpu_custom_call" | custom-call | flops 1000000000 | bytes 1000000 | tf_op jit(solution)/shard_map/pallas_call | solution.py:457
  56.3 12.2 %all_to_all.20.got_ref = bf16[32,8,128]{2,1,0:T(8,128)(2,1)S(1)} all-to-all(bf16[32,8,128]{2,1,0:T(8,128)(2,1)S(1)} %get-tuple-element.73), channel_id=1, replica_groups=mesh['zl'=8,'core'=2,'zh'=2,'y'=4,'x'=4] {'core','y','x'}, dimensions={0} | all-to-all | bytes 131072 | tf_op jit(solution)/shard_map/all_to_all | solution.py:464
  68.5 0.1 shard_map.165
  68.7 22.6 %all_to_all.21.got_ref = bf16[16,16,128]{2,1,0:T(8,128)(2,1)S(1)} all-to-all(bf16[16,16,128]{2,1,0:T(8,128)(2,1)S(1)} %shard_map.165), channel_id=1, replica_groups=mesh['zl'=8,'core'=2,'zh'=2,'y'=4,'x'=4] {'zl','zh'}, dimensions={0} | all-to-all | bytes 131072 | tf_op jit(solution)/shard_map/all_to_all | solution.py:467
  91.3 0.9 %shard_map.166 = (bf16[256,256]{1,0:T(8,128)(2,1)}, f32[1,32]{1,0:T(1,128)}) custom-call(bf16[16,16,128]{2,1,0:T(8,128)(2,1)S(1)} %all_to_all.21.got_ref, f32[256,256]{1,0:T(8,128)S(1)} %get-tuple-element.74.gated_ref, f32[8,256]{1,0:T(8,128)S(1)} %get-tuple-element.64.rows_ref), custom_call_target="tpu_custom_call" | custom-call | flops 1000000 | bytes 1000000 | tf_op jit(solution)/shard_map/pallas_call | solution.py:468
  (22 shorter events, 0.1 us)
Async XLA Ops:
  2.1 13.3 %copy-start = (bf16[256,256]{1,0:T(8,128)(2,1)S(1)}, bf16[256,256]{1,0:T(8,128)(2,1)}, u32[]{:S(2)}) copy-start(bf16[256,256]{1,0:T(8,128)(2,1)} %x_ref.3) | copy-start | bytes 393220
  2.1 13.3 %copy-start.1 = (bf16[256,256]{1,0:T(8,128)(2,1)S(1)}, bf16[256,256]{1,0:T(8,128)(2,1)}, u32[]{:S(2)}) copy-start(bf16[256,256]{1,0:T(8,128)(2,1)} %w_ref.3) | copy-start | bytes 393220
  2.2 13.3 %copy-start.7 = (f32[256]{0:T(256)S(1)}, f32[256]{0:T(256)}, u32[]{:S(2)}) copy-start(f32[256]{0:T(256)} %param.26) | copy-start | bytes 3076
  2.2 13.3 %copy-start.8 = (f32[256]{0:T(256)S(1)}, f32[256]{0:T(256)}, u32[]{:S(2)}) copy-start(f32[256]{0:T(256)} %param.25) | copy-start | bytes 3076
  2.2 13.3 %copy-start.9 = (s32[256]{0:T(256)S(1)}, s32[256]{0:T(256)}, u32[]{:S(2)}) copy-start(s32[256]{0:T(256)} %param.27) | copy-start | bytes 3076
  2.2 27.1 %all-to-all-start = ((bf16[8,128,128]{2,1,0:T(8,128)(2,1)}), bf16[8,128,128]{2,1,0:T(8,128)(2,1)S(1)}, u32[]{:S(2)}, u32[]{:S(2)}) async-start(bf16[8,128,128]{2,1,0:T(8,128)(2,1)} %shard_map.157), calls=%async_computation | async-start | bytes 524288 | tf_op jit(solution)/shard_map/all_to_all | solution.py:423
  15.4 0.7 copy-start.4
  15.4 0.7 copy-start.5
  15.4 0.7 copy-start.6
  16.1 11.8 %copy-start.2 = (bf16[256,256]{1,0:T(8,128)(2,1)S(1)}, bf16[256,256]{1,0:T(8,128)(2,1)}, u32[]{:S(2)}) copy-start(bf16[256,256]{1,0:T(8,128)(2,1)} %g_ref.1) | copy-start | bytes 393220
  16.1 11.8 %copy-start.3 = (bf16[256,256]{1,0:T(8,128)(2,1)S(1)}, bf16[256,256]{1,0:T(8,128)(2,1)}, u32[]{:S(2)}) copy-start(bf16[256,256]{1,0:T(8,128)(2,1)} %r_ref.3) | copy-start | bytes 393220
  17.2 10.7 %copy-start.10 = (f32[2]{0:T(128)S(1)}, f32[2]{0:T(128)}, u32[]{:S(2)}) copy-start(f32[2]{0:T(128)} %skip_ref.1) | copy-start | bytes 28
  17.2 17.2 %collective-permute-start.3 = (bf16[272,128]{1,0:T(8,128)(2,1)S(1)}, bf16[272,128]{1,0:T(8,128)(2,1)S(1)}, u32[]{:S(2)}, u32[]{:S(2)}) collective-permute-start(bf16[272,128]{1,0:T(8,128)(2,1)S(1)} %get-tuple-element.44), channel_id=1, source_target_pairs={{0,32},{32,64},{64,96},{96,128},{128,160},{160,192},{192,224},{224... | collective-permute-start | bytes 208904 | tf_op jit(solution)/shard_map/ppermute | solution.py:431
  21.7 12.7 %collective-permute-start.2 = (bf16[272,128]{1,0:T(8,128)(2,1)S(1)}, bf16[272,128]{1,0:T(8,128)(2,1)S(1)}, u32[]{:S(2)}, u32[]{:S(2)}) collective-permute-start(bf16[272,128]{1,0:T(8,128)(2,1)S(1)} %get-tuple-element.44), channel_id=1, source_target_pairs={{0,64},{32,96},{64,128},{96,160},{128,192},{160,224},{192,256},{22... | collective-permute-start | bytes 208904 | tf_op jit(solution)/shard_map/ppermute | solution.py:431
  24.8 9.7 %collective-permute-start.1 = (bf16[272,128]{1,0:T(8,128)(2,1)S(1)}, bf16[272,128]{1,0:T(8,128)(2,1)S(1)}, u32[]{:S(2)}, u32[]{:S(2)}) collective-permute-start(bf16[272,128]{1,0:T(8,128)(2,1)S(1)} %get-tuple-element.44), channel_id=1, source_target_pairs={{0,96},{32,128},{64,160},{96,192},{128,224},{160,256},{192,288},{2... | collective-permute-start | bytes 208904 | tf_op jit(solution)/shard_map/ppermute | solution.py:431
  30.4 14.8 %all-to-all-start.1 = ((bf16[4,8,128,128]{3,2,1,0:T(8,128)(2,1)}), bf16[4,8,128,128]{3,2,1,0:T(8,128)(2,1)S(1)}, u32[]{:S(2)}, u32[]{:S(2)}) async-start(bf16[4,8,128,128]{3,2,1,0:T(8,128)(2,1)} %shard_map.159), calls=%async_computation.1 | async-start | bytes 2097152 | tf_op jit(solution)/shard_map/all_to_all | solution.py:444
  34.4 17.9 %copy-start.11 = (bf16[256,256]{1,0:T(8,128)(2,1)S(1)}, bf16[256,256]{1,0:T(8,128)(2,1)}, u32[]{:S(2)}) copy-start(bf16[256,256]{1,0:T(8,128)(2,1)} %q_ref.1) | copy-start | bytes 393220
  34.5 18.7 %collective-permute-start.6 = (bf16[272,128]{1,0:T(8,128)(2,1)S(1)}, bf16[272,128]{1,0:T(8,128)(2,1)S(1)}, u32[]{:S(2)}, u32[]{:S(2)}) collective-permute-start(bf16[272,128]{1,0:T(8,128)(2,1)S(1)} %get-tuple-element.49), channel_id=1, source_target_pairs={{0,256},{32,288},{64,320},{96,352},{128,384},{160,416},{192,448},{... | collective-permute-start | bytes 208904 | tf_op jit(solution)/shard_map/ppermute | solution.py:431
  41.5 11.7 %collective-permute-start.5 = (bf16[272,128]{1,0:T(8,128)(2,1)S(1)}, bf16[272,128]{1,0:T(8,128)(2,1)S(1)}, u32[]{:S(2)}, u32[]{:S(2)}) collective-permute-start(bf16[272,128]{1,0:T(8,128)(2,1)S(1)} %get-tuple-element.49), channel_id=1, source_target_pairs={{0,384},{32,416},{64,448},{96,480},{1,385},{33,417},{65,449},{97,4... | collective-permute-start | bytes 208904 | tf_op jit(solution)/shard_map/ppermute | solution.py:431
  42.8 10.4 %collective-permute-start.4 = (bf16[272,128]{1,0:T(8,128)(2,1)S(1)}, bf16[272,128]{1,0:T(8,128)(2,1)S(1)}, u32[]{:S(2)}, u32[]{:S(2)}) collective-permute-start(bf16[272,128]{1,0:T(8,128)(2,1)S(1)} %get-tuple-element.49), channel_id=1, source_target_pairs={{0,128},{32,160},{64,192},{96,224},{128,256},{160,288},{192,320},{... | collective-permute-start | bytes 208904 | tf_op jit(solution)/shard_map/ppermute | solution.py:431
  45.2 9.4 %collective-permute-start = (bf16[4,8,128,128]{3,2,1,0:T(8,128)(2,1)S(1)}, bf16[4,8,128,128]{3,2,1,0:T(8,128)(2,1)S(1)}, u32[]{:S(2)}, u32[]{:S(2)}) collective-permute-start(bf16[4,8,128,128]{3,2,1,0:T(8,128)(2,1)S(1)} %all-to-all-done.1.kv_ref), channel_id=1, source_target_pairs={{0,32},{32,0},{1,33},{33,1},{2,34},{34,2},{3,35},{35,3},{4,36},{36... | collective-permute-start | bytes 3145736 | tf_op jit(solution)/shard_map/ppermute | solution.py:446

commit v8 on v7

--- a/solution.py
+++ b/solution.py
@@ -442,13 +442,13 @@
     )(*got[::-1], own)
 
     mine = lax.all_to_all(fan, "x", 0, 0)
-    arrived = tuple(shifted(send, by) for by in (4, 12, 8))
+    arrived = tuple(shifted(send, by) for by in (12, 4, 8))
     theirs = lax.ppermute(mine, "core", [(0, 1), (1, 0)])
     running = (shape((512, 256), BF16),) + (shape((512, DIM)),) * 3
     scores = pltpu.VMEM((chips // 2, 512, 512), F32)
     attention = call(attend_own_kernel, running, [VMEM] * 2, [scores], flops=10**9)(queries, mine)
     arrived, attention = together((arrived, attention))
-    near, far, mid = arrived
+    far, near, mid = arrived
     gated, stats = call(
         carried_kernel, (shape((tokens, 256)), shape((4, DIM))), [VMEM] * 8, flops=CARRIED_FLOPS
     )(near, mid, far, before, state_read, base, carry, rows)

time: 92.8 us -> 93.4 us (level)
  no operation moved by 1% of the time
where the time goes in v8:
time: 93.4 us; the launch traced here: 92.8 us
  starting transfers between devices  45.4 us (49%)
  blocking collectives  35.5 us (38%)
  Pallas kernels  9.02 us (10%)
  waiting for transfers between devices  1.3 us (1%)
    all_to_all x1, blocking collectives, per_device(): summed = lax.all_to_all(send, ('zl', 'zh'), 0, 0)  23.2 us
    ppermute x6, starting transfers between devices, shifted(): return lax.ppermute(v, CTX, [(i, i + by) for i in range(ctx - by)])  21 us
    all_to_all x1, starting transfers between devices, per_device(): quarter = lax.all_to_all(packed, 'zl', 0, 0)  13.2 us
    all_to_all x1, blocking collectives, per_device(): summed = lax.all_to_all(send, ('core', 'y', 'x'), 0, 0)  12.2 us
    ppermute x1, starting transfers between devices, per_device(): theirs = lax.ppermute(mine, 'core', [(0, 1), (1, 0)])  7.16 us
    all_to_all x1, starting transfers between devices, per_device(): mine = lax.all_to_all(fan, 'x', 0, 0)  4.01 us
  transfers between devices with their start and end apart: 9, of which 2 were waited for; matrix products, arithmetic and copies ran while one was open for 0% of the time, Pallas kernels for 5%

profile of v8, /device:TPU:1, one launch (start us, length us, event | category | flops | bytes accessed | tf_op | source)
XLA Modules:
  0.0 92.8 jit_solution(2386189536654738821)
XLA Ops:
  0.6 1.5 %shard_map.157 = bf16[8,128,128]{2,1,0:T(8,128)(2,1)} custom-call(bf16[256,1024]{1,0:T(8,128)(2,1)} %k_hbm.1, bf16[256,1024]{1,0:T(8,128)(2,1)} %v_hbm.1), custom_call_target="tpu_custom_call" | custom-call | flops 1000000 | bytes 1000000 | tf_op jit(solution)/shard_map/pallas_call | solution.py:415
  2.1 0.0 copy-start
  2.1 0.0 copy-start.1
  2.2 0.0 copy-start.7
  2.2 0.0 copy-start.8
  2.2 13.2 %all-to-all-start = ((bf16[8,128,128]{2,1,0:T(8,128)(2,1)}), bf16[8,128,128]{2,1,0:T(8,128)(2,1)S(1)}, u32[]{:S(2)}, u32[]{:S(2)}) async-start(bf16[8,128,128]{2,1,0:T(8,128)(2,1)} %shard_map.157), calls=%async_computation | async-start | bytes 524288 | tf_op jit(solution)/shard_map/all_to_all | solution.py:423
  15.4 0.0 copy-start.6
  15.5 0.6 copy-done.4
  16.1 0.0 copy-done.6
  16.1 1.0 %shard_map.160 = (f32[264,128]{1,0:T(8,128)S(1)}, bf16[272,128]{1,0:T(8,128)(2,1)S(1)}, f32[8,256]{1,0:T(8,128)S(1)}) custom-call(f32[2]{0:T(128)S(1)} %copy-done.5, bf16[256,256]{1,0:T(8,128)(2,1)S(1)} %copy-done, bf16[256,256]{1,0:T(8,128)(2,1)S(1)} %copy-done.1, s32[2,256]{1,0:T(2,128)S(1)} %bitcast.6, f32[1,256]{1,0:T(1,128)S(1)} %bitcast.8, ...), custom_call_target="tpu_custom_call" | custom-call | flops 1000000 | bytes 1000000 | tf_op jit(solution)/shard_map/pallas_call | solution.py:424
  17.2 0.0 copy-start.10
  17.2 4.5 %collective-permute-start.3 = (bf16[272,128]{1,0:T(8,128)(2,1)S(1)}, bf16[272,128]{1,0:T(8,128)(2,1)S(1)}, u32[]{:S(2)}, u32[]{:S(2)}) collective-permute-start(bf16[272,128]{1,0:T(8,128)(2,1)S(1)} %get-tuple-element.44), channel_id=1, source_target_pairs={{0,32},{32,64},{64,96},{96,128},{128,160},{160,192},{192,224},{224... | collective-permute-start | bytes 208904 | tf_op jit(solution)/shard_map/ppermute | solution.py:431
  21.7 3.1 %collective-permute-start.2 = (bf16[272,128]{1,0:T(8,128)(2,1)S(1)}, bf16[272,128]{1,0:T(8,128)(2,1)S(1)}, u32[]{:S(2)}, u32[]{:S(2)}) collective-permute-start(bf16[272,128]{1,0:T(8,128)(2,1)S(1)} %get-tuple-element.44), channel_id=1, source_target_pairs={{0,64},{32,96},{64,128},{96,160},{128,192},{160,224},{192,256},{22... | collective-permute-start | bytes 208904 | tf_op jit(solution)/shard_map/ppermute | solution.py:431
  24.8 3.1 %collective-permute-start.1 = (bf16[272,128]{1,0:T(8,128)(2,1)S(1)}, bf16[272,128]{1,0:T(8,128)(2,1)S(1)}, u32[]{:S(2)}, u32[]{:S(2)}) collective-permute-start(bf16[272,128]{1,0:T(8,128)(2,1)S(1)} %get-tuple-element.44), channel_id=1, source_target_pairs={{0,96},{32,128},{64,160},{96,192},{128,224},{160,256},{192,288},{2... | collective-permute-start | bytes 208904 | tf_op jit(solution)/shard_map/ppermute | solution.py:431
  27.9 1.4 %shard_map.158 = (f32[256,256]{1,0:T(8,128)S(1)}, f32[256,256]{1,0:T(8,128)S(1)}) custom-call(bf16[256,256]{1,0:T(8,128)(2,1)S(1)} %copy-done, bf16[256,256]{1,0:T(8,128)(2,1)S(1)} %copy-done.1, bf16[256,256]{1,0:T(8,128)(2,1)S(1)} %copy-done.3, bf16[256,256]{1,0:T(8,128)(2,1)S(1)} %copy-done.2, s32[2,256]{1,0:T(2,128)S(1)} %bitcast.7, f32[2]{0:T(128)S(1)} %copy-done.5, ...), custom_call_target="tpu_custom_call" | custom-call | flops 1000000 | bytes 1000000 | tf_op jit(solution)/shard_map/pallas_call | solution.py:434
  29.3 1.1 %shard_map.159 = bf16[4,8,128,128]{3,2,1,0:T(8,128)(2,1)} custom-call(bf16[8,128,128]{2,1,0:T(8,128)(2,1)S(1)} %all-to-all-done.quarter_ref), custom_call_target="tpu_custom_call" | custom-call | flops 1000000 | bytes 1000000 | tf_op jit(solution)/shard_map/pallas_call | solution.py:438
  30.4 4.0 %all-to-all-start.1 = ((bf16[4,8,128,128]{3,2,1,0:T(8,128)(2,1)}), bf16[4,8,128,128]{3,2,1,0:T(8,128)(2,1)S(1)}, u32[]{:S(2)}, u32[]{:S(2)}) async-start(bf16[4,8,128,128]{3,2,1,0:T(8,128)(2,1)} %shard_map.159), calls=%async_computation.1 | async-start | bytes 2097152 | tf_op jit(solution)/shard_map/all_to_all | solution.py:444
  34.4 0.0 copy-start.11
  34.4 0.1 shard_map.161
  34.5 7.0 %collective-permute-start.6 = (bf16[272,128]{1,0:T(8,128)(2,1)S(1)}, bf16[272,128]{1,0:T(8,128)(2,1)S(1)}, u32[]{:S(2)}, u32[]{:S(2)}) collective-permute-start(bf16[272,128]{1,0:T(8,128)(2,1)S(1)} %get-tuple-element.49), channel_id=1, source_target_pairs={{0,256},{32,288},{64,320},{96,352},{128,384},{160,416},{192,448},{... | collective-permute-start | bytes 208904 | tf_op jit(solution)/shard_map/ppermute | solution.py:431
  41.5 2.1 %collective-permute-start.5 = (bf16[272,128]{1,0:T(8,128)(2,1)S(1)}, bf16[272,128]{1,0:T(8,128)(2,1)S(1)}, u32[]{:S(2)}, u32[]{:S(2)}) collective-permute-start(bf16[272,128]{1,0:T(8,128)(2,1)S(1)} %get-tuple-element.49), channel_id=1, source_target_pairs={{0,128},{32,160},{64,192},{96,224},{128,256},{160,288},{192,320},{... | collective-permute-start | bytes 208904 | tf_op jit(solution)/shard_map/ppermute | solution.py:431
  43.6 1.3 %collective-permute-start.4 = (bf16[272,128]{1,0:T(8,128)(2,1)S(1)}, bf16[272,128]{1,0:T(8,128)(2,1)S(1)}, u32[]{:S(2)}, u32[]{:S(2)}) collective-permute-start(bf16[272,128]{1,0:T(8,128)(2,1)S(1)} %get-tuple-element.49), channel_id=1, source_target_pairs={{0,384},{32,416},{64,448},{96,480},{1,385},{33,417},{65,449},{97,4... | collective-permute-start | bytes 208904 | tf_op jit(solution)/shard_map/ppermute | solution.py:431
  44.9 0.3 all-to-all-done.1.kv_ref
  45.2 7.2 %collective-permute-start = (bf16[4,8,128,128]{3,2,1,0:T(8,128)(2,1)S(1)}, bf16[4,8,128,128]{3,2,1,0:T(8,128)(2,1)S(1)}, u32[]{:S(2)}, u32[]{:S(2)}) collective-permute-start(bf16[4,8,128,128]{3,2,1,0:T(8,128)(2,1)S(1)} %all-to-all-done.1.kv_ref), channel_id=1, source_target_pairs={{0,32},{32,0},{1,33},{33,1},{2,34},{34,2},{3,35},{35,3},{4,36},{36... | collective-permute-start | bytes 3145736 | tf_op jit(solution)/shard_map/ppermute | solution.py:446
  52.4 0.8 shard_map.162
  53.3 0.4 shard_map.163
  53.7 1.0 %collective-permute-done.kv_ref = bf16[4,8,128,128]{3,2,1,0:T(8,128)(2,1)S(1)} collective-permute-done((bf16[4,8,128,128]{3,2,1,0:T(8,128)(2,1)S(1)}, bf16[4,8,128,128]{3,2,1,0:T(8,128)(2,1)S(1)}, u32[]{:S(2)}, u32[]{:S(2)}) %collective-permute-start) | collective-permute-done | bytes 1048608 | tf_op jit(solution)/shard_map/ppermute | solution.py:446
  54.6 1.7 %shard_map.164 = (bf16[256,256]{1,0:T(8,128)(2,1)}, bf16[32,8,128]{2,1,0:T(8,128)(2,1)S(1)}) custom-call(bf16[512,256]{1,0:T(8,128)(2,1)S(1)} %get-tuple-element.66.scaled_ref, bf16[4,8,128,128]{3,2,1,0:T(8,128)(2,1)S(1)} %collective-permute-done.kv_ref, f32[512,128]{1,0:T(8,128)S(1)} %get-tuple-element.68.m_in, f32[512,128]{1,0:T(8,128)S(1)} %get-tuple-element.69.l_in, ...), custom_call_target="tpu_custom_call" | custom-call | flops 1000000000 | bytes 1000000 | tf_op jit(solution)/shard_map/pallas_call | solution.py:457
  56.3 12.2 %all_to_all.20.got_ref = bf16[32,8,128]{2,1,0:T(8,128)(2,1)S(1)} all-to-all(bf16[32,8,128]{2,1,0:T(8,128)(2,1)S(1)} %get-tuple-element.73), channel_id=1, replica_groups=mesh['zl'=8,'core'=2,'zh'=2,'y'=4,'x'=4] {'core','y','x'}, dimensions={0} | all-to-all | bytes 131072 | tf_op jit(solution)/shard_map/all_to_all | solution.py:464
  68.5 0.1 shard_map.165
  68.7 23.2 %all_to_all.21.got_ref = bf16[16,16,128]{2,1,0:T(8,128)(2,1)S(1)} all-to-all(bf16[16,16,128]{2,1,0:T(8,128)(2,1)S(1)} %shard_map.165), channel_id=1, replica_groups=mesh['zl'=8,'core'=2,'zh'=2,'y'=4,'x'=4] {'zl','zh'}, dimensions={0} | all-to-all | bytes 131072 | tf_op jit(solution)/shard_map/all_to_all | solution.py:467
  91.9 0.9 %shard_map.166 = (bf16[256,256]{1,0:T(8,128)(2,1)}, f32[1,32]{1,0:T(1,128)}) custom-call(bf16[16,16,128]{2,1,0:T(8,128)(2,1)S(1)} %all_to_all.21.got_ref, f32[256,256]{1,0:T(8,128)S(1)} %get-tuple-element.74.gated_ref, f32[8,256]{1,0:T(8,128)S(1)} %get-tuple-element.64.rows_ref), custom_call_target="tpu_custom_call" | custom-call | flops 1000000 | bytes 1000000 | tf_op jit(solution)/shard_map/pallas_call | solution.py:468
  (22 shorter events, 0.1 us)
Async XLA Ops:
  2.1 13.3 %copy-start = (bf16[256,256]{1,0:T(8,128)(2,1)S(1)}, bf16[256,256]{1,0:T(8,128)(2,1)}, u32[]{:S(2)}) copy-start(bf16[256,256]{1,0:T(8,128)(2,1)} %x_ref.3) | copy-start | bytes 393220
  2.1 13.3 %copy-start.1 = (bf16[256,256]{1,0:T(8,128)(2,1)S(1)}, bf16[256,256]{1,0:T(8,128)(2,1)}, u32[]{:S(2)}) copy-start(bf16[256,256]{1,0:T(8,128)(2,1)} %w_ref.3) | copy-start | bytes 393220
  2.2 13.3 %copy-start.7 = (f32[256]{0:T(256)S(1)}, f32[256]{0:T(256)}, u32[]{:S(2)}) copy-start(f32[256]{0:T(256)} %param.26) | copy-start | bytes 3076
  2.2 13.3 %copy-start.8 = (f32[256]{0:T(256)S(1)}, f32[256]{0:T(256)}, u32[]{:S(2)}) copy-start(f32[256]{0:T(256)} %param.25) | copy-start | bytes 3076
  2.2 13.3 %copy-start.9 = (s32[256]{0:T(256)S(1)}, s32[256]{0:T(256)}, u32[]{:S(2)}) copy-start(s32[256]{0:T(256)} %param.27) | copy-start | bytes 3076
  2.2 27.1 %all-to-all-start = ((bf16[8,128,128]{2,1,0:T(8,128)(2,1)}), bf16[8,128,128]{2,1,0:T(8,128)(2,1)S(1)}, u32[]{:S(2)}, u32[]{:S(2)}) async-start(bf16[8,128,128]{2,1,0:T(8,128)(2,1)} %shard_map.157), calls=%async_computation | async-start | bytes 524288 | tf_op jit(solution)/shard_map/all_to_all | solution.py:423
  15.4 0.7 copy-start.4
  15.4 0.7 copy-start.5
  15.4 0.7 copy-start.6
  16.1 11.8 %copy-start.2 = (bf16[256,256]{1,0:T(8,128)(2,1)S(1)}, bf16[256,256]{1,0:T(8,128)(2,1)}, u32[]{:S(2)}) copy-start(bf16[256,256]{1,0:T(8,128)(2,1)} %g_ref.1) | copy-start | bytes 393220
  16.1 11.8 %copy-start.3 = (bf16[256,256]{1,0:T(8,128)(2,1)S(1)}, bf16[256,256]{1,0:T(8,128)(2,1)}, u32[]{:S(2)}) copy-start(bf16[256,256]{1,0:T(8,128)(2,1)} %r_ref.3) | copy-start | bytes 393220
  17.2 10.7 %copy-start.10 = (f32[2]{0:T(128)S(1)}, f32[2]{0:T(128)}, u32[]{:S(2)}) copy-start(f32[2]{0:T(128)} %skip_ref.1) | copy-start | bytes 28
  17.2 17.2 %collective-permute-start.3 = (bf16[272,128]{1,0:T(8,128)(2,1)S(1)}, bf16[272,128]{1,0:T(8,128)(2,1)S(1)}, u32[]{:S(2)}, u32[]{:S(2)}) collective-permute-start(bf16[272,128]{1,0:T(8,128)(2,1)S(1)} %get-tuple-element.44), channel_id=1, source_target_pairs={{0,32},{32,64},{64,96},{96,128},{128,160},{160,192},{192,224},{224... | collective-permute-start | bytes 208904 | tf_op jit(solution)/shard_map/ppermute | solution.py:431
  21.7 12.7 %collective-permute-start.2 = (bf16[272,128]{1,0:T(8,128)(2,1)S(1)}, bf16[272,128]{1,0:T(8,128)(2,1)S(1)}, u32[]{:S(2)}, u32[]{:S(2)}) collective-permute-start(bf16[272,128]{1,0:T(8,128)(2,1)S(1)} %get-tuple-element.44), channel_id=1, source_target_pairs={{0,64},{32,96},{64,128},{96,160},{128,192},{160,224},{192,256},{22... | collective-permute-start | bytes 208904 | tf_op jit(solution)/shard_map/ppermute | solution.py:431
  24.8 9.7 %collective-permute-start.1 = (bf16[272,128]{1,0:T(8,128)(2,1)S(1)}, bf16[272,128]{1,0:T(8,128)(2,1)S(1)}, u32[]{:S(2)}, u32[]{:S(2)}) collective-permute-start(bf16[272,128]{1,0:T(8,128)(2,1)S(1)} %get-tuple-element.44), channel_id=1, source_target_pairs={{0,96},{32,128},{64,160},{96,192},{128,224},{160,256},{192,288},{2... | collective-permute-start | bytes 208904 | tf_op jit(solution)/shard_map/ppermute | solution.py:431
  30.4 14.8 %all-to-all-start.1 = ((bf16[4,8,128,128]{3,2,1,0:T(8,128)(2,1)}), bf16[4,8,128,128]{3,2,1,0:T(8,128)(2,1)S(1)}, u32[]{:S(2)}, u32[]{:S(2)}) async-start(bf16[4,8,128,128]{3,2,1,0:T(8,128)(2,1)} %shard_map.159), calls=%async_computation.1 | async-start | bytes 2097152 | tf_op jit(solution)/shard_map/all_to_all | solution.py:444
  34.4 17.9 %copy-start.11 = (bf16[256,256]{1,0:T(8,128)(2,1)S(1)}, bf16[256,256]{1,0:T(8,128)(2,1)}, u32[]{:S(2)}) copy-start(bf16[256,256]{1,0:T(8,128)(2,1)} %q_ref.1) | copy-start | bytes 393220
  34.5 18.7 %collective-permute-start.6 = (bf16[272,128]{1,0:T(8,128)(2,1)S(1)}, bf16[272,128]{1,0:T(8,128)(2,1)S(1)}, u32[]{:S(2)}, u32[]{:S(2)}) collective-permute-start(bf16[272,128]{1,0:T(8,128)(2,1)S(1)} %get-tuple-element.49), channel_id=1, source_target_pairs={{0,256},{32,288},{64,320},{96,352},{128,384},{160,416},{192,448},{... | collective-permute-start | bytes 208904 | tf_op jit(solution)/shard_map/ppermute | solution.py:431
  41.5 11.7 %collective-permute-start.5 = (bf16[272,128]{1,0:T(8,128)(2,1)S(1)}, bf16[272,128]{1,0:T(8,128)(2,1)S(1)}, u32[]{:S(2)}, u32[]{:S(2)}) collective-permute-start(bf16[272,128]{1,0:T(8,128)(2,1)S(1)} %get-tuple-element.49), channel_id=1, source_target_pairs={{0,128},{32,160},{64,192},{96,224},{128,256},{160,288},{192,320},{... | collective-permute-start | bytes 208904 | tf_op jit(solution)/shard_map/ppermute | solution.py:431
  43.6 9.7 %collective-permute-start.4 = (bf16[272,128]{1,0:T(8,128)(2,1)S(1)}, bf16[272,128]{1,0:T(8,128)(2,1)S(1)}, u32[]{:S(2)}, u32[]{:S(2)}) collective-permute-start(bf16[272,128]{1,0:T(8,128)(2,1)S(1)} %get-tuple-element.49), channel_id=1, source_target_pairs={{0,384},{32,416},{64,448},{96,480},{1,385},{33,417},{65,449},{97,4... | collective-permute-start | bytes 208904 | tf_op jit(solution)/shard_map/ppermute | solution.py:431
  45.2 9.4 %collective-permute-start = (bf16[4,8,128,128]{3,2,1,0:T(8,128)(2,1)S(1)}, bf16[4,8,128,128]{3,2,1,0:T(8,128)(2,1)S(1)}, u32[]{:S(2)}, u32[]{:S(2)}) collective-permute-start(bf16[4,8,128,128]{3,2,1,0:T(8,128)(2,1)S(1)} %all-to-all-done.1.kv_ref), channel_id=1, source_target_pairs={{0,32},{32,0},{1,33},{33,1},{2,34},{34,2},{3,35},{35,3},{4,36},{36... | collective-permute-start | bytes 3145736 | tf_op jit(solution)/shard_map/ppermute | solution.py:446
